TPU v7x, 512 devices: a whole 4x4x16 slice. The times are simulated.
512 devices in a mesh: aa: 32 (over z, core), ba: 16 (over x, y).
Axes of the slice: x: 4, y: 4, z: 16, core: 2. Of those that a mesh axis runs over, the one named last changes fastest.
Arguments:
- legendre: bfloat16 [640, 32, 16, 1, 1281], P('aa', None, 'ba'), may hold values from -0.15625 to 0.15625
- spectral: bfloat16 [640, 1281, 2, 64], P('aa', None, None, 'ba'), may hold values from -0.25 to 0.25
- slot_pairs: int32 [640], replicated, may hold values from 0 to 639, each once
- lat_shift: int32 [512, 5120], P('aa', 'ba'), may hold values from -1 to 1
- lon_shift: int32 [512, 5120], P('aa', 'ba'), may hold values from -8 to 8
Outputs:
- departed: bfloat16 [512, 64, 5120], P('aa', None, 'ba')
Inputs may be any that keep to these rules, and one draw needn't show every extreme that they name: `slot_pairs`: each pair index appears in exactly one slot.
All inputs are finite; a program needn't handle non-finite values.
Results may differ from a plain program's by a relative error of at most 0.0059.
Values may be sent and summed in bfloat16 or wider, within the bound.
No kernel may reach another device: no remote copies, remote signals or barrier semaphores. Data moves between devices by JAX's collectives and lax.ppermute only.
A program may use at most 64 MiB of HBM per device.

v0:
```python
import math

import jax
import jax.numpy as jnp
from jax import lax
from jax.sharding import PartitionSpec as P

WAVES = 1280
NLON = 5120
HMAX = 8
FL = 64
KPACK = 1281


STENCIL = (-0.0625, 0.5625, 0.5625, -0.0625)


def padded_2(cells, sides, width):
    for axis, dim in sides:
        count = lax.axis_size(axis)
        ends = count - 1
        head = lax.slice_in_dim(cells, 0, width, axis=dim)
        tail = lax.slice_in_dim(cells, cells.shape[dim] - width, cells.shape[dim], axis=dim)
        cells = jnp.concatenate(
            [
                lax.ppermute(tail, axis, [(i, (i + 1) % count) for i in range(ends)]),
                cells,
                lax.ppermute(head, axis, [((i + 1) % count, i) for i in range(ends)]),
            ],
            axis=dim,
        )
    return cells


def pair_masks(pairs):
    column = jnp.arange(KPACK, dtype=jnp.int32)[None, :]
    lower = column < (WAVES - pairs)[:, None]
    return jnp.stack([lower, jnp.logical_not(lower)], axis=-1).astype(jnp.bfloat16)


def fourier_table(slot_pairs, first_lon, lon_count):
    waves_of = jnp.stack([slot_pairs, WAVES - 1 - slot_pairs], axis=1)
    lon_ids = first_lon + jnp.arange(lon_count, dtype=jnp.int32)
    phases = waves_of[:, :, None] * lon_ids[None, None, :] % NLON
    angles = phases.reshape(WAVES, lon_count).astype(jnp.float32) * (2.0 * math.pi / NLON)
    factor = 1.0 / math.sqrt(WAVES)
    cos_rows = (jnp.cos(angles) * factor).astype(jnp.bfloat16)
    sin_rows = (-jnp.sin(angles) * factor).astype(jnp.bfloat16)
    return jnp.concatenate([cos_rows, sin_rows], axis=0)


def synthesize(coefficients, slot_pairs):
    block_width = 512
    count_blocks = NLON // block_width
    output_grid = jnp.zeros((coefficients.shape[0], NLON), jnp.bfloat16)

    def one_block(block_id, current):
        first = (block_id * block_width).astype(jnp.int32)
        synth_table = fourier_table(slot_pairs, first, block_width)
        piece = jnp.dot(coefficients, synth_table, preferred_element_type=jnp.float32).astype(
            jnp.bfloat16
        )
        return lax.dynamic_update_slice_in_dim(current, piece, first, 1)

    return lax.fori_loop(0, count_blocks, one_block, output_grid)


def depart(padded, lat_shift, lon_shift, halo_width):
    count_rows, columns = lat_shift.shape
    span = padded.shape[2] - 3
    result = None
    for lat_step in (-1, 0, 1):
        rows_part = padded[1 + lat_step : 1 + lat_step + count_rows]
        weighted = jnp.zeros((count_rows, padded.shape[1], span), jnp.float32)
        for position, weight in enumerate(STENCIL):
            weighted = weighted + weight * rows_part[:, :, position : position + span].astype(
                jnp.float32
            )
        lat_hit = lat_shift == lat_step
        for lon_step in range(-HMAX, HMAX + 1):
            first = halo_width - 1 + lon_step
            summed = weighted[:, :, first : first + columns]
            matched = jnp.logical_and(lat_hit, lon_shift == lon_step)
            result = summed if result is None else jnp.where(matched[:, None, :], summed, result)
    return result.astype(jnp.bfloat16)


def local(legendre, spectral, slot_pairs, lat_shift, lon_shift):
    pair_dev = legendre.shape[0]
    rows_dev = legendre.shape[3]
    local_lats = legendre.shape[1] * rows_dev
    leg_rows = legendre.reshape(pair_dev, local_lats, KPACK)
    my_pairs = lax.dynamic_slice_in_dim(slot_pairs, lax.axis_index("aa") * pair_dev, pair_dev)
    my_masks = pair_masks(my_pairs)
    selected = (
        lax.all_gather(spectral, "ba", axis=3, tiled=True)[:, :, None, :, :]
        * my_masks[:, :, :, None, None]
    )
    fourier_coef = jnp.einsum(
        "plk,pkjcf->lpjcf", leg_rows, selected, preferred_element_type=jnp.float32
    ).astype(jnp.bfloat16)
    sendable = fourier_coef.reshape(local_lats, pair_dev * 4 * FL)
    arrived = lax.all_to_all(sendable, "aa", split_axis=0, concat_axis=1, tiled=True)
    coefficients = (
        arrived.reshape(rows_dev, WAVES // 2, 2, 2, FL)
        .transpose(0, 4, 3, 1, 2)
        .reshape(rows_dev * FL, 2 * WAVES)
    )
    grid_rows = synthesize(coefficients, slot_pairs).reshape(rows_dev, FL, NLON)
    halo_width = HMAX + 2
    row_shifts = (
        lax.all_to_all(lat_shift, "ba", split_axis=0, concat_axis=1, tiled=True),
        lax.all_to_all(lon_shift, "ba", split_axis=0, concat_axis=1, tiled=True),
    )
    padded = padded_2(grid_rows, ((("aa", "ba"), 0),), 1)
    padded = jnp.concatenate(
        [padded[:, :, NLON - halo_width :], padded, padded[:, :, :halo_width]], axis=2
    )
    departed = depart(padded, row_shifts[0], row_shifts[1], halo_width)
    return lax.all_to_all(departed, "ba", split_axis=2, concat_axis=0, tiled=True)


def solution(mesh):
    placed = (
        P("aa", None, "ba", None, None),
        P("aa", None, None, "ba"),
        P(),
        P("aa", "ba"),
        P("aa", "ba"),
    )
    return jax.shard_map(
        local, mesh=mesh, in_specs=placed, out_specs=P("aa", None, "ba"), check_vma=False
    )
```

profile of v0, /device:TPU:1, one launch (start us, length us, event | category | flops | bytes accessed | tf_op | source)
XLA Modules:
  0.0 444.1 jit_solution(7801523761095744244)
XLA Ops:
  10.2 86.4 %all-gather.2.cloned.1.call-done = bf16[20,1281,2,64]{1,2,0,3:T(2,128)(2,1)} async-done(((bf16[20,1281,2,4]{1,2,0,3:T(2,128)(2,1)}), bf16[20,1281,2,64]{1,2,0,3:T(2,128)(2,1)}) %all-gather.2.cloned.1.call-update) | async-done | bytes 6558736 | tf_op jit(solution)/shard_map/all_gather | solution.py:96
  100.9 7.4 %fusion.78 = bf16[32,20,2,2,64]{4,0,3,2,1:T(8,128)(2,1)S(1)} fusion(bf16[20,32,1,1,1281]{4,1,3,2,0:T(8,128)(2,1)S(1)} %copy-done, bf16[20,1281,2]{1,2,0:T(2,128)(2,1)S(1)} %add_convert_fusion, bf16[20,1281,2,64]{1,3,2,0:T(8,128)(2,1)S(1)} %copy.23), kind=kOutput, calls=%fused_computation.81 | convolution fusion | flops 426480640 | bytes 8628560 | tf_op jit(solution)/shard_map/plk,pkjcf->lpjcf/dot_general | solution.py:99
  113.4 13.0 %all-to-all-start.2 = ((bf16[32,2,2560]{2,1,0:T(2,128)(2,1)}), bf16[32,2,2560]{2,1,0:T(2,128)(2,1)S(1)}, u32[]{:S(2)}, u32[]{:S(2)}) async-start(bf16[32,2,2560]{2,1,0:T(2,128)(2,1)} %reshape.1065), calls=%async_computation.2 | async-start | bytes 655360 | tf_op jit(solution)/shard_map/all_to_all | solution.py:103
  126.4 25.0 %all-to-all-done.2 = bf16[32,2,2560]{2,1,0:T(2,128)(2,1)S(1)} async-done(((bf16[32,2,2560]{2,1,0:T(2,128)(2,1)}), bf16[32,2,2560]{2,1,0:T(2,128)(2,1)S(1)}, u32[]{:S(2)}, u32[]{:S(2)}) %all-to-all-start.2) | async-done | bytes 327712 | tf_op jit(solution)/shard_map/all_to_all | solution.py:103
  154.7 127.1 %while.16 = (s32[]{:T(128)}, bf16[64,5120]{1,0:T(8,128)(2,1)S(1)}, s32[640]{0:T(1024)S(1)}, bf16[64,2560]{1,0:T(8,128)(2,1)S(1)}, s32[640,1]{0,1:T(1,128)S(1)}, ...) while((s32[]{:T(128)}, bf16[64,5120]{1,0:T(8,128)(2,1)S(1)}, s32[640]{0:T(1024)S(1)}, ...), condition=%wide.wide.region_1.2_spmd, body=%wide.wide.region_0.1_spmd.sunk | while | flops 182225280 | bytes 5681299 | solution.py:65
  155.2 11.7 %multiply_convert_fusion.4 = (bf16[1280,512]{1,0:T(8,128)(2,1)S(1)}, bf16[1280,512]{1,0:T(8,128)(2,1)S(1)}) fusion(s32[512]{0:T(512)S(1)} %iota_add_fusion.3, s32[1280]{0:T(1024)S(1)} %mul.240), kind=kLoop, calls=%fused_computation.8.clone.clone.1 | loop fusion | flops 9175040 | bytes 2628608 | tf_op jit(solution)/shard_map/while/body/eval_jaxpr/convert_element_type | solution.py:47
  167.9 11.7 %multiply_convert_fusion.4 = (bf16[1280,512]{1,0:T(8,128)(2,1)S(1)}, bf16[1280,512]{1,0:T(8,128)(2,1)S(1)}) fusion(s32[512]{0:T(512)S(1)} %iota_add_fusion.3, s32[1280]{0:T(1024)S(1)} %mul.240), kind=kLoop, calls=%fused_computation.8.clone.clone.1 | loop fusion | flops 9175040 | bytes 2628608 | tf_op jit(solution)/shard_map/while/body/eval_jaxpr/convert_element_type | solution.py:47
  180.6 11.7 %multiply_convert_fusion.4 = (bf16[1280,512]{1,0:T(8,128)(2,1)S(1)}, bf16[1280,512]{1,0:T(8,128)(2,1)S(1)}) fusion(s32[512]{0:T(512)S(1)} %iota_add_fusion.3, s32[1280]{0:T(1024)S(1)} %mul.240), kind=kLoop, calls=%fused_computation.8.clone.clone.1 | loop fusion | flops 9175040 | bytes 2628608 | tf_op jit(solution)/shard_map/while/body/eval_jaxpr/convert_element_type | solution.py:47
  193.3 11.7 %multiply_convert_fusion.4 = (bf16[1280,512]{1,0:T(8,128)(2,1)S(1)}, bf16[1280,512]{1,0:T(8,128)(2,1)S(1)}) fusion(s32[512]{0:T(512)S(1)} %iota_add_fusion.3, s32[1280]{0:T(1024)S(1)} %mul.240), kind=kLoop, calls=%fused_computation.8.clone.clone.1 | loop fusion | flops 9175040 | bytes 2628608 | tf_op jit(solution)/shard_map/while/body/eval_jaxpr/convert_element_type | solution.py:47
  206.0 11.7 %multiply_convert_fusion.4 = (bf16[1280,512]{1,0:T(8,128)(2,1)S(1)}, bf16[1280,512]{1,0:T(8,128)(2,1)S(1)}) fusion(s32[512]{0:T(512)S(1)} %iota_add_fusion.3, s32[1280]{0:T(1024)S(1)} %mul.240), kind=kLoop, calls=%fused_computation.8.clone.clone.1 | loop fusion | flops 9175040 | bytes 2628608 | tf_op jit(solution)/shard_map/while/body/eval_jaxpr/convert_element_type | solution.py:47
  218.7 11.7 %multiply_convert_fusion.4 = (bf16[1280,512]{1,0:T(8,128)(2,1)S(1)}, bf16[1280,512]{1,0:T(8,128)(2,1)S(1)}) fusion(s32[512]{0:T(512)S(1)} %iota_add_fusion.3, s32[1280]{0:T(1024)S(1)} %mul.240), kind=kLoop, calls=%fused_computation.8.clone.clone.1 | loop fusion | flops 9175040 | bytes 2628608 | tf_op jit(solution)/shard_map/while/body/eval_jaxpr/convert_element_type | solution.py:47
  231.4 11.7 %multiply_convert_fusion.4 = (bf16[1280,512]{1,0:T(8,128)(2,1)S(1)}, bf16[1280,512]{1,0:T(8,128)(2,1)S(1)}) fusion(s32[512]{0:T(512)S(1)} %iota_add_fusion.3, s32[1280]{0:T(1024)S(1)} %mul.240), kind=kLoop, calls=%fused_computation.8.clone.clone.1 | loop fusion | flops 9175040 | bytes 2628608 | tf_op jit(solution)/shard_map/while/body/eval_jaxpr/convert_element_type | solution.py:47
  244.1 11.7 %multiply_convert_fusion.4 = (bf16[1280,512]{1,0:T(8,128)(2,1)S(1)}, bf16[1280,512]{1,0:T(8,128)(2,1)S(1)}) fusion(s32[512]{0:T(512)S(1)} %iota_add_fusion.3, s32[1280]{0:T(1024)S(1)} %mul.240), kind=kLoop, calls=%fused_computation.8.clone.clone.1 | loop fusion | flops 9175040 | bytes 2628608 | tf_op jit(solution)/shard_map/while/body/eval_jaxpr/convert_element_type | solution.py:47
  256.8 11.7 %multiply_convert_fusion.4 = (bf16[1280,512]{1,0:T(8,128)(2,1)S(1)}, bf16[1280,512]{1,0:T(8,128)(2,1)S(1)}) fusion(s32[512]{0:T(512)S(1)} %iota_add_fusion.3, s32[1280]{0:T(1024)S(1)} %mul.240), kind=kLoop, calls=%fused_computation.8.clone.clone.1 | loop fusion | flops 9175040 | bytes 2628608 | tf_op jit(solution)/shard_map/while/body/eval_jaxpr/convert_element_type | solution.py:47
  269.5 11.7 %multiply_convert_fusion.4 = (bf16[1280,512]{1,0:T(8,128)(2,1)S(1)}, bf16[1280,512]{1,0:T(8,128)(2,1)S(1)}) fusion(s32[512]{0:T(512)S(1)} %iota_add_fusion.3, s32[1280]{0:T(1024)S(1)} %mul.240), kind=kLoop, calls=%fused_computation.8.clone.clone.1 | loop fusion | flops 9175040 | bytes 2628608 | tf_op jit(solution)/shard_map/while/body/eval_jaxpr/convert_element_type | solution.py:47
  284.9 5.8 %collective-permute-start.1 = (bf16[1,64,5120]{2,1,0:T(8,128)(2,1)S(1)}, bf16[1,64,5120]{2,1,0:T(8,128)(2,1)}, u32[]{:S(2)}, u32[]{:S(2)}) collective-permute-start(bf16[1,64,5120]{2,1,0:T(8,128)(2,1)S(1)} %bitcast.38), channel_id=1, source_target_pairs={{1,0},{2,1},{3,2},{4,3},{5,4},{6,5},{7,6},{8,7},{9,8},{10,9},{11,1... | collective-permute-start | bytes 1966088 | tf_op jit(solution)/shard_map/ppermute | solution.py:28
  294.9 10.7 %all-to-all-done = s32[16,1,320]{2,1,0:T(1,128)S(1)} async-done(((s32[16,1,320]{2,1,0:T(1,128)}), s32[16,1,320]{2,1,0:T(1,128)S(1)}, u32[]{:S(2)}, u32[]{:S(2)}) %all-to-all-start) | async-done | bytes 20512 | tf_op jit(solution)/shard_map/all_to_all | solution.py:112
  305.6 13.2 %all_to_all.58 = s32[16,1,320]{2,1,0:T(1,128)S(1)} all-to-all(s32[16,1,320]{2,1,0:T(1,128)S(1)} %all_to_all.45), channel_id=1, replica_groups=mesh['aa'=32,'ba'=16] {'ba'}, dimensions={0} | all-to-all | bytes 40960 | tf_op jit(solution)/shard_map/all_to_all | solution.py:113
  352.8 4.6 %concatenate.21 = bf16[3,64,5140]{2,1,0:T(8,128)(2,1)} concatenate(bf16[3,64,10]{2,1,0:T(8,128)(2,1)S(1)} %get-tuple-element.193, bf16[3,64,5120]{2,1,0:T(8,128)(2,1)} %copy-done.1, bf16[3,64,10]{2,1,0:T(8,128)(2,1)S(1)} %get-tuple-element.192), dimensions={2} | concatenate | bytes 3947520 | tf_op jit(solution)/shard_map/concatenate | solution.py:116
  357.8 7.0 %multiply_add_fusion.2 = (bf16[1,64,5137]{2,1,0:T(8,128)(2,1)S(1)}, bf16[1,64,5137]{2,1,0:T(8,128)(2,1)S(1)}, bf16[1,64,5137]{2,1,0:T(8,128)(2,1)S(1)}) fusion(bf16[3,64,5140]{2,1,0:T(8,128)(2,1)} %concatenate.21), kind=kLoop, calls=%fused_computation.29 | loop fusion | flops 11835648 | bytes 9863040 | tf_op jit(solution)/shard_map/add | solution.py:76
  365.2 12.4 %fusion.77 = bf16[1,64,5120]{2,1,0:T(8,128)(2,1)S(1)} fusion(bf16[1,64,5137]{2,1,0:T(8,128)(2,1)S(1)} %get-tuple-element.191, bf16[1,64,5137]{2,1,0:T(8,128)(2,1)S(1)} %get-tuple-element.190, bf16[1,64,5137]{2,1,0:T(8,128)(2,1)S(1)} %get-tuple-element.189, pred[5120]{0:T(1024)(128)(4,1)S(1)} %copy-done.40, pred[5120]{0:T(1024)(128)(4,1)S(1)} %copy-done.39, ...), kind=kLoop, calls=%fused_computation.80 | loop fusion | flops 16384000 | bytes 34334720 | tf_op jit(solution)/shard_map/convert_element_type | solution.py:85
  381.6 29.2 %reduce.102 = bf16[5120,64]{1,0:T(8,128)(2,1)S(1)} reduce(bf16[5120,1,64]{2,1,0:T(2,128)(2,1)} %bitcast.32, bf16[]{:T(256)} %broadcast.1023), dimensions={1}, to_apply=%bitcast.23.reduce_sub_computation | reduce | bytes 1310722
  412.5 14.6 %all_to_all.59 = bf16[16,2,10240]{2,1,0:T(2,128)(2,1)S(1)} all-to-all(bf16[16,2,10240]{2,1,0:T(2,128)(2,1)} %reshape.1067), channel_id=1, replica_groups=mesh['aa'=32,'ba'=16] {'ba'}, dimensions={0} | all-to-all | bytes 1310720 | tf_op jit(solution)/shard_map/all_to_all | solution.py:120
  430.8 4.8 %copy.29 = bf16[1,64,5120]{2,1,0:T(8,128)(2,1)S(1)} copy(bf16[1,64,5120]{1,0,2:T(2,128)(2,1)} %bitcast.33) | data formatting | bytes 1310720 | tf_op jit(solution)/shard_map/all_to_all | solution.py:120
  (225 shorter events, 78.4 us)
Async XLA Ops:
  6.5 94.4 %copy-start = (bf16[20,32,1,1,1281]{4,1,3,2,0:T(8,128)(2,1)S(1)}, bf16[20,32,1,1,1281]{4,1,3,2,0:T(8,128)(2,1)}, u32[]{:S(2)}) copy-start(bf16[20,32,1,1,1281]{4,1,3,2,0:T(8,128)(2,1)} %param.7) | copy-start | bytes 4919044
  6.5 90.1 %all-gather.2.cloned.1.call-start = ((), (), s32[]{:S(2)}) async-start(), calls=%async_computation.4 | async-start | bytes 7659520 | tf_op jit(solution)/shard_map/all_gather | solution.py:96
  108.8 17.6 %copy-start.2 = (s32[640]{0:T(1024)S(1)}, s32[640]{0:T(1024)}, u32[]{:S(2)}) copy-start(s32[640]{0:T(1024)} %param.9) | copy-start | bytes 7684
  113.4 38.1 %all-to-all-start.2 = ((bf16[32,2,2560]{2,1,0:T(2,128)(2,1)}), bf16[32,2,2560]{2,1,0:T(2,128)(2,1)S(1)}, u32[]{:S(2)}, u32[]{:S(2)}) async-start(bf16[32,2,2560]{2,1,0:T(2,128)(2,1)} %reshape.1065), calls=%async_computation.2 | async-start | bytes 655360 | tf_op jit(solution)/shard_map/all_to_all | solution.py:103
  154.7 136.0 %copy-start.3 = (s32[16,320]{1,0:T(8,128)S(1)}, s32[16,320]{1,0:T(8,128)}, u32[]{:S(2)}) copy-start(s32[16,320]{1,0:T(8,128)} %param.10) | copy-start | bytes 61444
  154.7 140.1 %copy-start.4 = (s32[16,320]{1,0:T(8,128)S(1)}, s32[16,320]{1,0:T(8,128)}, u32[]{:S(2)}) copy-start(s32[16,320]{1,0:T(8,128)} %param.11) | copy-start | bytes 61444
  281.8 68.4 %collective-permute-start = (bf16[1,64,5120]{2,1,0:T(8,128)(2,1)S(1)}, bf16[1,64,5120]{2,1,0:T(8,128)(2,1)S(1)}, u32[]{:S(2)}, u32[]{:S(2)}) collective-permute-start(bf16[1,64,5120]{2,1,0:T(8,128)(2,1)S(1)} %bitcast.37), channel_id=1, source_target_pairs={{0,1},{1,2},{2,3},{3,4},{4,5},{5,6},{6,7},{7,8},{8,9},{9,10},{10,1... | collective-permute-start | bytes 1966088 | tf_op jit(solution)/shard_map/ppermute | solution.py:26
  284.9 65.3 %collective-permute-start.1 = (bf16[1,64,5120]{2,1,0:T(8,128)(2,1)S(1)}, bf16[1,64,5120]{2,1,0:T(8,128)(2,1)}, u32[]{:S(2)}, u32[]{:S(2)}) collective-permute-start(bf16[1,64,5120]{2,1,0:T(8,128)(2,1)S(1)} %bitcast.38), channel_id=1, source_target_pairs={{1,0},{2,1},{3,2},{4,3},{5,4},{6,5},{7,6},{8,7},{9,8},{10,9},{11,1... | collective-permute-start | bytes 1966088 | tf_op jit(solution)/shard_map/ppermute | solution.py:28
  291.3 14.3 %all-to-all-start = ((s32[16,1,320]{2,1,0:T(1,128)}), s32[16,1,320]{2,1,0:T(1,128)S(1)}, u32[]{:S(2)}, u32[]{:S(2)}) async-start(s32[16,1,320]{2,1,0:T(1,128)} %all_to_all.43), calls=%async_computation | async-start | bytes 49152 | tf_op jit(solution)/shard_map/all_to_all | solution.py:112
  357.5 7.4 %copy-start.9 = (pred[5120]{0:T(1024)(128)(4,1)S(1)}, pred[5120]{0:T(1024)(128)(4,1)}, u32[]{:S(2)}) copy-start(pred[5120]{0:T(1024)(128)(4,1)} %and.650) | copy-start | bytes 15364
  357.5 7.4 %copy-start.10 = (pred[5120]{0:T(1024)(128)(4,1)S(1)}, pred[5120]{0:T(1024)(128)(4,1)}, u32[]{:S(2)}) copy-start(pred[5120]{0:T(1024)(128)(4,1)} %and.652) | copy-start | bytes 15364
  357.5 7.4 %copy-start.11 = (pred[5120]{0:T(1024)(128)(4,1)S(1)}, pred[5120]{0:T(1024)(128)(4,1)}, u32[]{:S(2)}) copy-start(pred[5120]{0:T(1024)(128)(4,1)} %and.654) | copy-start | bytes 15364
  357.5 7.4 %copy-start.12 = (pred[5120]{0:T(1024)(128)(4,1)S(1)}, pred[5120]{0:T(1024)(128)(4,1)}, u32[]{:S(2)}) copy-start(pred[5120]{0:T(1024)(128)(4,1)} %and.656) | copy-start | bytes 15364
  357.5 7.4 %copy-start.13 = (pred[5120]{0:T(1024)(128)(4,1)S(1)}, pred[5120]{0:T(1024)(128)(4,1)}, u32[]{:S(2)}) copy-start(pred[5120]{0:T(1024)(128)(4,1)} %and.658) | copy-start | bytes 15364
  357.5 7.4 %copy-start.14 = (pred[5120]{0:T(1024)(128)(4,1)S(1)}, pred[5120]{0:T(1024)(128)(4,1)}, u32[]{:S(2)}) copy-start(pred[5120]{0:T(1024)(128)(4,1)} %and.660) | copy-start | bytes 15364
  357.5 7.4 %copy-start.15 = (pred[5120]{0:T(1024)(128)(4,1)S(1)}, pred[5120]{0:T(1024)(128)(4,1)}, u32[]{:S(2)}) copy-start(pred[5120]{0:T(1024)(128)(4,1)} %and.662) | copy-start | bytes 15364
  357.5 7.4 %copy-start.16 = (pred[5120]{0:T(1024)(128)(4,1)S(1)}, pred[5120]{0:T(1024)(128)(4,1)}, u32[]{:S(2)}) copy-start(pred[5120]{0:T(1024)(128)(4,1)} %and.664) | copy-start | bytes 15364
  357.6 7.4 %copy-start.17 = (pred[5120]{0:T(1024)(128)(4,1)S(1)}, pred[5120]{0:T(1024)(128)(4,1)}, u32[]{:S(2)}) copy-start(pred[5120]{0:T(1024)(128)(4,1)} %and.666) | copy-start | bytes 15364
  357.6 7.4 %copy-start.18 = (pred[5120]{0:T(1024)(128)(4,1)S(1)}, pred[5120]{0:T(1024)(128)(4,1)}, u32[]{:S(2)}) copy-start(pred[5120]{0:T(1024)(128)(4,1)} %and.668) | copy-start | bytes 15364
  357.6 7.4 %copy-start.19 = (pred[5120]{0:T(1024)(128)(4,1)S(1)}, pred[5120]{0:T(1024)(128)(4,1)}, u32[]{:S(2)}) copy-start(pred[5120]{0:T(1024)(128)(4,1)} %and.670) | copy-start | bytes 15364
  357.6 7.4 %copy-start.20 = (pred[5120]{0:T(1024)(128)(4,1)S(1)}, pred[5120]{0:T(1024)(128)(4,1)}, u32[]{:S(2)}) copy-start(pred[5120]{0:T(1024)(128)(4,1)} %and.672) | copy-start | bytes 15364
  357.6 7.4 %copy-start.21 = (pred[5120]{0:T(1024)(128)(4,1)S(1)}, pred[5120]{0:T(1024)(128)(4,1)}, u32[]{:S(2)}) copy-start(pred[5120]{0:T(1024)(128)(4,1)} %and.674) | copy-start | bytes 15364
  357.6 7.4 %copy-start.22 = (pred[5120]{0:T(1024)(128)(4,1)S(1)}, pred[5120]{0:T(1024)(128)(4,1)}, u32[]{:S(2)}) copy-start(pred[5120]{0:T(1024)(128)(4,1)} %and.676) | copy-start | bytes 15364
  357.6 7.4 %copy-start.23 = (pred[5120]{0:T(1024)(128)(4,1)S(1)}, pred[5120]{0:T(1024)(128)(4,1)}, u32[]{:S(2)}) copy-start(pred[5120]{0:T(1024)(128)(4,1)} %and.678) | copy-start | bytes 15364
  (22 other events, 156.0 us)
Sparse Core Ops, SparseCore 0:
  10.4 86.1 all-gather.1
where the time goes:
time: 445 us; the launch traced here: 444 us
  other arithmetic  177 us (40%)
  waiting for transfers between devices  122 us (27%)
  local copies, waits for them, and re-layouts  64.1 us (14%)
  blocking collectives  27.7 us (6%)
  starting transfers between devices  25.4 us (6%)
  between operations  14.2 us (3%)
  matrix products  13 us (3%)
    convert_element_type x10, other arithmetic, fourier_table(): cos_rows = (jnp.cos(angles) * factor).astype(jnp.bfloat16)  117 us
    all_gather x1, waiting for transfers between devices, local(): lax.all_gather(spectral, 'ba', axis=3, tiled=True)[:, :, None, :, :]  86.4 us
    unnamed x1, other arithmetic  29.2 us
    and x50, local copies, waits for them, and re-layouts, depart(): matched = jnp.logical_and(lat_hit, lon_shift == lon_step)  27.3 us
    all_to_all x1, waiting for transfers between devices, local(): lax.all_to_all(sendable, 'aa', split_axis=0, concat_axis=1, tiled=True)  25 us
    all_to_all x1, blocking collectives, local(): lax.all_to_all(departed, 'ba', split_axis=2, concat_axis=0, tiled=True)  14.6 us
    all_to_all x1, blocking collectives, local(): lax.all_to_all(lon_shift, 'ba', split_axis=0, concat_axis=1, tiled=True)  13.2 us
    all_to_all x1, starting transfers between devices, local(): lax.all_to_all(sendable, 'aa', split_axis=0, concat_axis=1, tiled=True)  13 us
  transfers between devices with their start and end apart: 5, of which 3 were waited for; matrix products, arithmetic and copies ran while one was open for 7% of the time, Pallas kernels for 0%

commit v1 on v0

v1 whole, which is shorter than its diff:
```python
import math

import jax
import jax.numpy as jnp
import numpy as np
from jax import lax
from jax.experimental import pallas as pl
from jax.experimental.pallas import tpu as pltpu
from jax.sharding import PartitionSpec as P

WAVES = 1280
NLON = 5120
FL = 64
KPACK = 1281
KPAD = 1408
N_AA = 32
N_BA = 16
PAIRS = 20
HALO = 32
QUARTER = NLON // 4
BLOCK = NLON // N_BA
WINDOW = BLOCK + 2 * HALO
BF16 = jnp.bfloat16
F32 = jnp.float32
NT = (((1,), (1,)), ((), ()))
FAR = -1000.0


def params(mib):
    return pltpu.CompilerParams(vmem_limit_bytes=mib * 1024 * 1024)


def whole(count):
    return [pl.BlockSpec(memory_space=pltpu.VMEM)] * count


def wave_order():
    pairs = np.arange(WAVES // 2)
    return np.concatenate([pairs, WAVES - 1 - pairs])


def window_table():
    starts = np.arange(4)[:, None] * BLOCK - HALO
    lons = (starts + np.arange(WINDOW)[None, :]).reshape(-1)
    phases = wave_order()[:, None] * lons[None, :] % NLON
    angles = phases.astype(np.float32) * np.float32(2.0 * math.pi / NLON)
    factor = np.float32(1.0 / math.sqrt(WAVES))
    table = np.concatenate([np.cos(angles) * factor, -np.sin(angles) * factor], axis=0)
    return table.astype(np.float32).astype(BF16)


def quarter_turns():
    turns = wave_order()[None, :] * np.arange(4)[:, None] % 4
    real = np.array([1, 0, -1, 0])[turns]
    imag = np.array([0, 1, 0, -1])[turns]
    return np.concatenate([real, imag], axis=0).astype(np.float32)


def field_order():
    c, b, f4 = np.meshgrid(np.arange(2), np.arange(N_BA), np.arange(4), indexing="ij")
    lanes = (b * 8 + c * 4 + f4).reshape(-1)
    return (lanes[:, None] == np.arange(128)[None, :]).astype(np.float32).astype(BF16)


def legendre_kernel(pairs_ref, rows_ref, out_ref):
    column = lax.broadcasted_iota(jnp.int32, (1, KPAD), 1)
    for which, (first, count, spec) in enumerate(((0, 32, 40), (32, 8, 48))):
        lower = (column < WAVES - pairs_ref[which]).astype(F32)
        values = rows_ref[:, spec : spec + 8, :].reshape(128, KPAD)
        right = jnp.concatenate(
            [values * lower.astype(BF16), values * (1.0 - lower).astype(BF16)], axis=0
        )
        left = rows_ref[:, first : first + count, :].reshape(N_BA * count, KPAD)
        out = lax.dot_general(left, right, NT, preferred_element_type=F32).astype(BF16)
        out_ref[:, first : first + count, :] = out.reshape(N_BA, count, 256)


def synthesis_kernel(slots_ref, turns_ref, fields_ref, coef_ref, table_ref, out_ref, left_ref):
    rows = coef_ref[...].reshape(WAVES, 128)
    turned = lax.dot_general(fields_ref[...], rows, NT, preferred_element_type=F32).astype(BF16)
    place = lax.broadcasted_iota(jnp.int32, (WAVES, WAVES), 0)
    chosen = (place == slots_ref[...]).astype(F32).astype(BF16)
    ordered = lax.dot_general(turned, chosen, NT, preferred_element_type=F32)
    real, imag = ordered[:FL], ordered[FL:]
    for q in range(4):
        alpha, beta = turns_ref[q : q + 1, :], turns_ref[4 + q : 5 + q, :]
        here = pl.ds(q * FL, FL)
        left_ref[here, :WAVES] = (real * alpha - imag * beta).astype(BF16)
        left_ref[here, WAVES:] = (imag * alpha + real * beta).astype(BF16)
    for w in range(4):
        part = jnp.dot(
            left_ref[...],
            table_ref[:, w * WINDOW : (w + 1) * WINDOW],
            preferred_element_type=F32,
        ).astype(BF16)
        for q in range(4):
            out_ref[4 * q + w] = part[q * FL : (q + 1) * FL]


def band(target, first, count):
    offset = lax.broadcasted_iota(jnp.int32, (count, 128), 0) + (first - 96)
    distance = jnp.abs(offset.astype(F32).astype(BF16) - target.astype(BF16))
    inner = 0.875 - 0.625 * distance
    outer = jnp.minimum(0.0625 * distance - 0.15625, 0.0)
    return jnp.maximum(inner, outer).astype(BF16)


def depart_kernel(target_ref, top_ref, grid_ref, bottom_ref, out_ref, *bands):
    for held in bands:
        held[...] = jnp.zeros_like(held)
    count = out_ref.shape[0]

    def one_row(row, sources):
        for t, (lanes, last) in enumerate(((256, 176), (256, 176), (128, 112))):
            for step in range(3):
                target = target_ref[row, step : step + 1, t * 128 : (t + 1) * 128]
                target = jnp.broadcast_to(target, (last - 16, 128))
                bands[t][step * lanes + 16 : step * lanes + last, :] = band(target, 16, last - 16)
            left = jnp.concatenate([s[:, t * 128 : t * 128 + lanes] for s in sources], axis=1)
            out = jnp.dot(left, bands[t][...], preferred_element_type=F32).astype(BF16)
            width = min(128, BLOCK - t * 128)
            out_ref[row, :, t * 128 : t * 128 + width] = out[:, :width]

    one_row(0, (top_ref, grid_ref.at[0], grid_ref.at[1]))

    @pl.loop(1, count - 1)
    def _(row):
        one_row(row, (grid_ref.at[row - 1], grid_ref.at[row], grid_ref.at[row + 1]))

    one_row(count - 1, (grid_ref.at[count - 2], grid_ref.at[count - 1], bottom_ref))


def send_rows(legendre, spectral):
    rows = legendre.reshape(PAIRS, N_AA, KPACK)
    values = spectral.transpose(0, 2, 3, 1).reshape(PAIRS, 8, KPACK)
    packed = jnp.concatenate(
        [
            rows[:N_BA],
            rows[N_BA:].reshape(N_BA, 8, KPACK),
            values[:N_BA],
            jnp.repeat(values[N_BA:], 4, axis=0),
        ],
        axis=1,
    )
    return jnp.pad(packed, ((0, 0), (0, 0), (0, KPAD - KPACK)))


def legendre_sums(pairs, rows):
    return pl.pallas_call(
        legendre_kernel,
        out_shape=jax.ShapeDtypeStruct((N_BA, 40, 256), BF16),
        in_specs=[pl.BlockSpec(memory_space=pltpu.SMEM)] + whole(1),
        out_specs=whole(1)[0],
        compiler_params=params(24),
        name="legendre_sums",
    )(pairs, rows)


def synthesize(slots, coefficients):
    return pl.pallas_call(
        synthesis_kernel,
        out_shape=jax.ShapeDtypeStruct((N_BA, FL, WINDOW), BF16),
        in_specs=whole(5),
        out_specs=whole(1)[0],
        scratch_shapes=[pltpu.VMEM((4 * FL, 2 * WAVES), BF16)],
        compiler_params=params(32),
        name="synthesize",
    )(
        slots,
        jnp.asarray(quarter_turns()),
        jnp.asarray(field_order()),
        coefficients,
        jnp.asarray(window_table()),
    )


def depart(targets, top, grid, bottom):
    return pl.pallas_call(
        depart_kernel,
        out_shape=jax.ShapeDtypeStruct((N_BA, FL, BLOCK), BF16),
        in_specs=whole(4),
        out_specs=whole(1)[0],
        scratch_shapes=[
            pltpu.VMEM((768, 128), BF16),
            pltpu.VMEM((768, 128), BF16),
            pltpu.VMEM((384, 128), BF16),
        ],
        compiler_params=params(24),
        name="depart",
    )(targets, top, grid, bottom)


def depart_targets(lat_shift, lon_shift):
    x = jnp.arange(BLOCK, dtype=jnp.int32) % 128
    centre = (x + lon_shift).astype(F32) + (HALO - 1 + 1.5 - 96)
    targets = jnp.stack([jnp.where(lat_shift == s, centre, FAR) for s in (-1, 0, 1)], axis=1)
    return jnp.pad(targets, ((0, 0), (0, 0), (0, WINDOW - BLOCK)), constant_values=FAR)


def wave_places(slot_pairs):
    places = slot_pairs.reshape(N_AA, 1, PAIRS) + (jnp.arange(2) * (WAVES // 2))[None, :, None]
    return places.reshape(1, WAVES).astype(jnp.int32)


def local(legendre, spectral, slot_pairs, lat_shift, lon_shift):
    first = lax.axis_index("aa") * PAIRS
    own = lax.axis_index("ba")
    pairs = jnp.stack([slot_pairs[first + own], slot_pairs[first + N_BA + own // 4]])
    rows = lax.all_to_all(send_rows(legendre, spectral), "ba", 0, 0, tiled=True)
    sums = lax.all_to_all(legendre_sums(pairs, rows), "ba", 0, 0, tiled=True)
    by_pair = jnp.concatenate([sums[:, :N_AA], sums[:, N_AA:].reshape(4, N_AA, 256)], axis=0)
    by_row = by_pair.reshape(PAIRS, N_AA, 2, 128).transpose(1, 2, 0, 3).reshape(N_AA, 40, 128)
    coefficients = lax.all_to_all(by_row, "aa", 0, 0, tiled=True)
    blocks = synthesize(wave_places(slot_pairs), coefficients)
    grid = lax.all_to_all(blocks, "ba", 0, 0, tiled=True)
    ends = N_AA - 1
    top = lax.ppermute(grid[N_BA - 1], "aa", [(i, i + 1) for i in range(ends)])
    bottom = lax.ppermute(grid[0], "aa", [(i + 1, i) for i in range(ends)])
    return depart(depart_targets(lat_shift, lon_shift), top, grid, bottom)


def solution(mesh):
    placed = (
        P("aa", None, "ba", None, None),
        P("aa", None, None, "ba"),
        P(),
        P("aa", "ba"),
        P("aa", "ba"),
    )
    return jax.shard_map(
        local, mesh=mesh, in_specs=placed, out_specs=P("aa", None, "ba"), check_vma=False
    )
```

time: 445 us -> 145 us (0.33)
  other arithmetic: 177 us -> 3.2 us
  local copies, waits for them, and re-layouts: 64.1 us -> 8.66 us
  waiting for transfers between devices: 122 us -> 67.4 us
  between operations: 14.2 us -> 0.25 us
  matrix products: 13 us -> 0 us
  Pallas kernels: 0 us -> 12.6 us
  blocking collectives: 27.7 us -> 15.2 us
  starting transfers between devices: 25.4 us -> 37.2 us
    convert_element_type x12 -> x0, other arithmetic: 129 us -> none  [the longest x10 117 us: fourier_table(): cos_rows = (jnp.cos(angles) * factor).astype(jnp.bfloat16)]
    all_gather x1 -> x0, waiting for transfers between devices: 86.4 us -> none  [local(): lax.all_gather(spectral, 'ba', axis=3, tiled=True)[:, :, None, :, :]]
    unnamed x1 -> x0, other arithmetic: 29.2 us -> none
    all_to_all x2 -> x3, waiting for transfers between devices: 35.7 us -> 64.5 us  [the longest x1 27.3 us: local(): rows = lax.all_to_all(send_rows(legendre, spectral), 'ba', 0, 0, tiled=True)]
    and x50 -> x0, local copies, waits for them, and re-layouts: 27.3 us -> none  [depart(): matched = jnp.logical_and(lat_hit, lon_shift == lon_step)]
    all_to_all x2 -> x3, starting transfers between devices: 16.5 us -> 31.4 us  [the longest x1 20 us: local(): coefficients = lax.all_to_all(by_row, 'aa', 0, 0, tiled=True)]
    dot_general x11 -> x0, matrix products: 13 us -> none  [the longest x1 7.38 us: local(): jnp.einsum('plk,pkjcf->lpjcf', leg_rows, selected, preferred_element_type...]
    pallas_call x0 -> x3, Pallas kernels: none -> 12.6 us  [the longest x1 6.2 us: depart(): pl.pallas_call(depart_kernel, out_shape=jax.ShapeDtypeStruct((N_BA, FL, B...]
  transfers between devices with their start and end apart: 5 -> 5, of which waited for: 3 -> 4; matrix products, arithmetic and copies ran while one was open for 7% -> 2% of each run, Pallas kernels for 0% -> 0%
where the time goes in v1:
time: 145 us
  waiting for transfers between devices  67.4 us (46%)
  starting transfers between devices  37.2 us (26%)
  blocking collectives  15.2 us (10%)
  Pallas kernels  12.6 us (9%)
  local copies, waits for them, and re-layouts  8.66 us (6%)
  other arithmetic  3.2 us (2%)
    all_to_all x1, waiting for transfers between devices, local(): rows = lax.all_to_all(send_rows(legendre, spectral), 'ba', 0, 0, tiled=True)  27.3 us
    all_to_all x1, waiting for transfers between devices, local(): coefficients = lax.all_to_all(by_row, 'aa', 0, 0, tiled=True)  24.7 us
    all_to_all x1, starting transfers between devices, local(): coefficients = lax.all_to_all(by_row, 'aa', 0, 0, tiled=True)  20 us
    all_to_all x1, blocking collectives, local(): sums = lax.all_to_all(legendre_sums(pairs, rows), 'ba', 0, 0, tiled=True)  15.2 us
    all_to_all x1, waiting for transfers between devices, local(): grid = lax.all_to_all(blocks, 'ba', 0, 0, tiled=True)  12.5 us
    all_to_all x1, starting transfers between devices, local(): rows = lax.all_to_all(send_rows(legendre, spectral), 'ba', 0, 0, tiled=True)  7.72 us
    pallas_call x1, Pallas kernels, depart(): pl.pallas_call(depart_kernel, out_shape=jax.ShapeDtypeStruct((N_BA, FL, B...  6.2 us
    pallas_call x1, Pallas kernels, synthesize(): pl.pallas_call(synthesis_kernel, out_shape=jax.ShapeDtypeStruct((N_BA, FL...  5.1 us
  transfers between devices with their start and end apart: 5, of which 4 were waited for; matrix products, arithmetic and copies ran while one was open for 2% of the time, Pallas kernels for 0%

profile of v1, /device:TPU:1, one launch (start us, length us, event | category | flops | bytes accessed | tf_op | source)
XLA Modules:
  0.0 144.6 jit_solution(8345524450093659031)
XLA Ops:
  0.0 1.2 slice.46
  1.2 0.9 slice.47
  2.2 0.2 slice.38
  2.4 1.0 slice.36
  3.4 0.1 slice_bitcast_fusion
  3.6 1.6 %fusion.6 = bf16[16,56,1408]{2,1,0:T(8,128)(2,1)} fusion(bf16[16,8,1281]{2,1,0:T(8,128)(2,1)S(1)} %bitcast.24, bf16[16,8,1281]{2,1,0:T(8,128)(2,1)S(1)} %slice.38, bf16[16,8,1281]{2,1,0:T(8,128)(2,1)S(1)} %bitcast.23, bf16[16,32,1281]{2,1,0:T(8,128)(2,1)S(1)} %slice_bitcast_fusion), kind=kLoop, calls=%fused_computation.7 | loop fusion | flops 16400384 | bytes 4818688 | tf_op jit(solution)/shard_map/concatenate | solution.py:136
  5.2 7.7 %all-to-all-start = ((bf16[16,56,1408]{2,1,0:T(8,128)(2,1)}), bf16[16,56,1408]{2,1,0:T(8,128)(2,1)S(1)}, u32[]{:S(2)}, u32[]{:S(2)}) async-start(bf16[16,56,1408]{2,1,0:T(8,128)(2,1)} %fusion.6), calls=%async_computation | async-start | bytes 5046272 | tf_op jit(solution)/shard_map/all_to_all | solution.py:209
  13.0 0.6 fusion.10
  13.6 1.3 pad_add_fusion.pairs_ref
  14.9 27.3 %all-to-all-done.rows_ref = bf16[16,56,1408]{2,1,0:T(8,128)(2,1)S(1)} async-done(((bf16[16,56,1408]{2,1,0:T(8,128)(2,1)}), bf16[16,56,1408]{2,1,0:T(8,128)(2,1)S(1)}, u32[]{:S(2)}, u32[]{:S(2)}) %all-to-all-start) | async-done | bytes 2523168 | tf_op jit(solution)/shard_map/all_to_all | solution.py:209
  42.2 1.3 legendre_sums.1
  43.6 15.2 %all_to_all.20 = bf16[16,40,256]{2,1,0:T(8,128)(2,1)S(1)} all-to-all(bf16[16,40,256]{2,1,0:T(8,128)(2,1)S(1)} %legendre_sums.1), channel_id=1, replica_groups=mesh['aa'=32,'ba'=16] {'ba'}, dimensions={0} | all-to-all | bytes 655360 | tf_op jit(solution)/shard_map/all_to_all | solution.py:210
  58.9 0.9 copy.19
  59.8 20.0 %all-to-all-start.2 = ((bf16[32,40,128]{2,1,0:T(8,128)(2,1)}), bf16[32,40,128]{2,1,0:T(8,128)(2,1)S(1)}, u32[]{:S(2)}, u32[]{:S(2)}) async-start(bf16[32,40,128]{2,1,0:T(8,128)(2,1)} %copy.19), calls=%async_computation.2 | async-start | bytes 655360 | tf_op jit(solution)/shard_map/all_to_all | solution.py:213
  80.0 0.1 add.78.slots_ref
  80.1 24.7 %all-to-all-done.2.coef_ref = bf16[32,40,128]{2,1,0:T(8,128)(2,1)S(1)} async-done(((bf16[32,40,128]{2,1,0:T(8,128)(2,1)}), bf16[32,40,128]{2,1,0:T(8,128)(2,1)S(1)}, u32[]{:S(2)}, u32[]{:S(2)}) %all-to-all-start.2) | async-done | bytes 327712 | tf_op jit(solution)/shard_map/all_to_all | solution.py:213
  104.8 3.2 %copy-done = bf16[2560,1536]{1,0:T(8,128)(2,1)S(1)} copy-done((bf16[2560,1536]{1,0:T(8,128)(2,1)S(1)}, bf16[2560,1536]{1,0:T(8,128)(2,1)}, u32[]{:S(2)}) %copy-start) | copy-done | bytes 7864344
  108.1 5.1 %synthesize.1 = bf16[16,64,384]{2,1,0:T(8,128)(2,1)} custom-call(s32[1,1280]{1,0:T(1,128)S(1)} %add.78.slots_ref, f32[8,1280]{1,0:T(8,128)S(1)} %copy-done.1, bf16[128,128]{1,0:T(8,128)(2,1)S(1)} %copy-done.2, bf16[32,40,128]{2,1,0:T(8,128)(2,1)S(1)} %all-to-all-done.2.coef_ref, bf16[2560,1536]{1,0:T(8,128)(2,1)S(1)} %copy-done), custom_call_target="tpu_custom_call" | custom-call | tf_op jit(solution)/shard_map/synthesize/pallas_call | solution.py:160
  113.2 3.6 %all-to-all-start.3 = ((bf16[16,64,384]{2,1,0:T(8,128)(2,1)}), bf16[16,64,384]{2,1,0:T(8,128)(2,1)S(1)}, u32[]{:S(2)}, u32[]{:S(2)}) async-start(bf16[16,64,384]{2,1,0:T(8,128)(2,1)} %synthesize.1), calls=%async_computation.3 | async-start | bytes 1572864 | tf_op jit(solution)/shard_map/all_to_all | solution.py:215
  117.0 12.5 %all-to-all-done.3.grid_ref = bf16[16,64,384]{2,1,0:T(8,128)(2,1)S(1)} async-done(((bf16[16,64,384]{2,1,0:T(8,128)(2,1)}), bf16[16,64,384]{2,1,0:T(8,128)(2,1)S(1)}, u32[]{:S(2)}, u32[]{:S(2)}) %all-to-all-start.3) | async-done | bytes 786464 | tf_op jit(solution)/shard_map/all_to_all | solution.py:215
  129.5 3.4 %collective-permute-start = (bf16[64,384]{1,0:T(8,128)(2,1)S(1)}, bf16[64,384]{1,0:T(8,128)(2,1)S(1)}, u32[]{:S(2)}, u32[]{:S(2)}) collective-permute-start(bf16[64,384]{1,0:T(8,128)(2,1)S(1)} %get-tuple-element.6), channel_id=1, source_target_pairs={{0,16},{16,32},{32,48},{48,64},{64,80},{80,96},{96,112},{112,128},... | collective-permute-start | bytes 147464 | tf_op jit(solution)/shard_map/ppermute | solution.py:217
  133.0 2.4 %collective-permute-start.1 = (bf16[64,384]{1,0:T(8,128)(2,1)S(1)}, bf16[64,384]{1,0:T(8,128)(2,1)S(1)}, u32[]{:S(2)}, u32[]{:S(2)}) collective-permute-start(bf16[64,384]{1,0:T(8,128)(2,1)S(1)} %get-tuple-element.5), channel_id=1, source_target_pairs={{16,0},{32,16},{48,32},{64,48},{80,64},{96,80},{112,96},{128,112},... | collective-permute-start | bytes 147464 | tf_op jit(solution)/shard_map/ppermute | solution.py:218
  135.5 2.9 %collective-permute-done.1.bottom_ref = bf16[64,384]{1,0:T(8,128)(2,1)S(1)} collective-permute-done((bf16[64,384]{1,0:T(8,128)(2,1)S(1)}, bf16[64,384]{1,0:T(8,128)(2,1)S(1)}, u32[]{:S(2)}, u32[]{:S(2)}) %collective-permute-start.1) | collective-permute-done | bytes 49184 | tf_op jit(solution)/shard_map/ppermute | solution.py:218
  138.4 6.2 %depart.1 = bf16[16,64,320]{2,1,0:T(8,128)(2,1)} custom-call(f32[16,3,384]{2,1,0:T(4,128)S(1)} %select_maximum_fusion.target_ref, bf16[64,384]{1,0:T(8,128)(2,1)S(1)} %collective-permute-done.top_ref, bf16[16,64,384]{2,1,0:T(8,128)(2,1)S(1)} %all-to-all-done.3.grid_ref, bf16[64,384]{1,0:T(8,128)(2,1)S(1)} %collective-permute-done.1.bottom_ref), custom_call_target="tpu_custom_call" | custom-call | tf_op jit(solution)/shard_map/depart/pallas_call | solution.py:178
  (31 shorter events, 0.6 us)
Async XLA Ops:
  0.0 3.4 %copy-start.3 = (bf16[20,32,1,1,1281]{4,1,3,2,0:T(8,128)(2,1)S(1)}, bf16[20,32,1,1,1281]{4,1,3,2,0:T(8,128)(2,1)}, u32[]{:S(2)}) copy-start(bf16[20,32,1,1,1281]{4,1,3,2,0:T(8,128)(2,1)} %param.8) | copy-start | bytes 4919044
  5.2 7.8 %copy-start.6 = (s32[640]{0:T(1024)S(1)}, s32[640]{0:T(1024)}, u32[]{:S(2)}) copy-start(s32[640]{0:T(1024)} %param.10) | copy-start | bytes 7684
  5.2 37.0 %all-to-all-start = ((bf16[16,56,1408]{2,1,0:T(8,128)(2,1)}), bf16[16,56,1408]{2,1,0:T(8,128)(2,1)S(1)}, u32[]{:S(2)}, u32[]{:S(2)}) async-start(bf16[16,56,1408]{2,1,0:T(8,128)(2,1)} %fusion.6), calls=%async_computation | async-start | bytes 5046272 | tf_op jit(solution)/shard_map/all_to_all | solution.py:209
  43.6 61.3 %copy-start.1 = (f32[8,1280]{1,0:T(8,128)S(1)}, f32[8,1280]{1,0:T(8,128)}, u32[]{:S(2)}) copy-start(f32[8,1280]{1,0:T(8,128)} %constant.63.clone.turns_ref) | copy-start | bytes 122884
  43.6 61.3 %copy-start.2 = (bf16[128,128]{1,0:T(8,128)(2,1)S(1)}, bf16[128,128]{1,0:T(8,128)(2,1)}, u32[]{:S(2)}) copy-start(bf16[128,128]{1,0:T(8,128)(2,1)} %constant.64.clone.fields_ref) | copy-start | bytes 98308
  59.8 45.1 %all-to-all-start.2 = ((bf16[32,40,128]{2,1,0:T(8,128)(2,1)}), bf16[32,40,128]{2,1,0:T(8,128)(2,1)S(1)}, u32[]{:S(2)}, u32[]{:S(2)}) async-start(bf16[32,40,128]{2,1,0:T(8,128)(2,1)} %copy.19), calls=%async_computation.2 | async-start | bytes 655360 | tf_op jit(solution)/shard_map/all_to_all | solution.py:213
  104.8 3.2 %copy-start = (bf16[2560,1536]{1,0:T(8,128)(2,1)S(1)}, bf16[2560,1536]{1,0:T(8,128)(2,1)}, u32[]{:S(2)}) copy-start(bf16[2560,1536]{1,0:T(8,128)(2,1)} %constant.65.clone.table_ref) | copy-start | bytes 23592964
  108.1 8.7 %copy-start.4 = (s32[16,320]{1,0:T(8,128)S(1)}, s32[16,320]{1,0:T(8,128)}, u32[]{:S(2)}) copy-start(s32[16,320]{1,0:T(8,128)} %param.11) | copy-start | bytes 61444
  108.1 8.8 %copy-start.5 = (s32[16,320]{1,0:T(8,128)S(1)}, s32[16,320]{1,0:T(8,128)}, u32[]{:S(2)}) copy-start(s32[16,320]{1,0:T(8,128)} %param.12) | copy-start | bytes 61444
  113.2 16.3 %all-to-all-start.3 = ((bf16[16,64,384]{2,1,0:T(8,128)(2,1)}), bf16[16,64,384]{2,1,0:T(8,128)(2,1)S(1)}, u32[]{:S(2)}, u32[]{:S(2)}) async-start(bf16[16,64,384]{2,1,0:T(8,128)(2,1)} %synthesize.1), calls=%async_computation.3 | async-start | bytes 1572864 | tf_op jit(solution)/shard_map/all_to_all | solution.py:215
  129.5 6.0 %collective-permute-start = (bf16[64,384]{1,0:T(8,128)(2,1)S(1)}, bf16[64,384]{1,0:T(8,128)(2,1)S(1)}, u32[]{:S(2)}, u32[]{:S(2)}) collective-permute-start(bf16[64,384]{1,0:T(8,128)(2,1)S(1)} %get-tuple-element.6), channel_id=1, source_target_pairs={{0,16},{16,32},{32,48},{48,64},{64,80},{80,96},{96,112},{112,128},... | collective-permute-start | bytes 147464 | tf_op jit(solution)/shard_map/ppermute | solution.py:217
  133.0 5.4 %collective-permute-start.1 = (bf16[64,384]{1,0:T(8,128)(2,1)S(1)}, bf16[64,384]{1,0:T(8,128)(2,1)S(1)}, u32[]{:S(2)}, u32[]{:S(2)}) collective-permute-start(bf16[64,384]{1,0:T(8,128)(2,1)S(1)} %get-tuple-element.5), channel_id=1, source_target_pairs={{16,0},{32,16},{48,32},{64,48},{80,64},{96,80},{112,96},{128,112},... | collective-permute-start | bytes 147464 | tf_op jit(solution)/shard_map/ppermute | solution.py:218

commit v2 on v1

v2 whole, which is shorter than its diff:
```python
import math

import jax
import jax.numpy as jnp
import numpy as np
from jax import lax
from jax.experimental import pallas as pl
from jax.experimental.pallas import tpu as pltpu
from jax.sharding import PartitionSpec as P

WAVES = 1280
NLON = 5120
FL = 64
KPACK = 1281
KTILES = 10
TILES = 7 * KTILES + 1
N_AA = 32
N_BA = 16
PAIRS = 20
HALO = 32
QUARTER = NLON // 4
BLOCK = NLON // N_BA
WINDOW = BLOCK + 2 * HALO
BF16 = jnp.bfloat16
F32 = jnp.float32
NT = (((1,), (1,)), ((), ()))
FAR = -1000.0


def params(mib):
    return pltpu.CompilerParams(vmem_limit_bytes=mib * 1024 * 1024)


def whole(count):
    return [pl.BlockSpec(memory_space=pltpu.VMEM)] * count


def wave_order():
    pairs = np.arange(WAVES // 2)
    return np.concatenate([pairs, WAVES - 1 - pairs])


def window_table():
    starts = np.arange(2)[:, None] * BLOCK - HALO
    lons = (starts + np.arange(WINDOW)[None, :]).reshape(-1)
    phases = wave_order()[:, None] * lons[None, :] % NLON
    angles = phases.astype(np.float32) * np.float32(2.0 * math.pi / NLON)
    factor = np.float32(1.0 / math.sqrt(WAVES))
    table = np.stack([np.cos(angles) * factor, -np.sin(angles) * factor], axis=0)
    return table.astype(np.float32).astype(BF16)


def mirror():
    x = np.arange(WINDOW)
    return (x[:, None] + x[None, :] == WINDOW).astype(np.float32).astype(BF16)


def quarter_turns():
    turns = wave_order()[None, :] * np.arange(4)[:, None] % 4
    real = np.array([1, 0, -1, 0])[turns]
    imag = np.array([0, 1, 0, -1])[turns]
    return np.concatenate([real, imag], axis=0).astype(np.float32)


def field_order():
    c, b, f4 = np.meshgrid(np.arange(2), np.arange(N_BA), np.arange(4), indexing="ij")
    lanes = (b * 8 + c * 4 + f4).reshape(-1)
    return (lanes[:, None] == np.arange(128)[None, :]).astype(np.float32).astype(BF16)


def pack_kernel(main_ref, shared_ref, main_values_ref, shared_values_ref, out_ref):
    lane = lax.broadcasted_iota(jnp.int32, (8, 128), 1)
    for h in range(4):
        last = jnp.zeros((8, 128), F32)
        for g in range(7):
            for k in range(KTILES + 1):
                here = slice(128 * k, min(128 * k + 128, KPACK))
                if g < 4:
                    tile = main_ref[h, 8 * g : 8 * g + 8, here]
                elif g == 4:
                    tile = shared_ref[0, 8 * h : 8 * h + 8, here]
                else:
                    ref, at = ((main_values_ref, h), (shared_values_ref, 0))[g - 5]
                    tile = ref[at, :, :, here].reshape(8, here.stop - here.start)
                if k < KTILES:
                    out_ref[h, 7 * k + g] = tile
                else:
                    column = jnp.broadcast_to(tile.astype(F32), (8, 128))
                    last = jnp.where(lane == g, column, last)
        out_ref[h, TILES - 1] = last.astype(BF16)


def legendre_kernel(pairs_ref, rows_ref, out_ref):
    column = lax.broadcasted_iota(jnp.int32, (1, 128 * KTILES), 1)
    lane = lax.broadcasted_iota(jnp.int32, (1, 128), 1)
    last = rows_ref[:, TILES - 1]
    for which, (first, count, value) in enumerate(((0, 4, 5), (4, 1, 6))):
        total = N_BA * 8 * count
        left = [
            rows_ref[:, 7 * k + first : 7 * k + first + count].reshape(total, 128)
            for k in range(KTILES)
        ]
        ends = [last * (lane == first + g).astype(F32).astype(BF16) for g in range(count)]
        left.append(jnp.stack(ends, axis=1).reshape(total, 128))
        values = [rows_ref[:, 7 * k + value].reshape(128, 128) for k in range(KTILES)]
        values = jnp.concatenate(values, axis=1)
        end = last.reshape(128, 128)[:, value : value + 1].astype(F32)
        end = jnp.broadcast_to(end, (128, 128)).astype(BF16)
        lower = (column < WAVES - pairs_ref[which]).astype(F32)
        right = jnp.concatenate(
            [
                jnp.concatenate([values * lower.astype(BF16), jnp.zeros_like(end)], axis=1),
                jnp.concatenate([values * (1.0 - lower).astype(BF16), end], axis=1),
            ],
            axis=0,
        )
        left = jnp.concatenate(left, axis=1)
        out = lax.dot_general(left, right, NT, preferred_element_type=F32).astype(BF16)
        out_ref[:, 8 * first : 8 * (first + count), :] = out.reshape(N_BA, 8 * count, 256)


def synthesis_kernel(
    chosen_ref, turns_ref, fields_ref, mirror_ref, coef_ref, table_ref, out_ref, left_ref, held_ref, sems
):
    copies = [
        pltpu.make_async_copy(table_ref.at[c], held_ref.at[c], sems.at[c]) for c in range(2)
    ]
    for copy in copies:
        copy.start()
    rows = coef_ref[...].reshape(WAVES, 128)
    turned = lax.dot_general(fields_ref[...], rows, NT, preferred_element_type=F32).astype(BF16)
    ordered = lax.dot_general(turned, chosen_ref[...], NT, preferred_element_type=F32)
    real, imag = ordered[:FL], ordered[FL:]
    for q in range(4):
        alpha, beta = turns_ref[q : q + 1, :], turns_ref[4 + q : 5 + q, :]
        here = pl.ds(q * FL, FL)
        left_ref[0, here, :] = (real * alpha - imag * beta).astype(BF16)
        left_ref[1, here, :] = (imag * alpha + real * beta).astype(BF16)
    copies[0].wait()
    even = jnp.dot(left_ref[0], held_ref[0], preferred_element_type=F32)
    copies[1].wait()
    odd = jnp.dot(left_ref[1], held_ref[1], preferred_element_type=F32)
    ahead, behind = (even + odd).astype(BF16), (even - odd).astype(BF16)
    for w in range(2):
        lanes = slice(w * WINDOW, (w + 1) * WINDOW)
        back = jnp.dot(behind[:, lanes], mirror_ref[...], preferred_element_type=F32).astype(BF16)
        for q in range(4):
            here = slice(q * FL, (q + 1) * FL)
            out_ref[4 * q + w] = ahead[here, lanes]
            out_ref[(4 * q + N_BA - 1 - w) % N_BA] = back[here]


def band(target, first, count):
    offset = lax.broadcasted_iota(jnp.int32, (count, 128), 0) + (first - 96)
    distance = jnp.abs(offset.astype(F32).astype(BF16) - target.astype(BF16))
    inner = 0.875 - 0.625 * distance
    outer = jnp.minimum(0.0625 * distance - 0.15625, 0.0)
    return jnp.maximum(inner, outer).astype(BF16)


def clear(bands):
    for held in bands:
        held[...] = jnp.zeros_like(held)


def depart_row(target_ref, at, sources, bands, out_ref, to):
    for t, (part, lanes, last, first) in enumerate(((0, 384, 176, 0), (0, 384, 176, 128), (1, 128, 112, 0))):
        for step in range(3):
            target = target_ref[at, step : step + 1, t * 128 : (t + 1) * 128]
            target = jnp.broadcast_to(target, (last - 16, 128))
            begin = step * lanes + first + 16
            bands[part][begin : begin + last - 16, first : first + 128] = band(target, 16, last - 16)
    for part, (lane, x, width) in enumerate(((0, 0, 256), (256, 256, 64))):
        left = jnp.concatenate([s[:, lane:] for s in sources], axis=1)
        out = jnp.dot(left, bands[part][...], preferred_element_type=F32).astype(BF16)
        out_ref[to, :, x : x + width] = out[:, :width]


def inner_kernel(target_ref, grid_ref, out_ref, *bands):
    clear(bands)

    @pl.loop(1, N_BA - 1, unroll=7)
    def _(row):
        sources = [grid_ref.at[row - 1], grid_ref.at[row], grid_ref.at[row + 1]]
        depart_row(target_ref, row, sources, bands, out_ref, row)


def edge_kernel(inner_ref, target_ref, top_ref, grid_ref, bottom_ref, out_ref, *bands):
    clear(bands)

    @pl.when(pl.program_id(0) == 0)
    def _():
        sources = [top_ref, grid_ref.at[0], grid_ref.at[1]]
        depart_row(target_ref, 0, sources, bands, out_ref, 0)

    @pl.when(pl.program_id(0) == 1)
    def _():
        sources = [grid_ref.at[N_BA - 2], grid_ref.at[N_BA - 1], bottom_ref]
        depart_row(target_ref, N_BA - 1, sources, bands, out_ref, 0)


def pack(legendre, spectral):
    rows = legendre.reshape(PAIRS, N_AA, KPACK)
    values = spectral.transpose(0, 2, 3, 1)
    return pl.pallas_call(
        pack_kernel,
        grid=(4,),
        out_shape=jax.ShapeDtypeStruct((N_BA, TILES, 8, 128), BF16),
        in_specs=[
            pl.BlockSpec((4, N_AA, KPACK), lambda q: (q, 0, 0)),
            pl.BlockSpec((1, N_AA, KPACK), lambda q: (N_BA + q, 0, 0)),
            pl.BlockSpec((4, 2, 4, KPACK), lambda q: (q, 0, 0, 0)),
            pl.BlockSpec((1, 2, 4, KPACK), lambda q: (N_BA + q, 0, 0, 0)),
        ],
        out_specs=pl.BlockSpec((4, TILES, 8, 128), lambda q: (q, 0, 0, 0)),
        compiler_params=params(58),
        name="pack",
    )(rows, rows, values, values)


def legendre_sums(pairs, rows):
    return pl.pallas_call(
        legendre_kernel,
        out_shape=jax.ShapeDtypeStruct((N_BA, 40, 256), BF16),
        in_specs=[pl.BlockSpec(memory_space=pltpu.SMEM)] + whole(1),
        out_specs=whole(1)[0],
        compiler_params=params(24),
        name="legendre_sums",
    )(pairs, rows)


def synthesize(chosen, coefficients):
    return pl.pallas_call(
        synthesis_kernel,
        out_shape=jax.ShapeDtypeStruct((N_BA, FL, WINDOW), BF16),
        in_specs=whole(5) + [pl.BlockSpec(memory_space=pl.ANY)],
        out_specs=whole(1)[0],
        scratch_shapes=[
            pltpu.VMEM((2, 4 * FL, WAVES), BF16),
            pltpu.VMEM((2, WAVES, 2 * WINDOW), BF16),
            pltpu.SemaphoreType.DMA((2,)),
        ],
        compiler_params=params(32),
        name="synthesize",
    )(
        chosen,
        jnp.asarray(quarter_turns()),
        jnp.asarray(field_order()),
        jnp.asarray(mirror()),
        coefficients,
        jnp.asarray(window_table()),
    )


def band_scratch():
    return [pltpu.VMEM((1152, 256), BF16), pltpu.VMEM((384, 128), BF16)]


def depart_inner(targets, grid):
    return pl.pallas_call(
        inner_kernel,
        out_shape=jax.ShapeDtypeStruct((N_BA, FL, BLOCK), BF16),
        in_specs=whole(2),
        out_specs=whole(1)[0],
        scratch_shapes=band_scratch(),
        compiler_params=params(24),
        cost_estimate=pl.CostEstimate(
            flops=2 * 14 * FL * 1920 * 128, bytes_accessed=4000000, transcendentals=0
        ),
        name="depart_inner",
    )(targets, grid)


def depart_edges(inner, targets, top, grid, bottom):
    return pl.pallas_call(
        edge_kernel,
        grid=(2,),
        out_shape=jax.ShapeDtypeStruct((N_BA, FL, BLOCK), BF16),
        in_specs=[pl.BlockSpec(memory_space=pl.ANY)] + whole(4),
        out_specs=pl.BlockSpec((1, FL, BLOCK), lambda e: (e * (N_BA - 1), 0, 0)),
        scratch_shapes=band_scratch(),
        input_output_aliases={0: 0},
        compiler_params=params(24),
        name="depart_edges",
    )(inner, targets, top, grid, bottom)


def depart_targets(lat_shift, lon_shift):
    x = jnp.arange(BLOCK, dtype=jnp.int32) % 128
    centre = (x + lon_shift).astype(F32) + (HALO - 1 + 1.5 - 96)
    targets = jnp.stack([jnp.where(lat_shift == s, centre, FAR) for s in (-1, 0, 1)], axis=1)
    return jnp.pad(targets, ((0, 0), (0, 0), (0, WINDOW - BLOCK)), constant_values=FAR)


def wave_places(slot_pairs):
    places = slot_pairs.reshape(N_AA, 1, PAIRS) + (jnp.arange(2) * (WAVES // 2))[None, :, None]
    places = places.reshape(1, WAVES).astype(jnp.int32)
    return (jnp.arange(WAVES, dtype=jnp.int32)[:, None] == places).astype(BF16)


def local(legendre, spectral, slot_pairs, lat_shift, lon_shift):
    first = lax.axis_index("aa") * PAIRS
    own = lax.axis_index("ba")
    pairs = jnp.stack([slot_pairs[first + own], slot_pairs[first + N_BA + own // 4]])
    rows = lax.all_to_all(pack(legendre, spectral), "ba", 0, 0, tiled=True)
    sums = lax.all_to_all(legendre_sums(pairs, rows), "ba", 0, 0, tiled=True)
    by_pair = jnp.concatenate([sums[:, :N_AA], sums[:, N_AA:].reshape(4, N_AA, 256)], axis=0)
    by_row = by_pair.reshape(PAIRS, N_AA, 2, 128).transpose(1, 2, 0, 3).reshape(N_AA, 40, 128)
    coefficients = lax.all_to_all(by_row, "aa", 0, 0, tiled=True)
    blocks = synthesize(wave_places(slot_pairs), coefficients)
    grid = lax.all_to_all(blocks, "ba", 0, 0, tiled=True)
    ends = N_AA - 1
    top = lax.ppermute(grid[N_BA - 1], "aa", [(i, i + 1) for i in range(ends)])
    bottom = lax.ppermute(grid[0], "aa", [(i + 1, i) for i in range(ends)])
    targets = depart_targets(lat_shift, lon_shift)
    inner = depart_inner(targets, grid)
    return depart_edges(inner, targets, top, grid, bottom)


def solution(mesh):
    placed = (
        P("aa", None, "ba", None, None),
        P("aa", None, None, "ba"),
        P(),
        P("aa", "ba"),
        P("aa", "ba"),
    )
    return jax.shard_map(
        local, mesh=mesh, in_specs=placed, out_specs=P("aa", None, "ba"), check_vma=False
    )
```

time: 145 us -> 139 us (0.959)
  blocking collectives: 15.2 us -> 0 us
  starting transfers between devices: 37.2 us -> 43.9 us
  Pallas kernels: 12.6 us -> 16 us
  local copies, waits for them, and re-layouts: 8.66 us -> 5.85 us
  waiting for transfers between devices: 67.4 us -> 68.9 us
    all_to_all x1 -> x0, blocking collectives: 15.2 us -> none  [local(): sums = lax.all_to_all(legendre_sums(pairs, rows), 'ba', 0, 0, tiled=True)]
    all_to_all x1 -> x2, starting transfers between devices: 7.72 us -> 14.9 us  [the longest x1 7.72 us: local(): rows = lax.all_to_all(pack(legendre, spectral), 'ba', 0, 0, tiled=True)]
    all_to_all x1 -> x2, waiting for transfers between devices: 27.3 us -> 32.9 us  [the longest x1 25.3 us: local(): rows = lax.all_to_all(pack(legendre, spectral), 'ba', 0, 0, tiled=True)]
    slice x6 -> x0, local copies, waits for them, and re-layouts: 3.5 us -> none  [the longest x2 1.41 us: send_rows(): values[:N_BA]]
    ppermute x1, waiting for transfers between devices: 2.88 us -> 0.01 us  [local(): bottom = lax.ppermute(grid[0], 'aa', [(i + 1, i) for i in range(ends)])]
    pallas_call x1 -> x3, Pallas kernels: 6.2 us -> 9.01 us  [the longest x1 4 us: pack(): pl.pallas_call(pack_kernel, grid=(4,), out_shape=jax.ShapeDtypeStruct((N_...]
    concatenate x1 -> x0, other arithmetic: 1.64 us -> none  [send_rows(): jnp.concatenate([rows[:N_BA], rows[N_BA:].reshape(N_BA, 8, KPACK), values...]
    unnamed x14 -> x16, local copies, waits for them, and re-layouts: 3.27 us -> 3.97 us
  transfers between devices with their start and end apart: 5 -> 6, of which waited for: 4 -> 4; matrix products, arithmetic and copies ran while one was open for 2% -> 3% of each run, Pallas kernels for 0% -> 3%
where the time goes in v2:
time: 139 us; the launch traced here: 138 us
  waiting for transfers between devices  68.9 us (50%)
  starting transfers between devices  43.9 us (32%)
  Pallas kernels  16 us (12%)
  local copies, waits for them, and re-layouts  5.85 us (4%)
  other arithmetic  3 us (2%)
    all_to_all x1, waiting for transfers between devices, local(): rows = lax.all_to_all(pack(legendre, spectral), 'ba', 0, 0, tiled=True)  25.3 us
    all_to_all x1, waiting for transfers between devices, local(): coefficients = lax.all_to_all(by_row, 'aa', 0, 0, tiled=True)  23.5 us
    all_to_all x1, starting transfers between devices, local(): coefficients = lax.all_to_all(by_row, 'aa', 0, 0, tiled=True)  19.5 us
    all_to_all x1, waiting for transfers between devices, local(): grid = lax.all_to_all(blocks, 'ba', 0, 0, tiled=True)  12.5 us
    all_to_all x1, starting transfers between devices, local(): rows = lax.all_to_all(pack(legendre, spectral), 'ba', 0, 0, tiled=True)  7.72 us
    all_to_all x1, waiting for transfers between devices, local(): sums = lax.all_to_all(legendre_sums(pairs, rows), 'ba', 0, 0, tiled=True)  7.56 us
    all_to_all x1, starting transfers between devices, local(): sums = lax.all_to_all(legendre_sums(pairs, rows), 'ba', 0, 0, tiled=True)  7.23 us
    pallas_call x1, Pallas kernels, synthesize(): pl.pallas_call(synthesis_kernel, out_shape=jax.ShapeDtypeStruct((N_BA, FL...  4.94 us
  transfers between devices with their start and end apart: 6, of which 4 were waited for; matrix products, arithmetic and copies ran while one was open for 3% of the time, Pallas kernels for 3%

profile of v2, /device:TPU:1, one launch (start us, length us, event | category | flops | bytes accessed | tf_op | source)
XLA Modules:
  0.0 137.9 jit_solution(8651486414018452172)
XLA Ops:
  0.0 4.0 %pack.1 = bf16[16,71,8,128]{3,2,1,0:T(8,128)(2,1)} custom-call(bf16[20,32,1281]{2,1,0:T(8,128)(2,1)} %bitcast.18, bf16[20,32,1281]{2,1,0:T(8,128)(2,1)} %bitcast.19, bf16[20,2,4,1281]{3,2,1,0:T(4,128)(2,1)} %bitcast.20, bf16[20,2,4,1281]{3,2,1,0:T(4,128)(2,1)} %bitcast.21), custom_call_target="tpu_custom_call" | custom-call | tf_op jit(solution)/shard_map/pack/pallas_call | solution.py:205
  4.0 7.7 %all-to-all-start = ((bf16[16,71,8,128]{3,2,1,0:T(8,128)(2,1)}), bf16[16,71,8,128]{3,2,1,0:T(8,128)(2,1)S(1)}, u32[]{:S(2)}, u32[]{:S(2)}) async-start(bf16[16,71,8,128]{3,2,1,0:T(8,128)(2,1)} %pack.1), calls=%async_computation | async-start | bytes 4653056 | tf_op jit(solution)/shard_map/all_to_all | solution.py:305
  11.8 0.7 fusion.4
  12.4 1.4 %pad_add_fusion.pairs_ref = s32[2]{0:T(128)S(1)} fusion(s32[1]{0:T(128)} %get-tuple-element.11, s32[1]{0:T(128)} %get-tuple-element.10), kind=kLoop, calls=%fused_computation.20 | loop fusion | flops 2 | bytes 16 | tf_op jit(solution)/shard_map/stack | solution.py:304
  13.8 25.3 %all-to-all-done.rows_ref = bf16[16,71,8,128]{3,2,1,0:T(8,128)(2,1)S(1)} async-done(((bf16[16,71,8,128]{3,2,1,0:T(8,128)(2,1)}), bf16[16,71,8,128]{3,2,1,0:T(8,128)(2,1)S(1)}, u32[]{:S(2)}, u32[]{:S(2)}) %all-to-all-start) | async-done | bytes 2326560 | tf_op jit(solution)/shard_map/all_to_all | solution.py:305
  39.1 2.1 %legendre_sums.1 = bf16[16,40,256]{2,1,0:T(8,128)(2,1)} custom-call(s32[2]{0:T(128)S(1)} %pad_add_fusion.pairs_ref, bf16[16,71,8,128]{3,2,1,0:T(8,128)(2,1)S(1)} %all-to-all-done.rows_ref), custom_call_target="tpu_custom_call" | custom-call | tf_op jit(solution)/shard_map/legendre_sums/pallas_call | solution.py:222
  41.2 7.2 %all-to-all-start.1 = ((bf16[16,40,256]{2,1,0:T(8,128)(2,1)}), bf16[16,40,256]{2,1,0:T(8,128)(2,1)S(1)}, u32[]{:S(2)}, u32[]{:S(2)}) async-start(bf16[16,40,256]{2,1,0:T(8,128)(2,1)} %legendre_sums.1), calls=%async_computation.1 | async-start | bytes 655360 | tf_op jit(solution)/shard_map/all_to_all | solution.py:306
  48.4 0.1 add.69
  48.5 7.6 %all-to-all-done.1 = bf16[16,40,256]{2,1,0:T(8,128)(2,1)S(1)} async-done(((bf16[16,40,256]{2,1,0:T(8,128)(2,1)}), bf16[16,40,256]{2,1,0:T(8,128)(2,1)S(1)}, u32[]{:S(2)}, u32[]{:S(2)}) %all-to-all-start.1) | async-done | bytes 327712 | tf_op jit(solution)/shard_map/all_to_all | solution.py:306
  56.2 0.9 copy.19
  57.1 19.5 %all-to-all-start.2 = ((bf16[32,40,128]{2,1,0:T(8,128)(2,1)}), bf16[32,40,128]{2,1,0:T(8,128)(2,1)}, u32[]{:S(2)}, u32[]{:S(2)}) async-start(bf16[32,40,128]{2,1,0:T(8,128)(2,1)} %copy.19), calls=%async_computation.2 | async-start | bytes 655360 | tf_op jit(solution)/shard_map/all_to_all | solution.py:309
  76.7 0.1 add.73
  76.8 1.4 %fusion.chosen_ref = bf16[1280,1280]{1,0:T(8,128)(2,1)S(1)} fusion(s32[1280]{0:T(1024)S(1)} %add.73), kind=kLoop, calls=%fused_computation.1 | loop fusion | flops 3276800 | bytes 3281920 | tf_op jit(solution)/shard_map/convert_element_type | solution.py:298
  78.2 23.5 %all-to-all-done.2.coef_ref = bf16[32,40,128]{2,1,0:T(8,128)(2,1)} async-done(((bf16[32,40,128]{2,1,0:T(8,128)(2,1)}), bf16[32,40,128]{2,1,0:T(8,128)(2,1)}, u32[]{:S(2)}, u32[]{:S(2)}) %all-to-all-start.2) | async-done | bytes 327712 | tf_op jit(solution)/shard_map/all_to_all | solution.py:309
  101.7 2.1 %copy-done = bf16[2,1280,768]{2,1,0:T(8,128)(2,1)S(1)} copy-done((bf16[2,1280,768]{2,1,0:T(8,128)(2,1)S(1)}, bf16[2,1280,768]{2,1,0:T(8,128)(2,1)}, u32[]{:S(2)}) %copy-start) | copy-done | bytes 3932184
  103.8 1.0 copy-done.2
  104.8 4.9 %synthesize.1 = bf16[16,64,384]{2,1,0:T(8,128)(2,1)S(1)} custom-call(bf16[1280,1280]{1,0:T(8,128)(2,1)S(1)} %fusion.chosen_ref, f32[8,1280]{1,0:T(8,128)S(1)} %copy-done.3, bf16[128,128]{1,0:T(8,128)(2,1)S(1)} %copy-done.4, bf16[384,384]{1,0:T(8,128)(2,1)S(1)} %copy-done.2, bf16[32,40,128]{2,1,0:T(8,128)(2,1)} %all-to-all-done.2.coef_ref, ...), custom_call_target="tpu_custom_call" | custom-call | tf_op jit(solution)/shard_map/synthesize/pallas_call | solution.py:233
  109.8 0.9 copy-done.1
  110.6 3.6 %all-to-all-start.3 = ((bf16[16,64,384]{2,1,0:T(8,128)(2,1)}), bf16[16,64,384]{2,1,0:T(8,128)(2,1)S(1)}, u32[]{:S(2)}, u32[]{:S(2)}) async-start(bf16[16,64,384]{2,1,0:T(8,128)(2,1)} %copy-done.1), calls=%async_computation.3 | async-start | bytes 1572864 | tf_op jit(solution)/shard_map/all_to_all | solution.py:311
  114.4 12.5 %all-to-all-done.3.grid_ref = bf16[16,64,384]{2,1,0:T(8,128)(2,1)S(1)} async-done(((bf16[16,64,384]{2,1,0:T(8,128)(2,1)}), bf16[16,64,384]{2,1,0:T(8,128)(2,1)S(1)}, u32[]{:S(2)}, u32[]{:S(2)}) %all-to-all-start.3) | async-done | bytes 786464 | tf_op jit(solution)/shard_map/all_to_all | solution.py:311
  127.0 3.4 %collective-permute-start = (bf16[64,384]{1,0:T(8,128)(2,1)S(1)}, bf16[64,384]{1,0:T(8,128)(2,1)S(1)}, u32[]{:S(2)}, u32[]{:S(2)}) collective-permute-start(bf16[64,384]{1,0:T(8,128)(2,1)S(1)} %get-tuple-element.6), channel_id=1, source_target_pairs={{0,16},{16,32},{32,48},{48,64},{64,80},{80,96},{96,112},{112,128},... | collective-permute-start | bytes 147464 | tf_op jit(solution)/shard_map/ppermute | solution.py:313
  130.4 2.4 %collective-permute-start.1 = (bf16[64,384]{1,0:T(8,128)(2,1)S(1)}, bf16[64,384]{1,0:T(8,128)(2,1)S(1)}, u32[]{:S(2)}, u32[]{:S(2)}) collective-permute-start(bf16[64,384]{1,0:T(8,128)(2,1)S(1)} %get-tuple-element.5), channel_id=1, source_target_pairs={{16,0},{32,16},{48,32},{64,48},{80,64},{96,80},{112,96},{128,112},... | collective-permute-start | bytes 147464 | tf_op jit(solution)/shard_map/ppermute | solution.py:314
  132.9 3.6 %depart_inner.1.inner_ref = bf16[16,64,320]{2,1,0:T(8,128)(2,1)} custom-call(f32[16,3,384]{2,1,0:T(4,128)S(1)} %select_maximum_fusion.target_ref, bf16[16,64,384]{2,1,0:T(8,128)(2,1)S(1)} %all-to-all-done.3.grid_ref), custom_call_target="tpu_custom_call" | custom-call | flops 440401920 | bytes 4000000 | tf_op jit(solution)/shard_map/depart_inner/pallas_call | solution.py:260
  136.6 1.4 depart_edges.1
  (29 shorter events, 0.4 us)
Async XLA Ops:
  4.0 7.8 %copy-start.7 = (s32[640]{0:T(1024)S(1)}, s32[640]{0:T(1024)}, u32[]{:S(2)}) copy-start(s32[640]{0:T(1024)} %param.11) | copy-start | bytes 7684
  4.0 35.1 %all-to-all-start = ((bf16[16,71,8,128]{3,2,1,0:T(8,128)(2,1)}), bf16[16,71,8,128]{3,2,1,0:T(8,128)(2,1)S(1)}, u32[]{:S(2)}, u32[]{:S(2)}) async-start(bf16[16,71,8,128]{3,2,1,0:T(8,128)(2,1)} %pack.1), calls=%async_computation | async-start | bytes 4653056 | tf_op jit(solution)/shard_map/all_to_all | solution.py:305
  41.2 14.9 %all-to-all-start.1 = ((bf16[16,40,256]{2,1,0:T(8,128)(2,1)}), bf16[16,40,256]{2,1,0:T(8,128)(2,1)S(1)}, u32[]{:S(2)}, u32[]{:S(2)}) async-start(bf16[16,40,256]{2,1,0:T(8,128)(2,1)} %legendre_sums.1), calls=%async_computation.1 | async-start | bytes 655360 | tf_op jit(solution)/shard_map/all_to_all | solution.py:306
  48.4 53.3 %copy-start.3 = (f32[8,1280]{1,0:T(8,128)S(1)}, f32[8,1280]{1,0:T(8,128)}, u32[]{:S(2)}) copy-start(f32[8,1280]{1,0:T(8,128)} %constant.63.clone.turns_ref) | copy-start | bytes 122884
  48.4 53.3 %copy-start.4 = (bf16[128,128]{1,0:T(8,128)(2,1)S(1)}, bf16[128,128]{1,0:T(8,128)(2,1)}, u32[]{:S(2)}) copy-start(bf16[128,128]{1,0:T(8,128)(2,1)} %constant.64.clone.fields_ref) | copy-start | bytes 98308
  57.1 44.6 %all-to-all-start.2 = ((bf16[32,40,128]{2,1,0:T(8,128)(2,1)}), bf16[32,40,128]{2,1,0:T(8,128)(2,1)}, u32[]{:S(2)}, u32[]{:S(2)}) async-start(bf16[32,40,128]{2,1,0:T(8,128)(2,1)} %copy.19), calls=%async_computation.2 | async-start | bytes 655360 | tf_op jit(solution)/shard_map/all_to_all | solution.py:309
  101.7 2.1 %copy-start = (bf16[2,1280,768]{2,1,0:T(8,128)(2,1)S(1)}, bf16[2,1280,768]{2,1,0:T(8,128)(2,1)}, u32[]{:S(2)}) copy-start(bf16[2,1280,768]{2,1,0:T(8,128)(2,1)} %constant.66.clone.table_ref) | copy-start | bytes 11796484
  103.8 1.0 copy-start.2
  104.8 9.5 %copy-start.5 = (s32[16,320]{1,0:T(8,128)S(1)}, s32[16,320]{1,0:T(8,128)}, u32[]{:S(2)}) copy-start(s32[16,320]{1,0:T(8,128)} %param.12) | copy-start | bytes 61444
  104.8 9.5 %copy-start.6 = (s32[16,320]{1,0:T(8,128)S(1)}, s32[16,320]{1,0:T(8,128)}, u32[]{:S(2)}) copy-start(s32[16,320]{1,0:T(8,128)} %param.13) | copy-start | bytes 61444
  109.7 0.9 copy-start.1
  110.6 16.3 %all-to-all-start.3 = ((bf16[16,64,384]{2,1,0:T(8,128)(2,1)}), bf16[16,64,384]{2,1,0:T(8,128)(2,1)S(1)}, u32[]{:S(2)}, u32[]{:S(2)}) async-start(bf16[16,64,384]{2,1,0:T(8,128)(2,1)} %copy-done.1), calls=%async_computation.3 | async-start | bytes 1572864 | tf_op jit(solution)/shard_map/all_to_all | solution.py:311
  127.0 9.6 %collective-permute-start = (bf16[64,384]{1,0:T(8,128)(2,1)S(1)}, bf16[64,384]{1,0:T(8,128)(2,1)S(1)}, u32[]{:S(2)}, u32[]{:S(2)}) collective-permute-start(bf16[64,384]{1,0:T(8,128)(2,1)S(1)} %get-tuple-element.6), channel_id=1, source_target_pairs={{0,16},{16,32},{32,48},{48,64},{64,80},{80,96},{96,112},{112,128},... | collective-permute-start | bytes 147464 | tf_op jit(solution)/shard_map/ppermute | solution.py:313
  130.4 6.1 %collective-permute-start.1 = (bf16[64,384]{1,0:T(8,128)(2,1)S(1)}, bf16[64,384]{1,0:T(8,128)(2,1)S(1)}, u32[]{:S(2)}, u32[]{:S(2)}) collective-permute-start(bf16[64,384]{1,0:T(8,128)(2,1)S(1)} %get-tuple-element.5), channel_id=1, source_target_pairs={{16,0},{32,16},{48,32},{64,48},{80,64},{96,80},{112,96},{128,112},... | collective-permute-start | bytes 147464 | tf_op jit(solution)/shard_map/ppermute | solution.py:314

commit v3 on v2

--- a/solution.py
+++ b/solution.py
@@ -50,44 +50,41 @@
     return table.astype(np.float32).astype(BF16)
 
 
-def mirror():
-    x = np.arange(WINDOW)
-    return (x[:, None] + x[None, :] == WINDOW).astype(np.float32).astype(BF16)
-
-
-def quarter_turns():
-    turns = wave_order()[None, :] * np.arange(4)[:, None] % 4
-    real = np.array([1, 0, -1, 0])[turns]
-    imag = np.array([0, 1, 0, -1])[turns]
-    return np.concatenate([real, imag], axis=0).astype(np.float32)
-
-
-def field_order():
-    c, b, f4 = np.meshgrid(np.arange(2), np.arange(N_BA), np.arange(4), indexing="ij")
-    lanes = (b * 8 + c * 4 + f4).reshape(-1)
-    return (lanes[:, None] == np.arange(128)[None, :]).astype(np.float32).astype(BF16)
-
-
-def pack_kernel(main_ref, shared_ref, main_values_ref, shared_values_ref, out_ref):
+def pack_kernel(rows_ref, values_ref, out_ref, rows_held, values_held, out_held, sems):
+    into = [pltpu.make_async_copy(values_ref, values_held, sems.at[PAIRS])]
+    for pair in [i for q in range(4) for i in (N_BA + q, 4 * q, 4 * q + 1, 4 * q + 2, 4 * q + 3)]:
+        into.append(pltpu.make_async_copy(rows_ref.at[pair], rows_held.at[pair], sems.at[pair]))
+    for copy in into:
+        copy.start()
+    into[0].wait()
+    out = []
     lane = lax.broadcasted_iota(jnp.int32, (8, 128), 1)
-    for h in range(4):
+    for d in range(N_BA):
+        q, h = d // 4, d % 4
+        if h == 0:
+            into[1 + 5 * q].wait()
+        into[2 + 5 * q + h].wait()
         last = jnp.zeros((8, 128), F32)
         for g in range(7):
             for k in range(KTILES + 1):
                 here = slice(128 * k, min(128 * k + 128, KPACK))
                 if g < 4:
-                    tile = main_ref[h, 8 * g : 8 * g + 8, here]
+                    tile = rows_held[d, 8 * g : 8 * g + 8, here]
                 elif g == 4:
-                    tile = shared_ref[0, 8 * h : 8 * h + 8, here]
+                    tile = rows_held[N_BA + q, 8 * h : 8 * h + 8, here]
                 else:
-                    ref, at = ((main_values_ref, h), (shared_values_ref, 0))[g - 5]
-                    tile = ref[at, :, :, here].reshape(8, here.stop - here.start)
+                    pair = (d, N_BA + q)[g - 5]
+                    tile = values_held[pair, :, :, here].reshape(8, here.stop - here.start)
                 if k < KTILES:
-                    out_ref[h, 7 * k + g] = tile
+                    out_held[d, 7 * k + g] = tile
                 else:
                     column = jnp.broadcast_to(tile.astype(F32), (8, 128))
                     last = jnp.where(lane == g, column, last)
-        out_ref[h, TILES - 1] = last.astype(BF16)
+        out_held[d, TILES - 1] = last.astype(BF16)
+        out.append(pltpu.make_async_copy(out_held.at[d], out_ref.at[d], sems.at[PAIRS + 1 + d]))
+        out[-1].start()
+    for copy in out:
+        copy.wait()
 
 
 def legendre_kernel(pairs_ref, rows_ref, out_ref):
@@ -119,20 +116,38 @@
         out_ref[:, 8 * first : 8 * (first + count), :] = out.reshape(N_BA, 8 * count, 256)
 
 
+def iota(shape, dim):
+    return lax.broadcasted_iota(jnp.int32, shape, dim)
+
+
+def ones_where(chosen):
+    return chosen.astype(F32).astype(BF16)
+
+
 def synthesis_kernel(
-    chosen_ref, turns_ref, fields_ref, mirror_ref, coef_ref, table_ref, out_ref, left_ref, held_ref, sems
+    places_ref, coef_ref, table_ref, out_ref, rows_ref, left_ref, held_ref, blocks_ref, sems
 ):
+    arriving = pltpu.make_async_copy(coef_ref, rows_ref, sems.at[2 + N_BA])
+    arriving.start()
     copies = [
         pltpu.make_async_copy(table_ref.at[c], held_ref.at[c], sems.at[c]) for c in range(2)
     ]
     for copy in copies:
         copy.start()
-    rows = coef_ref[...].reshape(WAVES, 128)
-    turned = lax.dot_general(fields_ref[...], rows, NT, preferred_element_type=F32).astype(BF16)
-    ordered = lax.dot_general(turned, chosen_ref[...], NT, preferred_element_type=F32)
+    row, lane = iota((128, 128), 0), iota((128, 128), 1)
+    fields = ones_where(lane == (row % FL) // 4 * 8 + row // FL * 4 + row % 4)
+    chosen = ones_where(iota((WAVES, WAVES), 0) == places_ref[...])
+    arriving.wait()
+    rows = rows_ref[...].reshape(WAVES, 128)
+    turned = lax.dot_general(fields, rows, NT, preferred_element_type=F32).astype(BF16)
+    ordered = lax.dot_general(turned, chosen, NT, preferred_element_type=F32)
     real, imag = ordered[:FL], ordered[FL:]
+    place = iota((1, WAVES), 1)
+    wave = jnp.where(place < WAVES // 2, place, WAVES + WAVES // 2 - 1 - place)
     for q in range(4):
-        alpha, beta = turns_ref[q : q + 1, :], turns_ref[4 + q : 5 + q, :]
+        turn = wave * q % 4
+        alpha = (turn == 0).astype(F32) - (turn == 2).astype(F32)
+        beta = (turn == 1).astype(F32) - (turn == 3).astype(F32)
         here = pl.ds(q * FL, FL)
         left_ref[0, here, :] = (real * alpha - imag * beta).astype(BF16)
         left_ref[1, here, :] = (imag * alpha + real * beta).astype(BF16)
@@ -141,13 +156,23 @@
     copies[1].wait()
     odd = jnp.dot(left_ref[1], held_ref[1], preferred_element_type=F32)
     ahead, behind = (even + odd).astype(BF16), (even - odd).astype(BF16)
+    mirror = ones_where(iota((WINDOW, WINDOW), 0) + iota((WINDOW, WINDOW), 1) == WINDOW)
+    sent = []
+
+    def finish(block, value):
+        blocks_ref[block] = value
+        sent.append(pltpu.make_async_copy(blocks_ref.at[block], out_ref.at[block], sems.at[2 + block]))
+        sent[-1].start()
+
     for w in range(2):
         lanes = slice(w * WINDOW, (w + 1) * WINDOW)
-        back = jnp.dot(behind[:, lanes], mirror_ref[...], preferred_element_type=F32).astype(BF16)
+        back = jnp.dot(behind[:, lanes], mirror, preferred_element_type=F32).astype(BF16)
         for q in range(4):
             here = slice(q * FL, (q + 1) * FL)
-            out_ref[4 * q + w] = ahead[here, lanes]
-            out_ref[(4 * q + N_BA - 1 - w) % N_BA] = back[here]
+            finish(4 * q + w, ahead[here, lanes])
+            finish((4 * q + N_BA - 1 - w) % N_BA, back[here])
+    for copy in sent:
+        copy.wait()
 
 
 def band(target, first, count):
@@ -202,20 +227,21 @@
 def pack(legendre, spectral):
     rows = legendre.reshape(PAIRS, N_AA, KPACK)
     values = spectral.transpose(0, 2, 3, 1)
+    anywhere = pl.BlockSpec(memory_space=pl.ANY)
     return pl.pallas_call(
         pack_kernel,
-        grid=(4,),
         out_shape=jax.ShapeDtypeStruct((N_BA, TILES, 8, 128), BF16),
-        in_specs=[
-            pl.BlockSpec((4, N_AA, KPACK), lambda q: (q, 0, 0)),
-            pl.BlockSpec((1, N_AA, KPACK), lambda q: (N_BA + q, 0, 0)),
-            pl.BlockSpec((4, 2, 4, KPACK), lambda q: (q, 0, 0, 0)),
-            pl.BlockSpec((1, 2, 4, KPACK), lambda q: (N_BA + q, 0, 0, 0)),
+        in_specs=[anywhere, anywhere],
+        out_specs=anywhere,
+        scratch_shapes=[
+            pltpu.VMEM((PAIRS, N_AA, KPACK), BF16),
+            pltpu.VMEM((PAIRS, 2, 4, KPACK), BF16),
+            pltpu.VMEM((N_BA, TILES, 8, 128), BF16),
+            pltpu.SemaphoreType.DMA((PAIRS + 1 + N_BA,)),
         ],
-        out_specs=pl.BlockSpec((4, TILES, 8, 128), lambda q: (q, 0, 0, 0)),
-        compiler_params=params(58),
+        compiler_params=params(59),
         name="pack",
-    )(rows, rows, values, values)
+    )(rows, values)
 
 
 def legendre_sums(pairs, rows):
@@ -229,27 +255,23 @@
     )(pairs, rows)
 
 
-def synthesize(chosen, coefficients):
+def synthesize(places, coefficients):
+    anywhere = pl.BlockSpec(memory_space=pl.ANY)
     return pl.pallas_call(
         synthesis_kernel,
         out_shape=jax.ShapeDtypeStruct((N_BA, FL, WINDOW), BF16),
-        in_specs=whole(5) + [pl.BlockSpec(memory_space=pl.ANY)],
-        out_specs=whole(1)[0],
+        in_specs=whole(1) + [anywhere] * 2,
+        out_specs=anywhere,
         scratch_shapes=[
+            pltpu.VMEM((N_AA, 40, 128), BF16),
             pltpu.VMEM((2, 4 * FL, WAVES), BF16),
             pltpu.VMEM((2, WAVES, 2 * WINDOW), BF16),
-            pltpu.SemaphoreType.DMA((2,)),
+            pltpu.VMEM((N_BA, FL, WINDOW), BF16),
+            pltpu.SemaphoreType.DMA((3 + N_BA,)),
         ],
-        compiler_params=params(32),
+        compiler_params=params(59),
         name="synthesize",
-    )(
-        chosen,
-        jnp.asarray(quarter_turns()),
-        jnp.asarray(field_order()),
-        jnp.asarray(mirror()),
-        coefficients,
-        jnp.asarray(window_table()),
-    )
+    )(places, coefficients, jnp.asarray(window_table()))
 
 
 def band_scratch():
@@ -294,8 +316,7 @@
 
 def wave_places(slot_pairs):
     places = slot_pairs.reshape(N_AA, 1, PAIRS) + (jnp.arange(2) * (WAVES // 2))[None, :, None]
-    places = places.reshape(1, WAVES).astype(jnp.int32)
-    return (jnp.arange(WAVES, dtype=jnp.int32)[:, None] == places).astype(BF16)
+    return places.reshape(1, WAVES).astype(jnp.int32)
 
 
 def local(legendre, spectral, slot_pairs, lat_shift, lon_shift):

time: 139 us -> 134 us (0.964)
  blocking collectives: 0 us -> 14.7 us
  starting transfers between devices: 43.9 us -> 36.6 us
  waiting for transfers between devices: 68.9 us -> 62.1 us
  local copies, waits for them, and re-layouts: 5.85 us -> 3.17 us
  other arithmetic: 3 us -> 1.56 us
    all_to_all x0 -> x1, blocking collectives: none -> 14.7 us  [local(): sums = lax.all_to_all(legendre_sums(pairs, rows), 'ba', 0, 0, tiled=True)]
    all_to_all x1 -> x0, waiting for transfers between devices: 7.56 us -> none  [local(): sums = lax.all_to_all(legendre_sums(pairs, rows), 'ba', 0, 0, tiled=True)]
    all_to_all x1 -> x0, starting transfers between devices: 7.23 us -> none  [local(): sums = lax.all_to_all(legendre_sums(pairs, rows), 'ba', 0, 0, tiled=True)]
    unnamed x16 -> x8, local copies, waits for them, and re-layouts: 3.97 us -> 0.74 us
    convert_element_type x1 -> x0, other arithmetic: 1.4 us -> none  [wave_places(): return (jnp.arange(WAVES, dtype=jnp.int32)[:, None] == places).astype(BF16)]
  transfers between devices with their start and end apart: 6 -> 5, of which waited for: 4 -> 3; matrix products, arithmetic and copies ran while one was open for 3% -> 2% of each run, Pallas kernels for 3% -> 3%
where the time goes in v3:
time: 134 us
  waiting for transfers between devices  62.1 us (46%)
  starting transfers between devices  36.6 us (27%)
  Pallas kernels  15.5 us (12%)
  blocking collectives  14.7 us (11%)
  local copies, waits for them, and re-layouts  3.17 us (2%)
  other arithmetic  1.56 us (1%)
    all_to_all x1, waiting for transfers between devices, local(): rows = lax.all_to_all(pack(legendre, spectral), 'ba', 0, 0, tiled=True)  25.4 us
    all_to_all x1, waiting for transfers between devices, local(): coefficients = lax.all_to_all(by_row, 'aa', 0, 0, tiled=True)  24.1 us
    all_to_all x1, starting transfers between devices, local(): coefficients = lax.all_to_all(by_row, 'aa', 0, 0, tiled=True)  19.5 us
    all_to_all x1, blocking collectives, local(): sums = lax.all_to_all(legendre_sums(pairs, rows), 'ba', 0, 0, tiled=True)  14.7 us
    all_to_all x1, waiting for transfers between devices, local(): grid = lax.all_to_all(blocks, 'ba', 0, 0, tiled=True)  12.5 us
    all_to_all x1, starting transfers between devices, local(): rows = lax.all_to_all(pack(legendre, spectral), 'ba', 0, 0, tiled=True)  7.6 us
    pallas_call x1, Pallas kernels, synthesize(): pl.pallas_call(synthesis_kernel, out_shape=jax.ShapeDtypeStruct((N_BA, FL...  5.87 us
    pallas_call x1, Pallas kernels, depart_inner(): pl.pallas_call(inner_kernel, out_shape=jax.ShapeDtypeStruct((N_BA, FL, BL...  3.63 us
  transfers between devices with their start and end apart: 5, of which 3 were waited for; matrix products, arithmetic and copies ran while one was open for 2% of the time, Pallas kernels for 3%

profile of v3, /device:TPU:1, one launch (start us, length us, event | category | flops | bytes accessed | tf_op | source)
XLA Modules:
  0.0 133.8 jit_solution(18395563462712296633)
XLA Ops:
  0.0 3.3 %pack.1 = bf16[16,71,8,128]{3,2,1,0:T(8,128)(2,1)} custom-call(bf16[20,32,1281]{2,1,0:T(8,128)(2,1)} %bitcast.18, bf16[20,2,4,1281]{3,2,1,0:T(4,128)(2,1)} %bitcast.20), custom_call_target="tpu_custom_call" | custom-call | tf_op jit(solution)/shard_map/pack/pallas_call | solution.py:231
  3.3 0.0 copy-start.3
  3.4 7.6 %all-to-all-start = ((bf16[16,71,8,128]{3,2,1,0:T(8,128)(2,1)}), bf16[16,71,8,128]{3,2,1,0:T(8,128)(2,1)S(1)}, u32[]{:S(2)}, u32[]{:S(2)}) async-start(bf16[16,71,8,128]{3,2,1,0:T(8,128)(2,1)} %pack.1), calls=%async_computation | async-start | bytes 4653056 | tf_op jit(solution)/shard_map/all_to_all | solution.py:326
  11.0 0.6 fusion.3
  11.6 1.3 %pad_add_fusion.pairs_ref = s32[2]{0:T(128)S(1)} fusion(s32[1]{0:T(128)} %get-tuple-element.11, s32[1]{0:T(128)} %get-tuple-element.10), kind=kLoop, calls=%fused_computation.18 | loop fusion | flops 2 | bytes 16 | tf_op jit(solution)/shard_map/stack | solution.py:325
  12.9 25.4 %all-to-all-done.rows_ref = bf16[16,71,8,128]{3,2,1,0:T(8,128)(2,1)S(1)} async-done(((bf16[16,71,8,128]{3,2,1,0:T(8,128)(2,1)}), bf16[16,71,8,128]{3,2,1,0:T(8,128)(2,1)S(1)}, u32[]{:S(2)}, u32[]{:S(2)}) %all-to-all-start) | async-done | bytes 2326560 | tf_op jit(solution)/shard_map/all_to_all | solution.py:326
  38.3 1.3 legendre_sums.1
  39.7 14.7 %all_to_all.20 = bf16[16,40,256]{2,1,0:T(8,128)(2,1)S(1)} all-to-all(bf16[16,40,256]{2,1,0:T(8,128)(2,1)S(1)} %legendre_sums.1), channel_id=1, replica_groups=mesh['aa'=32,'ba'=16] {'ba'}, dimensions={0} | all-to-all | bytes 655360 | tf_op jit(solution)/shard_map/all_to_all | solution.py:327
  54.5 0.9 copy.16
  55.4 19.5 %all-to-all-start.2 = ((bf16[32,40,128]{2,1,0:T(8,128)(2,1)}), bf16[32,40,128]{2,1,0:T(8,128)(2,1)S(1)}, u32[]{:S(2)}, u32[]{:S(2)}) async-start(bf16[32,40,128]{2,1,0:T(8,128)(2,1)} %copy.16), calls=%async_computation.2 | async-start | bytes 655360 | tf_op jit(solution)/shard_map/all_to_all | solution.py:330
  74.9 0.1 add.72
  75.0 0.1 broadcast_add_fusion
  75.1 0.7 add.76.places_ref
  75.8 24.1 %all-to-all-done.2.coef_ref = bf16[32,40,128]{2,1,0:T(8,128)(2,1)S(1)} async-done(((bf16[32,40,128]{2,1,0:T(8,128)(2,1)}), bf16[32,40,128]{2,1,0:T(8,128)(2,1)S(1)}, u32[]{:S(2)}, u32[]{:S(2)}) %all-to-all-start.2) | async-done | bytes 327712 | tf_op jit(solution)/shard_map/all_to_all | solution.py:330
  99.9 0.7 copy-done
  100.6 5.9 %synthesize.1 = bf16[16,64,384]{2,1,0:T(8,128)(2,1)} custom-call(s32[1,1280]{1,0:T(1,128)} %add.76.places_ref, bf16[32,40,128]{2,1,0:T(8,128)(2,1)} %copy-done, bf16[2,1280,768]{2,1,0:T(8,128)(2,1)} %constant.57.clone.table_ref), custom_call_target="tpu_custom_call" | custom-call | tf_op jit(solution)/shard_map/synthesize/pallas_call | solution.py:260
  106.5 3.6 %all-to-all-start.3 = ((bf16[16,64,384]{2,1,0:T(8,128)(2,1)}), bf16[16,64,384]{2,1,0:T(8,128)(2,1)S(1)}, u32[]{:S(2)}, u32[]{:S(2)}) async-start(bf16[16,64,384]{2,1,0:T(8,128)(2,1)} %synthesize.1), calls=%async_computation.3 | async-start | bytes 1572864 | tf_op jit(solution)/shard_map/all_to_all | solution.py:332
  110.3 12.5 %all-to-all-done.3.grid_ref = bf16[16,64,384]{2,1,0:T(8,128)(2,1)S(1)} async-done(((bf16[16,64,384]{2,1,0:T(8,128)(2,1)}), bf16[16,64,384]{2,1,0:T(8,128)(2,1)S(1)}, u32[]{:S(2)}, u32[]{:S(2)}) %all-to-all-start.3) | async-done | bytes 786464 | tf_op jit(solution)/shard_map/all_to_all | solution.py:332
  122.8 3.5 %collective-permute-start = (bf16[64,384]{1,0:T(8,128)(2,1)S(1)}, bf16[64,384]{1,0:T(8,128)(2,1)S(1)}, u32[]{:S(2)}, u32[]{:S(2)}) collective-permute-start(bf16[64,384]{1,0:T(8,128)(2,1)S(1)} %get-tuple-element.6), channel_id=1, source_target_pairs={{0,16},{16,32},{32,48},{48,64},{64,80},{80,96},{96,112},{112,128},... | collective-permute-start | bytes 147464 | tf_op jit(solution)/shard_map/ppermute | solution.py:334
  126.3 2.4 %collective-permute-start.1 = (bf16[64,384]{1,0:T(8,128)(2,1)S(1)}, bf16[64,384]{1,0:T(8,128)(2,1)S(1)}, u32[]{:S(2)}, u32[]{:S(2)}) collective-permute-start(bf16[64,384]{1,0:T(8,128)(2,1)S(1)} %get-tuple-element.5), channel_id=1, source_target_pairs={{16,0},{32,16},{48,32},{64,48},{80,64},{96,80},{112,96},{128,112},... | collective-permute-start | bytes 147464 | tf_op jit(solution)/shard_map/ppermute | solution.py:335
  128.7 0.1 select_maximum_fusion.target_ref
  128.8 3.6 %depart_inner.1.inner_ref = bf16[16,64,320]{2,1,0:T(8,128)(2,1)} custom-call(f32[16,3,384]{2,1,0:T(4,128)S(1)} %select_maximum_fusion.target_ref, bf16[16,64,384]{2,1,0:T(8,128)(2,1)S(1)} %all-to-all-done.3.grid_ref), custom_call_target="tpu_custom_call" | custom-call | flops 440401920 | bytes 4000000 | tf_op jit(solution)/shard_map/depart_inner/pallas_call | solution.py:282
  132.4 0.0 collective-permute-done.top_ref
  132.4 1.4 %depart_edges.1 = bf16[16,64,320]{2,1,0:T(8,128)(2,1)} custom-call(bf16[16,64,320]{2,1,0:T(8,128)(2,1)} %depart_inner.1.inner_ref, f32[16,3,384]{2,1,0:T(4,128)S(1)} %select_maximum_fusion.target_ref, bf16[64,384]{1,0:T(8,128)(2,1)S(1)} %collective-permute-done.top_ref, ...), custom_call_target="tpu_custom_call", output_to_operand_aliasing={{}: (0, {})} | custom-call | tf_op jit(solution)/shard_map/depart_edges/pallas_call | solution.py:297
  (19 shorter events, 0.2 us)
Async XLA Ops:
  3.3 7.6 %copy-start.3 = (s32[640]{0:T(1024)S(1)}, s32[640]{0:T(1024)}, u32[]{:S(2)}) copy-start(s32[640]{0:T(1024)} %param.8) | copy-start | bytes 7684
  3.4 35.0 %all-to-all-start = ((bf16[16,71,8,128]{3,2,1,0:T(8,128)(2,1)}), bf16[16,71,8,128]{3,2,1,0:T(8,128)(2,1)S(1)}, u32[]{:S(2)}, u32[]{:S(2)}) async-start(bf16[16,71,8,128]{3,2,1,0:T(8,128)(2,1)} %pack.1), calls=%async_computation | async-start | bytes 4653056 | tf_op jit(solution)/shard_map/all_to_all | solution.py:326
  55.4 44.5 %all-to-all-start.2 = ((bf16[32,40,128]{2,1,0:T(8,128)(2,1)}), bf16[32,40,128]{2,1,0:T(8,128)(2,1)S(1)}, u32[]{:S(2)}, u32[]{:S(2)}) async-start(bf16[32,40,128]{2,1,0:T(8,128)(2,1)} %copy.16), calls=%async_computation.2 | async-start | bytes 655360 | tf_op jit(solution)/shard_map/all_to_all | solution.py:330
  75.8 34.4 %copy-start.1 = (s32[16,320]{1,0:T(8,128)S(1)}, s32[16,320]{1,0:T(8,128)}, u32[]{:S(2)}) copy-start(s32[16,320]{1,0:T(8,128)} %param.9) | copy-start | bytes 61444
  75.8 34.4 %copy-start.2 = (s32[16,320]{1,0:T(8,128)S(1)}, s32[16,320]{1,0:T(8,128)}, u32[]{:S(2)}) copy-start(s32[16,320]{1,0:T(8,128)} %param.10) | copy-start | bytes 61444
  99.9 0.7 copy-start
  106.5 16.3 %all-to-all-start.3 = ((bf16[16,64,384]{2,1,0:T(8,128)(2,1)}), bf16[16,64,384]{2,1,0:T(8,128)(2,1)S(1)}, u32[]{:S(2)}, u32[]{:S(2)}) async-start(bf16[16,64,384]{2,1,0:T(8,128)(2,1)} %synthesize.1), calls=%async_computation.3 | async-start | bytes 1572864 | tf_op jit(solution)/shard_map/all_to_all | solution.py:332
  122.8 9.6 %collective-permute-start = (bf16[64,384]{1,0:T(8,128)(2,1)S(1)}, bf16[64,384]{1,0:T(8,128)(2,1)S(1)}, u32[]{:S(2)}, u32[]{:S(2)}) collective-permute-start(bf16[64,384]{1,0:T(8,128)(2,1)S(1)} %get-tuple-element.6), channel_id=1, source_target_pairs={{0,16},{16,32},{32,48},{48,64},{64,80},{80,96},{96,112},{112,128},... | collective-permute-start | bytes 147464 | tf_op jit(solution)/shard_map/ppermute | solution.py:334
  126.3 6.1 %collective-permute-start.1 = (bf16[64,384]{1,0:T(8,128)(2,1)S(1)}, bf16[64,384]{1,0:T(8,128)(2,1)S(1)}, u32[]{:S(2)}, u32[]{:S(2)}) collective-permute-start(bf16[64,384]{1,0:T(8,128)(2,1)S(1)} %get-tuple-element.5), channel_id=1, source_target_pairs={{16,0},{32,16},{48,32},{64,48},{80,64},{96,80},{112,96},{128,112},... | collective-permute-start | bytes 147464 | tf_op jit(solution)/shard_map/ppermute | solution.py:335

commit v4 on v3

--- a/solution.py
+++ b/solution.py
@@ -116,6 +116,14 @@
         out_ref[:, 8 * first : 8 * (first + count), :] = out.reshape(N_BA, 8 * count, 256)
 
 
+def regroup_kernel(perm_ref, sums_ref, out_ref):
+    sums = sums_ref[...].reshape(N_BA * 40, 256)
+    both = jnp.dot(perm_ref[...], sums, preferred_element_type=F32)
+    first = iota((WAVES, 128), 0) // PAIRS % 2 == 0
+    out = jnp.where(first, both[:, :128], both[:, 128:]).astype(BF16)
+    out_ref[...] = out.reshape(N_AA, 40, 128)
+
+
 def iota(shape, dim):
     return lax.broadcasted_iota(jnp.int32, shape, dim)
 
@@ -204,24 +212,18 @@
 def inner_kernel(target_ref, grid_ref, out_ref, *bands):
     clear(bands)
 
-    @pl.loop(1, N_BA - 1, unroll=7)
+    @pl.loop(2, N_BA, unroll=7)
     def _(row):
-        sources = [grid_ref.at[row - 1], grid_ref.at[row], grid_ref.at[row + 1]]
+        above = jnp.where(row == N_BA - 1, 0, row + 1)
+        sources = [grid_ref.at[row - 1], grid_ref.at[row], grid_ref.at[above]]
         depart_row(target_ref, row, sources, bands, out_ref, row)
 
 
-def edge_kernel(inner_ref, target_ref, top_ref, grid_ref, bottom_ref, out_ref, *bands):
+def edge_kernel(inner_ref, target_ref, beside_ref, grid_ref, out_ref, *bands):
     clear(bands)
-
-    @pl.when(pl.program_id(0) == 0)
-    def _():
-        sources = [top_ref, grid_ref.at[0], grid_ref.at[1]]
-        depart_row(target_ref, 0, sources, bands, out_ref, 0)
-
-    @pl.when(pl.program_id(0) == 1)
-    def _():
-        sources = [grid_ref.at[N_BA - 2], grid_ref.at[N_BA - 1], bottom_ref]
-        depart_row(target_ref, N_BA - 1, sources, bands, out_ref, 0)
+    sources = [beside_ref.at[0], beside_ref.at[1], grid_ref.at[1], grid_ref.at[2]]
+    for row in range(2):
+        depart_row(target_ref, row, sources[row : row + 3], bands, out_ref, row)
 
 
 def pack(legendre, spectral):
@@ -253,6 +255,26 @@
         compiler_params=params(24),
         name="legendre_sums",
     )(pairs, rows)
+
+
+def regroup(perm, sums):
+    return pl.pallas_call(
+        regroup_kernel,
+        out_shape=jax.ShapeDtypeStruct((N_AA, 40, 128), BF16),
+        in_specs=whole(2),
+        out_specs=whole(1)[0],
+        compiler_params=params(24),
+        name="regroup",
+    )(perm, sums)
+
+
+def regroup_rows(own):
+    row = jnp.arange(WAVES, dtype=jnp.int32)
+    lat = (row // 40 + (own == 0).astype(jnp.int32)) % N_AA
+    pair = row % PAIRS
+    shared = (4 * (pair - N_BA) + lat // 8) * 40 + 32 + lat % 8
+    source = jnp.where(pair < N_BA, pair * 40 + lat, shared)
+    return (source[:, None] == jnp.arange(N_BA * 40, dtype=jnp.int32)[None, :]).astype(BF16)
 
 
 def synthesize(places, coefficients):
@@ -293,23 +315,26 @@
     )(targets, grid)
 
 
-def depart_edges(inner, targets, top, grid, bottom):
+def depart_edges(inner, targets, beside, grid):
     return pl.pallas_call(
         edge_kernel,
-        grid=(2,),
+        grid=(1,),
         out_shape=jax.ShapeDtypeStruct((N_BA, FL, BLOCK), BF16),
-        in_specs=[pl.BlockSpec(memory_space=pl.ANY)] + whole(4),
-        out_specs=pl.BlockSpec((1, FL, BLOCK), lambda e: (e * (N_BA - 1), 0, 0)),
+        in_specs=[pl.BlockSpec(memory_space=pl.ANY)] + whole(3),
+        out_specs=pl.BlockSpec((2, FL, BLOCK), lambda e: (0, 0, 0)),
         scratch_shapes=band_scratch(),
         input_output_aliases={0: 0},
         compiler_params=params(24),
         name="depart_edges",
-    )(inner, targets, top, grid, bottom)
-
-
-def depart_targets(lat_shift, lon_shift):
+    )(inner, targets, beside, grid)
+
+
+def depart_targets(lat_shift, lon_shift, first_row):
     x = jnp.arange(BLOCK, dtype=jnp.int32) % 128
     centre = (x + lon_shift).astype(F32) + (HALO - 1 + 1.5 - 96)
+    sources = first_row + jnp.arange(N_BA, dtype=jnp.int32)[:, None] + lat_shift
+    inside = jnp.logical_and(sources >= 0, sources < N_AA * N_BA)
+    centre = jnp.where(inside, centre, FAR)
     targets = jnp.stack([jnp.where(lat_shift == s, centre, FAR) for s in (-1, 0, 1)], axis=1)
     return jnp.pad(targets, ((0, 0), (0, 0), (0, WINDOW - BLOCK)), constant_values=FAR)
 
@@ -325,17 +350,15 @@
     pairs = jnp.stack([slot_pairs[first + own], slot_pairs[first + N_BA + own // 4]])
     rows = lax.all_to_all(pack(legendre, spectral), "ba", 0, 0, tiled=True)
     sums = lax.all_to_all(legendre_sums(pairs, rows), "ba", 0, 0, tiled=True)
-    by_pair = jnp.concatenate([sums[:, :N_AA], sums[:, N_AA:].reshape(4, N_AA, 256)], axis=0)
-    by_row = by_pair.reshape(PAIRS, N_AA, 2, 128).transpose(1, 2, 0, 3).reshape(N_AA, 40, 128)
+    by_row = regroup(regroup_rows(own), sums)
     coefficients = lax.all_to_all(by_row, "aa", 0, 0, tiled=True)
     blocks = synthesize(wave_places(slot_pairs), coefficients)
     grid = lax.all_to_all(blocks, "ba", 0, 0, tiled=True)
-    ends = N_AA - 1
-    top = lax.ppermute(grid[N_BA - 1], "aa", [(i, i + 1) for i in range(ends)])
-    bottom = lax.ppermute(grid[0], "aa", [(i + 1, i) for i in range(ends)])
-    targets = depart_targets(lat_shift, lon_shift)
+    ends = jnp.stack([grid[N_BA - 1], grid[0]])
+    beside = lax.ppermute(ends, "aa", [(i, (i + 1) % N_AA) for i in range(N_AA)])
+    targets = depart_targets(lat_shift, lon_shift, lax.axis_index("aa") * N_BA)
     inner = depart_inner(targets, grid)
-    return depart_edges(inner, targets, top, grid, bottom)
+    return depart_edges(inner, targets, beside, grid)
 
 
 def solution(mesh):

time: 134 us -> 131 us (0.978)
  blocking collectives: 14.7 us -> 0 us
  waiting for transfers between devices: 62.1 us -> 69.4 us
  starting transfers between devices: 36.6 us -> 39.5 us
  Pallas kernels: 15.5 us -> 17.5 us
    all_to_all x1 -> x0, blocking collectives: 14.7 us -> none  [local(): sums = lax.all_to_all(legendre_sums(pairs, rows), 'ba', 0, 0, tiled=True)]
    all_to_all x0 -> x1, waiting for transfers between devices: none -> 7.35 us  [local(): sums = lax.all_to_all(legendre_sums(pairs, rows), 'ba', 0, 0, tiled=True)]
    all_to_all x0 -> x1, starting transfers between devices: none -> 7.23 us  [local(): sums = lax.all_to_all(legendre_sums(pairs, rows), 'ba', 0, 0, tiled=True)]
    ppermute x2 -> x1, starting transfers between devices: 5.86 us -> 1.56 us  [local(): lax.ppermute(ends, 'aa', [(i, (i + 1) % N_AA) for i in range(N_AA)])]
  transfers between devices with their start and end apart: 5 -> 5, of which waited for: 3 -> 4; matrix products, arithmetic and copies ran while one was open for 2% -> 3% of each run, Pallas kernels for 3% -> 3%
where the time goes in v4:
time: 131 us
  waiting for transfers between devices  69.4 us (53%)
  starting transfers between devices  39.5 us (30%)
  Pallas kernels  17.5 us (13%)
  local copies, waits for them, and re-layouts  2.21 us (2%)
  other arithmetic  1.93 us (1%)
    all_to_all x1, waiting for transfers between devices, local(): rows = lax.all_to_all(pack(legendre, spectral), 'ba', 0, 0, tiled=True)  25.4 us
    all_to_all x1, waiting for transfers between devices, local(): coefficients = lax.all_to_all(by_row, 'aa', 0, 0, tiled=True)  24.1 us
    all_to_all x1, starting transfers between devices, local(): coefficients = lax.all_to_all(by_row, 'aa', 0, 0, tiled=True)  19.5 us
    all_to_all x1, waiting for transfers between devices, local(): grid = lax.all_to_all(blocks, 'ba', 0, 0, tiled=True)  12.5 us
    all_to_all x1, starting transfers between devices, local(): rows = lax.all_to_all(pack(legendre, spectral), 'ba', 0, 0, tiled=True)  7.6 us
    all_to_all x1, waiting for transfers between devices, local(): sums = lax.all_to_all(legendre_sums(pairs, rows), 'ba', 0, 0, tiled=True)  7.35 us
    all_to_all x1, starting transfers between devices, local(): sums = lax.all_to_all(legendre_sums(pairs, rows), 'ba', 0, 0, tiled=True)  7.23 us
    pallas_call x1, Pallas kernels, synthesize(): pl.pallas_call(synthesis_kernel, out_shape=jax.ShapeDtypeStruct((N_BA, FL...  5.88 us
  transfers between devices with their start and end apart: 5, of which 4 were waited for; matrix products, arithmetic and copies ran while one was open for 3% of the time, Pallas kernels for 3%

profile of v4, /device:TPU:1, one launch (start us, length us, event | category | flops | bytes accessed | tf_op | source)
XLA Modules:
  0.0 130.7 jit_solution(2990870024897508155)
XLA Ops:
  0.0 3.3 %pack.1 = bf16[16,71,8,128]{3,2,1,0:T(8,128)(2,1)} custom-call(bf16[20,32,1281]{2,1,0:T(8,128)(2,1)} %bitcast.6, bf16[20,2,4,1281]{3,2,1,0:T(4,128)(2,1)} %bitcast.7), custom_call_target="tpu_custom_call" | custom-call | tf_op jit(solution)/shard_map/pack/pallas_call | solution.py:233
  3.3 7.6 %all-to-all-start = ((bf16[16,71,8,128]{3,2,1,0:T(8,128)(2,1)}), bf16[16,71,8,128]{3,2,1,0:T(8,128)(2,1)S(1)}, u32[]{:S(2)}, u32[]{:S(2)}) async-start(bf16[16,71,8,128]{3,2,1,0:T(8,128)(2,1)} %pack.1), calls=%async_computation | async-start | bytes 4653056 | tf_op jit(solution)/shard_map/all_to_all | solution.py:351
  11.0 0.6 fusion.23
  11.6 1.3 pad_add_fusion.pairs_ref
  12.9 25.4 %all-to-all-done.rows_ref = bf16[16,71,8,128]{3,2,1,0:T(8,128)(2,1)S(1)} async-done(((bf16[16,71,8,128]{3,2,1,0:T(8,128)(2,1)}), bf16[16,71,8,128]{3,2,1,0:T(8,128)(2,1)S(1)}, u32[]{:S(2)}, u32[]{:S(2)}) %all-to-all-start) | async-done | bytes 2326560 | tf_op jit(solution)/shard_map/all_to_all | solution.py:351
  38.3 2.1 %legendre_sums.1 = bf16[16,40,256]{2,1,0:T(8,128)(2,1)} custom-call(s32[2]{0:T(128)S(1)} %pad_add_fusion.pairs_ref, bf16[16,71,8,128]{3,2,1,0:T(8,128)(2,1)S(1)} %all-to-all-done.rows_ref), custom_call_target="tpu_custom_call" | custom-call | tf_op jit(solution)/shard_map/legendre_sums/pallas_call | solution.py:250
  40.4 7.2 %all-to-all-start.1 = ((bf16[16,40,256]{2,1,0:T(8,128)(2,1)}), bf16[16,40,256]{2,1,0:T(8,128)(2,1)S(1)}, u32[]{:S(2)}, u32[]{:S(2)}) async-start(bf16[16,40,256]{2,1,0:T(8,128)(2,1)} %legendre_sums.1), calls=%async_computation.1 | async-start | bytes 655360 | tf_op jit(solution)/shard_map/all_to_all | solution.py:352
  47.6 0.3 fusion.perm_ref
  48.0 7.3 %all-to-all-done.1.sums_ref = bf16[16,40,256]{2,1,0:T(8,128)(2,1)S(1)} async-done(((bf16[16,40,256]{2,1,0:T(8,128)(2,1)}), bf16[16,40,256]{2,1,0:T(8,128)(2,1)S(1)}, u32[]{:S(2)}, u32[]{:S(2)}) %all-to-all-start.1) | async-done | bytes 327712 | tf_op jit(solution)/shard_map/all_to_all | solution.py:352
  55.3 1.4 %regroup.1 = bf16[32,40,128]{2,1,0:T(8,128)(2,1)} custom-call(bf16[1280,640]{1,0:T(8,128)(2,1)S(1)} %fusion.perm_ref, bf16[16,40,256]{2,1,0:T(8,128)(2,1)S(1)} %all-to-all-done.1.sums_ref), custom_call_target="tpu_custom_call" | custom-call | tf_op jit(solution)/shard_map/regroup/pallas_call | solution.py:261
  56.8 19.5 %all-to-all-start.2 = ((bf16[32,40,128]{2,1,0:T(8,128)(2,1)}), bf16[32,40,128]{2,1,0:T(8,128)(2,1)S(1)}, u32[]{:S(2)}, u32[]{:S(2)}) async-start(bf16[32,40,128]{2,1,0:T(8,128)(2,1)} %regroup.1), calls=%async_computation.2 | async-start | bytes 655360 | tf_op jit(solution)/shard_map/all_to_all | solution.py:354
  76.2 0.1 add.179
  76.3 0.1 broadcast_add_fusion
  76.4 0.7 add.183.places_ref
  77.2 24.1 %all-to-all-done.2.coef_ref = bf16[32,40,128]{2,1,0:T(8,128)(2,1)S(1)} async-done(((bf16[32,40,128]{2,1,0:T(8,128)(2,1)}), bf16[32,40,128]{2,1,0:T(8,128)(2,1)S(1)}, u32[]{:S(2)}, u32[]{:S(2)}) %all-to-all-start.2) | async-done | bytes 327712 | tf_op jit(solution)/shard_map/all_to_all | solution.py:354
  101.3 0.7 copy-done
  102.0 5.9 %synthesize.1 = bf16[16,64,384]{2,1,0:T(8,128)(2,1)} custom-call(s32[1,1280]{1,0:T(1,128)} %add.183.places_ref, bf16[32,40,128]{2,1,0:T(8,128)(2,1)} %copy-done, bf16[2,1280,768]{2,1,0:T(8,128)(2,1)} %constant.113.clone.table_ref), custom_call_target="tpu_custom_call" | custom-call | tf_op jit(solution)/shard_map/synthesize/pallas_call | solution.py:282
  107.9 3.6 %all-to-all-start.3 = ((bf16[16,64,384]{2,1,0:T(8,128)(2,1)}), bf16[16,64,384]{2,1,0:T(8,128)(2,1)S(1)}, u32[]{:S(2)}, u32[]{:S(2)}) async-start(bf16[16,64,384]{2,1,0:T(8,128)(2,1)} %synthesize.1), calls=%async_computation.3 | async-start | bytes 1572864 | tf_op jit(solution)/shard_map/all_to_all | solution.py:356
  111.6 0.1 select_bitcast_fusion.1
  111.7 12.5 %all-to-all-done.3.grid_ref = bf16[16,64,384]{2,1,0:T(8,128)(2,1)S(1)} async-done(((bf16[16,64,384]{2,1,0:T(8,128)(2,1)}), bf16[16,64,384]{2,1,0:T(8,128)(2,1)S(1)}, u32[]{:S(2)}, u32[]{:S(2)}) %all-to-all-start.3) | async-done | bytes 786464 | tf_op jit(solution)/shard_map/all_to_all | solution.py:356
  124.2 1.6 %collective-permute-start = (bf16[2,64,384]{2,1,0:T(8,128)(2,1)S(1)}, bf16[2,64,384]{2,1,0:T(8,128)(2,1)S(1)}, u32[]{:S(2)}, u32[]{:S(2)}) collective-permute-start(bf16[2,64,384]{2,1,0:T(8,128)(2,1)S(1)} %pad_maximum_fusion), channel_id=1, source_target_pairs={{0,16},{16,32},{32,48},{48,64},{64,80},{80,96},{96,112},{112,128},... | collective-permute-start | bytes 294920 | tf_op jit(solution)/shard_map/ppermute | solution.py:358
  125.8 0.1 select_maximum_fusion.target_ref
  125.9 3.6 %depart_inner.1.inner_ref = bf16[16,64,320]{2,1,0:T(8,128)(2,1)} custom-call(f32[16,3,384]{2,1,0:T(4,128)S(1)} %select_maximum_fusion.target_ref, bf16[16,64,384]{2,1,0:T(8,128)(2,1)S(1)} %all-to-all-done.3.grid_ref), custom_call_target="tpu_custom_call" | custom-call | flops 440401920 | bytes 4000000 | tf_op jit(solution)/shard_map/depart_inner/pallas_call | solution.py:304
  129.5 1.2 depart_edges.1
  (17 shorter events, 0.2 us)
Async XLA Ops:
  3.3 7.6 %copy-start.3 = (s32[640]{0:T(1024)S(1)}, s32[640]{0:T(1024)}, u32[]{:S(2)}) copy-start(s32[640]{0:T(1024)} %param.8) | copy-start | bytes 7684
  3.3 35.0 %all-to-all-start = ((bf16[16,71,8,128]{3,2,1,0:T(8,128)(2,1)}), bf16[16,71,8,128]{3,2,1,0:T(8,128)(2,1)S(1)}, u32[]{:S(2)}, u32[]{:S(2)}) async-start(bf16[16,71,8,128]{3,2,1,0:T(8,128)(2,1)} %pack.1), calls=%async_computation | async-start | bytes 4653056 | tf_op jit(solution)/shard_map/all_to_all | solution.py:351
  40.4 14.9 %all-to-all-start.1 = ((bf16[16,40,256]{2,1,0:T(8,128)(2,1)}), bf16[16,40,256]{2,1,0:T(8,128)(2,1)S(1)}, u32[]{:S(2)}, u32[]{:S(2)}) async-start(bf16[16,40,256]{2,1,0:T(8,128)(2,1)} %legendre_sums.1), calls=%async_computation.1 | async-start | bytes 655360 | tf_op jit(solution)/shard_map/all_to_all | solution.py:352
  56.8 44.5 %all-to-all-start.2 = ((bf16[32,40,128]{2,1,0:T(8,128)(2,1)}), bf16[32,40,128]{2,1,0:T(8,128)(2,1)S(1)}, u32[]{:S(2)}, u32[]{:S(2)}) async-start(bf16[32,40,128]{2,1,0:T(8,128)(2,1)} %regroup.1), calls=%async_computation.2 | async-start | bytes 655360 | tf_op jit(solution)/shard_map/all_to_all | solution.py:354
  77.1 34.4 %copy-start.1 = (s32[16,320]{1,0:T(8,128)S(1)}, s32[16,320]{1,0:T(8,128)}, u32[]{:S(2)}) copy-start(s32[16,320]{1,0:T(8,128)} %param.9) | copy-start | bytes 61444
  77.2 34.4 %copy-start.2 = (s32[16,320]{1,0:T(8,128)S(1)}, s32[16,320]{1,0:T(8,128)}, u32[]{:S(2)}) copy-start(s32[16,320]{1,0:T(8,128)} %param.10) | copy-start | bytes 61444
  101.3 0.7 copy-start
  107.9 16.3 %all-to-all-start.3 = ((bf16[16,64,384]{2,1,0:T(8,128)(2,1)}), bf16[16,64,384]{2,1,0:T(8,128)(2,1)S(1)}, u32[]{:S(2)}, u32[]{:S(2)}) async-start(bf16[16,64,384]{2,1,0:T(8,128)(2,1)} %synthesize.1), calls=%async_computation.3 | async-start | bytes 1572864 | tf_op jit(solution)/shard_map/all_to_all | solution.py:356
  124.2 5.2 %collective-permute-start = (bf16[2,64,384]{2,1,0:T(8,128)(2,1)S(1)}, bf16[2,64,384]{2,1,0:T(8,128)(2,1)S(1)}, u32[]{:S(2)}, u32[]{:S(2)}) collective-permute-start(bf16[2,64,384]{2,1,0:T(8,128)(2,1)S(1)} %pad_maximum_fusion), channel_id=1, source_target_pairs={{0,16},{16,32},{32,48},{48,64},{64,80},{80,96},{96,112},{112,128},... | collective-permute-start | bytes 294920 | tf_op jit(solution)/shard_map/ppermute | solution.py:358

commit v5 on v4

--- a/solution.py
+++ b/solution.py
@@ -116,6 +116,15 @@
         out_ref[:, 8 * first : 8 * (first + count), :] = out.reshape(N_BA, 8 * count, 256)
 
 
+def regroup_rows_kernel(own_ref, out_ref):
+    row = iota((WAVES, 1), 0)
+    lat = (row // 40 + jnp.where(own_ref[0] == 0, 1, 0)) % N_AA
+    pair = row % PAIRS
+    shared = (4 * (pair - N_BA) + lat // 8) * 40 + 32 + lat % 8
+    source = jnp.where(pair < N_BA, pair * 40 + lat, shared)
+    out_ref[...] = ones_where(iota((WAVES, N_BA * 40), 1) == source)
+
+
 def regroup_kernel(perm_ref, sums_ref, out_ref):
     sums = sums_ref[...].reshape(N_BA * 40, 256)
     both = jnp.dot(perm_ref[...], sums, preferred_element_type=F32)
@@ -269,12 +278,14 @@
 
 
 def regroup_rows(own):
-    row = jnp.arange(WAVES, dtype=jnp.int32)
-    lat = (row // 40 + (own == 0).astype(jnp.int32)) % N_AA
-    pair = row % PAIRS
-    shared = (4 * (pair - N_BA) + lat // 8) * 40 + 32 + lat % 8
-    source = jnp.where(pair < N_BA, pair * 40 + lat, shared)
-    return (source[:, None] == jnp.arange(N_BA * 40, dtype=jnp.int32)[None, :]).astype(BF16)
+    return pl.pallas_call(
+        regroup_rows_kernel,
+        out_shape=jax.ShapeDtypeStruct((WAVES, N_BA * 40), BF16),
+        in_specs=[pl.BlockSpec(memory_space=pltpu.SMEM)],
+        out_specs=whole(1)[0],
+        compiler_params=params(8),
+        name="regroup_rows",
+    )(own.reshape(1).astype(jnp.int32))
 
 
 def synthesize(places, coefficients):
@@ -291,7 +302,7 @@
             pltpu.VMEM((N_BA, FL, WINDOW), BF16),
             pltpu.SemaphoreType.DMA((3 + N_BA,)),
         ],
-        compiler_params=params(59),
+        compiler_params=params(50),
         name="synthesize",
     )(places, coefficients, jnp.asarray(window_table()))
 
@@ -349,8 +360,9 @@
     own = lax.axis_index("ba")
     pairs = jnp.stack([slot_pairs[first + own], slot_pairs[first + N_BA + own // 4]])
     rows = lax.all_to_all(pack(legendre, spectral), "ba", 0, 0, tiled=True)
+    pairs, perm = lax.optimization_barrier((pairs, regroup_rows(own)))
     sums = lax.all_to_all(legendre_sums(pairs, rows), "ba", 0, 0, tiled=True)
-    by_row = regroup(regroup_rows(own), sums)
+    by_row = regroup(perm, sums)
     coefficients = lax.all_to_all(by_row, "aa", 0, 0, tiled=True)
     blocks = synthesize(wave_places(slot_pairs), coefficients)
     grid = lax.all_to_all(blocks, "ba", 0, 0, tiled=True)

time: 131 us -> 129 us (0.985)
  blocking collectives: 0 us -> 14.7 us
  waiting for transfers between devices: 69.4 us -> 60 us
  starting transfers between devices: 39.5 us -> 32.3 us
    all_to_all x0 -> x1, blocking collectives: none -> 14.7 us  [local(): sums = lax.all_to_all(legendre_sums(pairs, rows), 'ba', 0, 0, tiled=True)]
    all_to_all x1 -> x0, waiting for transfers between devices: 7.35 us -> none  [local(): sums = lax.all_to_all(legendre_sums(pairs, rows), 'ba', 0, 0, tiled=True)]
    all_to_all x1 -> x0, starting transfers between devices: 7.23 us -> none  [local(): sums = lax.all_to_all(legendre_sums(pairs, rows), 'ba', 0, 0, tiled=True)]
    all_to_all x1, waiting for transfers between devices: 25.4 us -> 22.8 us  [local(): rows = lax.all_to_all(pack(legendre, spectral), 'ba', 0, 0, tiled=True)]
    pallas_call x0 -> x1, Pallas kernels: none -> 1.47 us  [regroup_rows(): pl.pallas_call(regroup_rows_kernel, out_shape=jax.ShapeDtypeStruct((WAVES...]
  transfers between devices with their start and end apart: 5 -> 4, of which waited for: 4 -> 3; matrix products, arithmetic and copies ran while one was open for 3% -> 2% of each run, Pallas kernels for 3% -> 4%
where the time goes in v5:
time: 129 us; the launch traced here: 128 us
  waiting for transfers between devices  60 us (47%)
  starting transfers between devices  32.3 us (25%)
  Pallas kernels  17.5 us (14%)
  blocking collectives  14.7 us (11%)
  local copies, waits for them, and re-layouts  2.08 us (2%)
  other arithmetic  1.59 us (1%)
    all_to_all x1, waiting for transfers between devices, local(): coefficients = lax.all_to_all(by_row, 'aa', 0, 0, tiled=True)  24.7 us
    all_to_all x1, waiting for transfers between devices, local(): rows = lax.all_to_all(pack(legendre, spectral), 'ba', 0, 0, tiled=True)  22.8 us
    all_to_all x1, starting transfers between devices, local(): coefficients = lax.all_to_all(by_row, 'aa', 0, 0, tiled=True)  19.5 us
    all_to_all x1, blocking collectives, local(): sums = lax.all_to_all(legendre_sums(pairs, rows), 'ba', 0, 0, tiled=True)  14.7 us
    all_to_all x1, waiting for transfers between devices, local(): grid = lax.all_to_all(blocks, 'ba', 0, 0, tiled=True)  12.5 us
    all_to_all x1, starting transfers between devices, local(): rows = lax.all_to_all(pack(legendre, spectral), 'ba', 0, 0, tiled=True)  7.6 us
    pallas_call x1, Pallas kernels, synthesize(): pl.pallas_call(synthesis_kernel, out_shape=jax.ShapeDtypeStruct((N_BA, FL...  5.15 us
    all_to_all x1, starting transfers between devices, local(): grid = lax.all_to_all(blocks, 'ba', 0, 0, tiled=True)  3.63 us
  transfers between devices with their start and end apart: 4, of which 3 were waited for; matrix products, arithmetic and copies ran while one was open for 2% of the time, Pallas kernels for 4%

profile of v5, /device:TPU:1, one launch (start us, length us, event | category | flops | bytes accessed | tf_op | source)
XLA Modules:
  0.0 128.3 jit_solution(1090137005235760480)
XLA Ops:
  0.0 3.3 %pack.1 = bf16[16,71,8,128]{3,2,1,0:T(8,128)(2,1)} custom-call(bf16[20,32,1281]{2,1,0:T(8,128)(2,1)} %bitcast.7, bf16[20,2,4,1281]{3,2,1,0:T(4,128)(2,1)} %bitcast.8), custom_call_target="tpu_custom_call" | custom-call | tf_op jit(solution)/shard_map/pack/pallas_call | solution.py:242
  3.3 0.0 copy-start.4
  3.4 7.6 %all-to-all-start = ((bf16[16,71,8,128]{3,2,1,0:T(8,128)(2,1)}), bf16[16,71,8,128]{3,2,1,0:T(8,128)(2,1)S(1)}, u32[]{:S(2)}, u32[]{:S(2)}) async-start(bf16[16,71,8,128]{3,2,1,0:T(8,128)(2,1)} %pack.1), calls=%async_computation | async-start | bytes 4653056 | tf_op jit(solution)/shard_map/all_to_all | solution.py:362
  11.0 1.5 %regroup_rows.1.perm_ref = bf16[1280,640]{1,0:T(8,128)(2,1)S(1)} custom-call(s32[1]{0:T(128)} %bitcast.2.own_ref), custom_call_target="tpu_custom_call" | custom-call | tf_op jit(solution)/shard_map/regroup_rows/pallas_call | solution.py:281
  12.5 1.2 copy-done
  13.6 0.6 fusion.4
  14.2 1.3 %pad_add_fusion.pairs_ref = s32[2]{0:T(128)S(1)} fusion(s32[1]{0:T(128)} %get-tuple-element.15, s32[1]{0:T(128)} %get-tuple-element.14), kind=kLoop, calls=%fused_computation.14 | loop fusion | flops 2 | bytes 16 | tf_op jit(solution)/shard_map/stack | solution.py:361
  15.6 22.8 %all-to-all-done.rows_ref = bf16[16,71,8,128]{3,2,1,0:T(8,128)(2,1)S(1)} async-done(((bf16[16,71,8,128]{3,2,1,0:T(8,128)(2,1)}), bf16[16,71,8,128]{3,2,1,0:T(8,128)(2,1)S(1)}, u32[]{:S(2)}, u32[]{:S(2)}) %all-to-all-start) | async-done | bytes 2326560 | tf_op jit(solution)/shard_map/all_to_all | solution.py:362
  38.3 1.3 %legendre_sums.1 = bf16[16,40,256]{2,1,0:T(8,128)(2,1)S(1)} custom-call(s32[2]{0:T(128)S(1)} %pad_add_fusion.pairs_ref, bf16[16,71,8,128]{3,2,1,0:T(8,128)(2,1)S(1)} %all-to-all-done.rows_ref), custom_call_target="tpu_custom_call" | custom-call | tf_op jit(solution)/shard_map/legendre_sums/pallas_call | solution.py:259
  39.7 14.7 %all_to_all.20.sums_ref = bf16[16,40,256]{2,1,0:T(8,128)(2,1)S(1)} all-to-all(bf16[16,40,256]{2,1,0:T(8,128)(2,1)S(1)} %legendre_sums.1), channel_id=1, replica_groups=mesh['aa'=32,'ba'=16] {'ba'}, dimensions={0} | all-to-all | bytes 655360 | tf_op jit(solution)/shard_map/all_to_all | solution.py:364
  54.4 1.4 %regroup.1 = bf16[32,40,128]{2,1,0:T(8,128)(2,1)} custom-call(bf16[1280,640]{1,0:T(8,128)(2,1)S(1)} %copy-done.1, bf16[16,40,256]{2,1,0:T(8,128)(2,1)S(1)} %all_to_all.20.sums_ref), custom_call_target="tpu_custom_call" | custom-call | tf_op jit(solution)/shard_map/regroup/pallas_call | solution.py:270
  55.8 19.5 %all-to-all-start.2 = ((bf16[32,40,128]{2,1,0:T(8,128)(2,1)}), bf16[32,40,128]{2,1,0:T(8,128)(2,1)S(1)}, u32[]{:S(2)}, u32[]{:S(2)}) async-start(bf16[32,40,128]{2,1,0:T(8,128)(2,1)} %regroup.1), calls=%async_computation.2 | async-start | bytes 655360 | tf_op jit(solution)/shard_map/all_to_all | solution.py:366
  75.3 0.1 add.95
  75.4 0.1 broadcast_add_fusion
  75.5 0.1 add.99.places_ref
  75.7 24.7 %all-to-all-done.2.coef_ref = bf16[32,40,128]{2,1,0:T(8,128)(2,1)S(1)} async-done(((bf16[32,40,128]{2,1,0:T(8,128)(2,1)}), bf16[32,40,128]{2,1,0:T(8,128)(2,1)S(1)}, u32[]{:S(2)}, u32[]{:S(2)}) %all-to-all-start.2) | async-done | bytes 327712 | tf_op jit(solution)/shard_map/all_to_all | solution.py:366
  100.3 5.1 %synthesize.1 = bf16[16,64,384]{2,1,0:T(8,128)(2,1)} custom-call(s32[1,1280]{1,0:T(1,128)S(1)} %add.99.places_ref, bf16[32,40,128]{2,1,0:T(8,128)(2,1)S(1)} %all-to-all-done.2.coef_ref, bf16[2,1280,768]{2,1,0:T(8,128)(2,1)} %constant.59.clone.table_ref), custom_call_target="tpu_custom_call" | custom-call | tf_op jit(solution)/shard_map/synthesize/pallas_call | solution.py:293
  105.5 3.6 %all-to-all-start.3 = ((bf16[16,64,384]{2,1,0:T(8,128)(2,1)}), bf16[16,64,384]{2,1,0:T(8,128)(2,1)S(1)}, u32[]{:S(2)}, u32[]{:S(2)}) async-start(bf16[16,64,384]{2,1,0:T(8,128)(2,1)} %synthesize.1), calls=%async_computation.3 | async-start | bytes 1572864 | tf_op jit(solution)/shard_map/all_to_all | solution.py:368
  109.2 0.1 select_bitcast_fusion.1
  109.4 12.5 %all-to-all-done.3.grid_ref = bf16[16,64,384]{2,1,0:T(8,128)(2,1)S(1)} async-done(((bf16[16,64,384]{2,1,0:T(8,128)(2,1)}), bf16[16,64,384]{2,1,0:T(8,128)(2,1)S(1)}, u32[]{:S(2)}, u32[]{:S(2)}) %all-to-all-start.3) | async-done | bytes 786464 | tf_op jit(solution)/shard_map/all_to_all | solution.py:368
  121.9 1.6 %collective-permute-start = (bf16[2,64,384]{2,1,0:T(8,128)(2,1)S(1)}, bf16[2,64,384]{2,1,0:T(8,128)(2,1)S(1)}, u32[]{:S(2)}, u32[]{:S(2)}) collective-permute-start(bf16[2,64,384]{2,1,0:T(8,128)(2,1)S(1)} %pad_maximum_fusion), channel_id=1, source_target_pairs={{0,16},{16,32},{32,48},{48,64},{64,80},{80,96},{96,112},{112,128},... | collective-permute-start | bytes 294920 | tf_op jit(solution)/shard_map/ppermute | solution.py:370
  123.4 0.1 select_maximum_fusion.target_ref
  123.5 3.6 %depart_inner.1.inner_ref = bf16[16,64,320]{2,1,0:T(8,128)(2,1)} custom-call(f32[16,3,384]{2,1,0:T(4,128)S(1)} %select_maximum_fusion.target_ref, bf16[16,64,384]{2,1,0:T(8,128)(2,1)S(1)} %all-to-all-done.3.grid_ref), custom_call_target="tpu_custom_call" | custom-call | flops 440401920 | bytes 4000000 | tf_op jit(solution)/shard_map/depart_inner/pallas_call | solution.py:315
  127.1 1.2 depart_edges.1
  (17 shorter events, 0.1 us)
Async XLA Ops:
  3.3 10.3 %copy-start.4 = (s32[640]{0:T(1024)S(1)}, s32[640]{0:T(1024)}, u32[]{:S(2)}) copy-start(s32[640]{0:T(1024)} %param.8) | copy-start | bytes 7684
  3.4 35.0 %all-to-all-start = ((bf16[16,71,8,128]{3,2,1,0:T(8,128)(2,1)}), bf16[16,71,8,128]{3,2,1,0:T(8,128)(2,1)S(1)}, u32[]{:S(2)}, u32[]{:S(2)}) async-start(bf16[16,71,8,128]{3,2,1,0:T(8,128)(2,1)} %pack.1), calls=%async_computation | async-start | bytes 4653056 | tf_op jit(solution)/shard_map/all_to_all | solution.py:362
  12.4 1.2 copy-start
  38.3 16.1 %copy-start.1 = (bf16[1280,640]{1,0:T(8,128)(2,1)S(1)}, bf16[1280,640]{1,0:T(8,128)(2,1)}, u32[]{:S(2)}) copy-start(bf16[1280,640]{1,0:T(8,128)(2,1)} %copy-done) | copy-start | bytes 4915204
  55.8 44.5 %all-to-all-start.2 = ((bf16[32,40,128]{2,1,0:T(8,128)(2,1)}), bf16[32,40,128]{2,1,0:T(8,128)(2,1)S(1)}, u32[]{:S(2)}, u32[]{:S(2)}) async-start(bf16[32,40,128]{2,1,0:T(8,128)(2,1)} %regroup.1), calls=%async_computation.2 | async-start | bytes 655360 | tf_op jit(solution)/shard_map/all_to_all | solution.py:366
  75.6 33.5 %copy-start.2 = (s32[16,320]{1,0:T(8,128)S(1)}, s32[16,320]{1,0:T(8,128)}, u32[]{:S(2)}) copy-start(s32[16,320]{1,0:T(8,128)} %param.9) | copy-start | bytes 61444
  75.6 33.5 %copy-start.3 = (s32[16,320]{1,0:T(8,128)S(1)}, s32[16,320]{1,0:T(8,128)}, u32[]{:S(2)}) copy-start(s32[16,320]{1,0:T(8,128)} %param.10) | copy-start | bytes 61444
  105.5 16.3 %all-to-all-start.3 = ((bf16[16,64,384]{2,1,0:T(8,128)(2,1)}), bf16[16,64,384]{2,1,0:T(8,128)(2,1)S(1)}, u32[]{:S(2)}, u32[]{:S(2)}) async-start(bf16[16,64,384]{2,1,0:T(8,128)(2,1)} %synthesize.1), calls=%async_computation.3 | async-start | bytes 1572864 | tf_op jit(solution)/shard_map/all_to_all | solution.py:368
  121.9 5.2 %collective-permute-start = (bf16[2,64,384]{2,1,0:T(8,128)(2,1)S(1)}, bf16[2,64,384]{2,1,0:T(8,128)(2,1)S(1)}, u32[]{:S(2)}, u32[]{:S(2)}) collective-permute-start(bf16[2,64,384]{2,1,0:T(8,128)(2,1)S(1)} %pad_maximum_fusion), channel_id=1, source_target_pairs={{0,16},{16,32},{32,48},{48,64},{64,80},{80,96},{96,112},{112,128},... | collective-permute-start | bytes 294920 | tf_op jit(solution)/shard_map/ppermute | solution.py:370

commit v6 on v5

--- a/solution.py
+++ b/solution.py
@@ -141,21 +141,11 @@
     return chosen.astype(F32).astype(BF16)
 
 
-def synthesis_kernel(
-    places_ref, coef_ref, table_ref, out_ref, rows_ref, left_ref, held_ref, blocks_ref, sems
-):
-    arriving = pltpu.make_async_copy(coef_ref, rows_ref, sems.at[2 + N_BA])
-    arriving.start()
-    copies = [
-        pltpu.make_async_copy(table_ref.at[c], held_ref.at[c], sems.at[c]) for c in range(2)
-    ]
-    for copy in copies:
-        copy.start()
+def synthesis_kernel(places_ref, coef_ref, table_ref, out_ref, left_ref):
     row, lane = iota((128, 128), 0), iota((128, 128), 1)
     fields = ones_where(lane == (row % FL) // 4 * 8 + row // FL * 4 + row % 4)
     chosen = ones_where(iota((WAVES, WAVES), 0) == places_ref[...])
-    arriving.wait()
-    rows = rows_ref[...].reshape(WAVES, 128)
+    rows = coef_ref[...].reshape(WAVES, 128)
     turned = lax.dot_general(fields, rows, NT, preferred_element_type=F32).astype(BF16)
     ordered = lax.dot_general(turned, chosen, NT, preferred_element_type=F32)
     real, imag = ordered[:FL], ordered[FL:]
@@ -168,28 +158,17 @@
         here = pl.ds(q * FL, FL)
         left_ref[0, here, :] = (real * alpha - imag * beta).astype(BF16)
         left_ref[1, here, :] = (imag * alpha + real * beta).astype(BF16)
-    copies[0].wait()
-    even = jnp.dot(left_ref[0], held_ref[0], preferred_element_type=F32)
-    copies[1].wait()
-    odd = jnp.dot(left_ref[1], held_ref[1], preferred_element_type=F32)
+    even = jnp.dot(left_ref[0], table_ref[0], preferred_element_type=F32)
+    odd = jnp.dot(left_ref[1], table_ref[1], preferred_element_type=F32)
     ahead, behind = (even + odd).astype(BF16), (even - odd).astype(BF16)
     mirror = ones_where(iota((WINDOW, WINDOW), 0) + iota((WINDOW, WINDOW), 1) == WINDOW)
-    sent = []
-
-    def finish(block, value):
-        blocks_ref[block] = value
-        sent.append(pltpu.make_async_copy(blocks_ref.at[block], out_ref.at[block], sems.at[2 + block]))
-        sent[-1].start()
-
     for w in range(2):
         lanes = slice(w * WINDOW, (w + 1) * WINDOW)
         back = jnp.dot(behind[:, lanes], mirror, preferred_element_type=F32).astype(BF16)
         for q in range(4):
             here = slice(q * FL, (q + 1) * FL)
-            finish(4 * q + w, ahead[here, lanes])
-            finish((4 * q + N_BA - 1 - w) % N_BA, back[here])
-    for copy in sent:
-        copy.wait()
+            out_ref[4 * q + w] = ahead[here, lanes]
+            out_ref[(4 * q + N_BA - 1 - w) % N_BA] = back[here]
 
 
 def band(target, first, count):
@@ -289,20 +268,13 @@
 
 
 def synthesize(places, coefficients):
-    anywhere = pl.BlockSpec(memory_space=pl.ANY)
     return pl.pallas_call(
         synthesis_kernel,
         out_shape=jax.ShapeDtypeStruct((N_BA, FL, WINDOW), BF16),
-        in_specs=whole(1) + [anywhere] * 2,
-        out_specs=anywhere,
-        scratch_shapes=[
-            pltpu.VMEM((N_AA, 40, 128), BF16),
-            pltpu.VMEM((2, 4 * FL, WAVES), BF16),
-            pltpu.VMEM((2, WAVES, 2 * WINDOW), BF16),
-            pltpu.VMEM((N_BA, FL, WINDOW), BF16),
-            pltpu.SemaphoreType.DMA((3 + N_BA,)),
-        ],
-        compiler_params=params(50),
+        in_specs=whole(3),
+        out_specs=whole(1)[0],
+        scratch_shapes=[pltpu.VMEM((2, 4 * FL, WAVES), BF16)],
+        compiler_params=params(24),
         name="synthesize",
     )(places, coefficients, jnp.asarray(window_table()))
 
@@ -360,15 +332,17 @@
     own = lax.axis_index("ba")
     pairs = jnp.stack([slot_pairs[first + own], slot_pairs[first + N_BA + own // 4]])
     rows = lax.all_to_all(pack(legendre, spectral), "ba", 0, 0, tiled=True)
-    pairs, perm = lax.optimization_barrier((pairs, regroup_rows(own)))
+    targets = depart_targets(lat_shift, lon_shift, lax.axis_index("aa") * N_BA)
+    pairs, perm, places, targets = lax.optimization_barrier(
+        (pairs, regroup_rows(own), wave_places(slot_pairs), targets)
+    )
     sums = lax.all_to_all(legendre_sums(pairs, rows), "ba", 0, 0, tiled=True)
     by_row = regroup(perm, sums)
     coefficients = lax.all_to_all(by_row, "aa", 0, 0, tiled=True)
-    blocks = synthesize(wave_places(slot_pairs), coefficients)
+    blocks = synthesize(places, coefficients)
     grid = lax.all_to_all(blocks, "ba", 0, 0, tiled=True)
     ends = jnp.stack([grid[N_BA - 1], grid[0]])
     beside = lax.ppermute(ends, "aa", [(i, (i + 1) % N_AA) for i in range(N_AA)])
-    targets = depart_targets(lat_shift, lon_shift, lax.axis_index("aa") * N_BA)
     inner = depart_inner(targets, grid)
     return depart_edges(inner, targets, beside, grid)
 

time: 129 us -> 125 us (0.969)
  blocking collectives: 14.7 us -> 75.7 us
  waiting for transfers between devices: 60 us -> 22.1 us
  starting transfers between devices: 32.3 us -> 8.48 us
  Pallas kernels: 17.5 us -> 14.3 us
    all_to_all x0 -> x2, blocking collectives: none -> 60.8 us  [the longest x1 44.3 us: local(): coefficients = lax.all_to_all(by_row, 'aa', 0, 0, tiled=True)]
    all_to_all x2 -> x0, waiting for transfers between devices: 37.2 us -> none  [the longest x1 24.7 us: local(): coefficients = lax.all_to_all(by_row, 'aa', 0, 0, tiled=True)]
    all_to_all x2 -> x0, starting transfers between devices: 23.1 us -> none  [the longest x1 19.5 us: local(): coefficients = lax.all_to_all(by_row, 'aa', 0, 0, tiled=True)]
    pallas_call x1, Pallas kernels: 5.15 us -> 2.64 us  [synthesize(): pl.pallas_call(synthesis_kernel, out_shape=jax.ShapeDtypeStruct((N_BA, FL...]
  transfers between devices with their start and end apart: 4 -> 2, of which waited for: 3 -> 1; matrix products, arithmetic and copies ran while one was open for 2% -> 2% of each run, Pallas kernels for 4% -> 4%
where the time goes in v6:
time: 125 us; the launch traced here: 124 us
  blocking collectives  75.7 us (61%)
  waiting for transfers between devices  22.1 us (18%)
  Pallas kernels  14.3 us (11%)
  starting transfers between devices  8.48 us (7%)
  local copies, waits for them, and re-layouts  2.08 us (2%)
  other arithmetic  1.62 us (1%)
    all_to_all x1, blocking collectives, local(): coefficients = lax.all_to_all(by_row, 'aa', 0, 0, tiled=True)  44.3 us
    all_to_all x1, waiting for transfers between devices, local(): rows = lax.all_to_all(pack(legendre, spectral), 'ba', 0, 0, tiled=True)  22.1 us
    all_to_all x1, blocking collectives, local(): grid = lax.all_to_all(blocks, 'ba', 0, 0, tiled=True)  16.5 us
    all_to_all x1, blocking collectives, local(): sums = lax.all_to_all(legendre_sums(pairs, rows), 'ba', 0, 0, tiled=True)  14.9 us
    all_to_all x1, starting transfers between devices, local(): rows = lax.all_to_all(pack(legendre, spectral), 'ba', 0, 0, tiled=True)  7.73 us
    pallas_call x1, Pallas kernels, depart_inner(): pl.pallas_call(inner_kernel, out_shape=jax.ShapeDtypeStruct((N_BA, FL, BL...  3.59 us
    pallas_call x1, Pallas kernels, pack(): pl.pallas_call(pack_kernel, out_shape=jax.ShapeDtypeStruct((N_BA, TILES,...  3.34 us
    pallas_call x1, Pallas kernels, synthesize(): pl.pallas_call(synthesis_kernel, out_shape=jax.ShapeDtypeStruct((N_BA, FL...  2.64 us
  transfers between devices with their start and end apart: 2, of which 1 were waited for; matrix products, arithmetic and copies ran while one was open for 2% of the time, Pallas kernels for 4%

profile of v6, /device:TPU:1, one launch (start us, length us, event | category | flops | bytes accessed | tf_op | source)
XLA Modules:
  0.0 124.5 jit_solution(4977296929830536434)
XLA Ops:
  0.0 3.3 %pack.1 = bf16[16,71,8,128]{3,2,1,0:T(8,128)(2,1)} custom-call(bf16[20,32,1281]{2,1,0:T(8,128)(2,1)} %bitcast.7, bf16[20,2,4,1281]{3,2,1,0:T(4,128)(2,1)} %bitcast.8), custom_call_target="tpu_custom_call" | custom-call | tf_op jit(solution)/shard_map/pack/pallas_call | solution.py:221
  3.3 0.0 copy-start.5
  3.4 0.0 copy-start.3
  3.4 0.0 copy-start.4
  3.4 7.7 %all-to-all-start = ((bf16[16,71,8,128]{3,2,1,0:T(8,128)(2,1)}), bf16[16,71,8,128]{3,2,1,0:T(8,128)(2,1)S(1)}, u32[]{:S(2)}, u32[]{:S(2)}) async-start(bf16[16,71,8,128]{3,2,1,0:T(8,128)(2,1)} %pack.1), calls=%async_computation | async-start | bytes 4653056 | tf_op jit(solution)/shard_map/all_to_all | solution.py:334
  11.2 0.1 add.91
  11.3 0.1 broadcast_add_fusion
  11.3 0.1 add.95.places_ref
  11.5 0.1 select_bitcast_fusion.1
  11.7 1.5 %regroup_rows.1.perm_ref = bf16[1280,640]{1,0:T(8,128)(2,1)S(1)} custom-call(s32[1]{0:T(128)} %bitcast.own_ref), custom_call_target="tpu_custom_call" | custom-call | tf_op jit(solution)/shard_map/regroup_rows/pallas_call | solution.py:260
  13.2 1.1 copy-done
  14.3 0.6 fusion.4
  14.9 1.4 %pad_add_fusion.pairs_ref = s32[2]{0:T(128)S(1)} fusion(s32[1]{0:T(128)} %get-tuple-element.19, s32[1]{0:T(128)} %get-tuple-element.18), kind=kLoop, calls=%fused_computation.14 | loop fusion | flops 2 | bytes 16 | tf_op jit(solution)/shard_map/stack | solution.py:333
  16.3 0.1 select_maximum_fusion.target_ref
  16.4 22.1 %all-to-all-done.rows_ref = bf16[16,71,8,128]{3,2,1,0:T(8,128)(2,1)S(1)} async-done(((bf16[16,71,8,128]{3,2,1,0:T(8,128)(2,1)}), bf16[16,71,8,128]{3,2,1,0:T(8,128)(2,1)S(1)}, u32[]{:S(2)}, u32[]{:S(2)}) %all-to-all-start) | async-done | bytes 2326560 | tf_op jit(solution)/shard_map/all_to_all | solution.py:334
  38.5 1.3 %legendre_sums.1 = bf16[16,40,256]{2,1,0:T(8,128)(2,1)S(1)} custom-call(s32[2]{0:T(128)S(1)} %pad_add_fusion.pairs_ref, bf16[16,71,8,128]{3,2,1,0:T(8,128)(2,1)S(1)} %all-to-all-done.rows_ref), custom_call_target="tpu_custom_call" | custom-call | tf_op jit(solution)/shard_map/legendre_sums/pallas_call | solution.py:238
  39.8 14.9 %all_to_all.20.sums_ref = bf16[16,40,256]{2,1,0:T(8,128)(2,1)S(1)} all-to-all(bf16[16,40,256]{2,1,0:T(8,128)(2,1)S(1)} %legendre_sums.1), channel_id=1, replica_groups=mesh['aa'=32,'ba'=16] {'ba'}, dimensions={0} | all-to-all | bytes 655360 | tf_op jit(solution)/shard_map/all_to_all | solution.py:339
  54.7 0.7 regroup.1
  55.4 44.3 %all_to_all.21.coef_ref = bf16[32,40,128]{2,1,0:T(8,128)(2,1)S(1)} all-to-all(bf16[32,40,128]{2,1,0:T(8,128)(2,1)S(1)} %regroup.1), channel_id=1, replica_groups=mesh['aa'=32,'ba'=16] {'aa'}, dimensions={0} | all-to-all | bytes 655360 | tf_op jit(solution)/shard_map/all_to_all | solution.py:341
  99.7 2.6 %synthesize.1 = bf16[16,64,384]{2,1,0:T(8,128)(2,1)S(1)} custom-call(s32[1,1280]{1,0:T(1,128)S(1)} %add.95.places_ref, bf16[32,40,128]{2,1,0:T(8,128)(2,1)S(1)} %all_to_all.21.coef_ref, bf16[2,1280,768]{2,1,0:T(8,128)(2,1)S(1)} %copy-done.2), custom_call_target="tpu_custom_call" | custom-call | tf_op jit(solution)/shard_map/synthesize/pallas_call | solution.py:271
  102.4 16.5 %all_to_all.22.grid_ref = bf16[16,64,384]{2,1,0:T(8,128)(2,1)S(1)} all-to-all(bf16[16,64,384]{2,1,0:T(8,128)(2,1)S(1)} %synthesize.1), channel_id=1, replica_groups=mesh['aa'=32,'ba'=16] {'ba'}, dimensions={0} | all-to-all | bytes 1572864 | tf_op jit(solution)/shard_map/all_to_all | solution.py:343
  119.0 0.8 collective-permute-start
  119.7 3.6 %depart_inner.1.inner_ref = bf16[16,64,320]{2,1,0:T(8,128)(2,1)} custom-call(f32[16,3,384]{2,1,0:T(4,128)S(1)} %select_maximum_fusion.target_ref, bf16[16,64,384]{2,1,0:T(8,128)(2,1)S(1)} %all_to_all.22.grid_ref), custom_call_target="tpu_custom_call" | custom-call | flops 440401920 | bytes 4000000 | tf_op jit(solution)/shard_map/depart_inner/pallas_call | solution.py:287
  123.3 1.2 depart_edges.1
  (17 shorter events, 0.1 us)
Async XLA Ops:
  3.3 7.8 %copy-start.5 = (s32[640]{0:T(1024)S(1)}, s32[640]{0:T(1024)}, u32[]{:S(2)}) copy-start(s32[640]{0:T(1024)} %param.8) | copy-start | bytes 7684
  3.4 8.1 %copy-start.3 = (s32[16,320]{1,0:T(8,128)S(1)}, s32[16,320]{1,0:T(8,128)}, u32[]{:S(2)}) copy-start(s32[16,320]{1,0:T(8,128)} %param.9) | copy-start | bytes 61444
  3.4 8.1 %copy-start.4 = (s32[16,320]{1,0:T(8,128)S(1)}, s32[16,320]{1,0:T(8,128)}, u32[]{:S(2)}) copy-start(s32[16,320]{1,0:T(8,128)} %param.10) | copy-start | bytes 61444
  3.4 35.1 %all-to-all-start = ((bf16[16,71,8,128]{3,2,1,0:T(8,128)(2,1)}), bf16[16,71,8,128]{3,2,1,0:T(8,128)(2,1)S(1)}, u32[]{:S(2)}, u32[]{:S(2)}) async-start(bf16[16,71,8,128]{3,2,1,0:T(8,128)(2,1)} %pack.1), calls=%async_computation | async-start | bytes 4653056 | tf_op jit(solution)/shard_map/all_to_all | solution.py:334
  13.2 1.2 copy-start
  38.5 16.2 %copy-start.1 = (bf16[1280,640]{1,0:T(8,128)(2,1)S(1)}, bf16[1280,640]{1,0:T(8,128)(2,1)}, u32[]{:S(2)}) copy-start(bf16[1280,640]{1,0:T(8,128)(2,1)} %copy-done) | copy-start | bytes 4915204
  38.5 61.2 %copy-start.2 = (bf16[2,1280,768]{2,1,0:T(8,128)(2,1)S(1)}, bf16[2,1280,768]{2,1,0:T(8,128)(2,1)}, u32[]{:S(2)}) copy-start(bf16[2,1280,768]{2,1,0:T(8,128)(2,1)} %constant.59.clone.table_ref) | copy-start | bytes 11796484
  119.0 4.3 %collective-permute-start = (bf16[2,64,384]{2,1,0:T(8,128)(2,1)S(1)}, bf16[2,64,384]{2,1,0:T(8,128)(2,1)S(1)}, u32[]{:S(2)}, u32[]{:S(2)}) collective-permute-start(bf16[2,64,384]{2,1,0:T(8,128)(2,1)S(1)} %pad_maximum_fusion), channel_id=1, source_target_pairs={{0,16},{16,32},{32,48},{48,64},{64,80},{80,96},{96,112},{112,128},... | collective-permute-start | bytes 294920 | tf_op jit(solution)/shard_map/ppermute | solution.py:345

commit v7 on v6

--- a/solution.py
+++ b/solution.py
@@ -51,19 +51,26 @@
 
 
 def pack_kernel(rows_ref, values_ref, out_ref, rows_held, values_held, out_held, sems):
-    into = [pltpu.make_async_copy(values_ref, values_held, sems.at[PAIRS])]
-    for pair in [i for q in range(4) for i in (N_BA + q, 4 * q, 4 * q + 1, 4 * q + 2, 4 * q + 3)]:
-        into.append(pltpu.make_async_copy(rows_ref.at[pair], rows_held.at[pair], sems.at[pair]))
-    for copy in into:
-        copy.start()
-    into[0].wait()
+    into = []
+    for q in range(4):
+        four = pl.ds(4 * q, 4)
+        into.append(
+            [
+                pltpu.make_async_copy(rows_ref.at[N_BA + q], rows_held.at[N_BA + q], sems.at[q]),
+                pltpu.make_async_copy(values_ref.at[N_BA + q], values_held.at[N_BA + q], sems.at[4 + q]),
+                pltpu.make_async_copy(rows_ref.at[four], rows_held.at[four], sems.at[8 + q]),
+                pltpu.make_async_copy(values_ref.at[four], values_held.at[four], sems.at[12 + q]),
+            ]
+        )
+        for copy in into[q]:
+            copy.start()
     out = []
     lane = lax.broadcasted_iota(jnp.int32, (8, 128), 1)
     for d in range(N_BA):
         q, h = d // 4, d % 4
         if h == 0:
-            into[1 + 5 * q].wait()
-        into[2 + 5 * q + h].wait()
+            for copy in into[q]:
+                copy.wait()
         last = jnp.zeros((8, 128), F32)
         for g in range(7):
             for k in range(KTILES + 1):
@@ -184,13 +191,16 @@
         held[...] = jnp.zeros_like(held)
 
 
-def depart_row(target_ref, at, sources, bands, out_ref, to):
+def fill_bands(target_ref, at, bands):
     for t, (part, lanes, last, first) in enumerate(((0, 384, 176, 0), (0, 384, 176, 128), (1, 128, 112, 0))):
         for step in range(3):
             target = target_ref[at, step : step + 1, t * 128 : (t + 1) * 128]
             target = jnp.broadcast_to(target, (last - 16, 128))
             begin = step * lanes + first + 16
             bands[part][begin : begin + last - 16, first : first + 128] = band(target, 16, last - 16)
+
+
+def multiply_bands(sources, bands, out_ref, to):
     for part, (lane, x, width) in enumerate(((0, 0, 256), (256, 256, 64))):
         left = jnp.concatenate([s[:, lane:] for s in sources], axis=1)
         out = jnp.dot(left, bands[part][...], preferred_element_type=F32).astype(BF16)
@@ -200,18 +210,25 @@
 def inner_kernel(target_ref, grid_ref, out_ref, *bands):
     clear(bands)
 
-    @pl.loop(2, N_BA, unroll=7)
+    @pl.loop(2, N_BA, unroll=14)
     def _(row):
         above = jnp.where(row == N_BA - 1, 0, row + 1)
         sources = [grid_ref.at[row - 1], grid_ref.at[row], grid_ref.at[above]]
-        depart_row(target_ref, row, sources, bands, out_ref, row)
-
-
-def edge_kernel(inner_ref, target_ref, beside_ref, grid_ref, out_ref, *bands):
+        fill_bands(target_ref, row, bands)
+        multiply_bands(sources, bands, out_ref, row)
+
+
+def edge_bands_kernel(target_ref, *bands):
     clear(bands)
+    for row in range(2):
+        fill_bands(target_ref, row, [held.at[row] for held in bands])
+
+
+def edge_kernel(inner_ref, wide_ref, narrow_ref, beside_ref, grid_ref, out_ref):
     sources = [beside_ref.at[0], beside_ref.at[1], grid_ref.at[1], grid_ref.at[2]]
     for row in range(2):
-        depart_row(target_ref, row, sources[row : row + 3], bands, out_ref, row)
+        bands = [wide_ref.at[row], narrow_ref.at[row]]
+        multiply_bands(sources[row : row + 3], bands, out_ref, row)
 
 
 def pack(legendre, spectral):
@@ -298,18 +315,31 @@
     )(targets, grid)
 
 
-def depart_edges(inner, targets, beside, grid):
+def edge_bands(targets):
+    return pl.pallas_call(
+        edge_bands_kernel,
+        out_shape=(
+            jax.ShapeDtypeStruct((2, 1152, 256), BF16),
+            jax.ShapeDtypeStruct((2, 384, 128), BF16),
+        ),
+        in_specs=whole(1),
+        out_specs=tuple(whole(2)),
+        compiler_params=params(8),
+        name="edge_bands",
+    )(targets)
+
+
+def depart_edges(inner, bands, beside, grid):
     return pl.pallas_call(
         edge_kernel,
         grid=(1,),
         out_shape=jax.ShapeDtypeStruct((N_BA, FL, BLOCK), BF16),
-        in_specs=[pl.BlockSpec(memory_space=pl.ANY)] + whole(3),
+        in_specs=[pl.BlockSpec(memory_space=pl.ANY)] + whole(4),
         out_specs=pl.BlockSpec((2, FL, BLOCK), lambda e: (0, 0, 0)),
-        scratch_shapes=band_scratch(),
         input_output_aliases={0: 0},
         compiler_params=params(24),
         name="depart_edges",
-    )(inner, targets, beside, grid)
+    )(inner, *bands, beside, grid)
 
 
 def depart_targets(lat_shift, lon_shift, first_row):
@@ -333,8 +363,8 @@
     pairs = jnp.stack([slot_pairs[first + own], slot_pairs[first + N_BA + own // 4]])
     rows = lax.all_to_all(pack(legendre, spectral), "ba", 0, 0, tiled=True)
     targets = depart_targets(lat_shift, lon_shift, lax.axis_index("aa") * N_BA)
-    pairs, perm, places, targets = lax.optimization_barrier(
-        (pairs, regroup_rows(own), wave_places(slot_pairs), targets)
+    pairs, perm, places, targets, bands = lax.optimization_barrier(
+        (pairs, regroup_rows(own), wave_places(slot_pairs), targets, edge_bands(targets))
     )
     sums = lax.all_to_all(legendre_sums(pairs, rows), "ba", 0, 0, tiled=True)
     by_row = regroup(perm, sums)
@@ -344,7 +374,7 @@
     ends = jnp.stack([grid[N_BA - 1], grid[0]])
     beside = lax.ppermute(ends, "aa", [(i, (i + 1) % N_AA) for i in range(N_AA)])
     inner = depart_inner(targets, grid)
-    return depart_edges(inner, targets, beside, grid)
+    return depart_edges(inner, bands, beside, grid)
 
 
 def solution(mesh):

time: 125 us -> 124 us (level)
  no operation moved by 1% of the time
where the time goes in v7:
time: 124 us
  blocking collectives  75.8 us (61%)
  waiting for transfers between devices  21 us (17%)
  Pallas kernels  13.8 us (11%)
  starting transfers between devices  8.48 us (7%)
  local copies, waits for them, and re-layouts  3.04 us (2%)
  other arithmetic  1.46 us (1%)
    all_to_all x1, blocking collectives, local(): coefficients = lax.all_to_all(by_row, 'aa', 0, 0, tiled=True)  44.3 us
    all_to_all x1, waiting for transfers between devices, local(): rows = lax.all_to_all(pack(legendre, spectral), 'ba', 0, 0, tiled=True)  21 us
    all_to_all x1, blocking collectives, local(): grid = lax.all_to_all(blocks, 'ba', 0, 0, tiled=True)  16.7 us
    all_to_all x1, blocking collectives, local(): sums = lax.all_to_all(legendre_sums(pairs, rows), 'ba', 0, 0, tiled=True)  14.8 us
    all_to_all x1, starting transfers between devices, local(): rows = lax.all_to_all(pack(legendre, spectral), 'ba', 0, 0, tiled=True)  7.73 us
    pallas_call x1, Pallas kernels, depart_inner(): pl.pallas_call(inner_kernel, out_shape=jax.ShapeDtypeStruct((N_BA, FL, BL...  3.44 us
    pallas_call x1, Pallas kernels, pack(): pl.pallas_call(pack_kernel, out_shape=jax.ShapeDtypeStruct((N_BA, TILES,...  2.91 us
    pallas_call x1, Pallas kernels, synthesize(): pl.pallas_call(synthesis_kernel, out_shape=jax.ShapeDtypeStruct((N_BA, FL...  2.64 us
  transfers between devices with their start and end apart: 2, of which 1 were waited for; matrix products, arithmetic and copies ran while one was open for 2% of the time, Pallas kernels for 4%

profile of v7, /device:TPU:1, one launch (start us, length us, event | category | flops | bytes accessed | tf_op | source)
XLA Modules:
  0.0 123.9 jit_solution(3611509090784418776)
XLA Ops:
  0.0 2.9 %pack.1 = bf16[16,71,8,128]{3,2,1,0:T(8,128)(2,1)} custom-call(bf16[20,32,1281]{2,1,0:T(8,128)(2,1)} %bitcast.7, bf16[20,2,4,1281]{3,2,1,0:T(4,128)(2,1)} %bitcast.8), custom_call_target="tpu_custom_call" | custom-call | tf_op jit(solution)/shard_map/pack/pallas_call | solution.py:238
  3.0 7.7 %all-to-all-start = ((bf16[16,71,8,128]{3,2,1,0:T(8,128)(2,1)}), bf16[16,71,8,128]{3,2,1,0:T(8,128)(2,1)S(1)}, u32[]{:S(2)}, u32[]{:S(2)}) async-start(bf16[16,71,8,128]{3,2,1,0:T(8,128)(2,1)} %pack.1), calls=%async_computation | async-start | bytes 4653056 | tf_op jit(solution)/shard_map/all_to_all | solution.py:364
  10.7 0.1 add.91
  10.8 0.1 broadcast_add_fusion
  10.9 0.1 add.95.places_ref
  11.1 0.1 select_bitcast_fusion.1
  11.3 0.1 select_maximum_fusion.target_ref
  11.4 0.3 edge_bands.1
  11.7 0.3 copy-done.3
  12.0 0.7 copy-done.5
  12.6 1.5 %regroup_rows.1.perm_ref = bf16[1280,640]{1,0:T(8,128)(2,1)S(1)} custom-call(s32[1]{0:T(128)} %bitcast.own_ref), custom_call_target="tpu_custom_call" | custom-call | tf_op jit(solution)/shard_map/regroup_rows/pallas_call | solution.py:277
  14.1 1.2 copy-done
  15.3 0.6 fusion.4
  15.9 1.2 pad_add_fusion.pairs_ref
  17.1 21.0 %all-to-all-done.rows_ref = bf16[16,71,8,128]{3,2,1,0:T(8,128)(2,1)S(1)} async-done(((bf16[16,71,8,128]{3,2,1,0:T(8,128)(2,1)}), bf16[16,71,8,128]{3,2,1,0:T(8,128)(2,1)S(1)}, u32[]{:S(2)}, u32[]{:S(2)}) %all-to-all-start) | async-done | bytes 2326560 | tf_op jit(solution)/shard_map/all_to_all | solution.py:364
  38.1 1.3 %legendre_sums.1 = bf16[16,40,256]{2,1,0:T(8,128)(2,1)S(1)} custom-call(s32[2]{0:T(128)S(1)} %pad_add_fusion.pairs_ref, bf16[16,71,8,128]{3,2,1,0:T(8,128)(2,1)S(1)} %all-to-all-done.rows_ref), custom_call_target="tpu_custom_call" | custom-call | tf_op jit(solution)/shard_map/legendre_sums/pallas_call | solution.py:255
  39.4 14.8 %all_to_all.20.sums_ref = bf16[16,40,256]{2,1,0:T(8,128)(2,1)S(1)} all-to-all(bf16[16,40,256]{2,1,0:T(8,128)(2,1)S(1)} %legendre_sums.1), channel_id=1, replica_groups=mesh['aa'=32,'ba'=16] {'ba'}, dimensions={0} | all-to-all | bytes 655360 | tf_op jit(solution)/shard_map/all_to_all | solution.py:369
  54.3 0.7 regroup.1
  55.0 44.3 %all_to_all.21.coef_ref = bf16[32,40,128]{2,1,0:T(8,128)(2,1)S(1)} all-to-all(bf16[32,40,128]{2,1,0:T(8,128)(2,1)S(1)} %regroup.1), channel_id=1, replica_groups=mesh['aa'=32,'ba'=16] {'aa'}, dimensions={0} | all-to-all | bytes 655360 | tf_op jit(solution)/shard_map/all_to_all | solution.py:371
  99.3 2.6 %synthesize.1 = bf16[16,64,384]{2,1,0:T(8,128)(2,1)S(1)} custom-call(s32[1,1280]{1,0:T(1,128)S(1)} %add.95.places_ref, bf16[32,40,128]{2,1,0:T(8,128)(2,1)S(1)} %all_to_all.21.coef_ref, bf16[2,1280,768]{2,1,0:T(8,128)(2,1)S(1)} %copy-done.2), custom_call_target="tpu_custom_call" | custom-call | tf_op jit(solution)/shard_map/synthesize/pallas_call | solution.py:288
  101.9 16.7 %all_to_all.22.grid_ref = bf16[16,64,384]{2,1,0:T(8,128)(2,1)S(1)} all-to-all(bf16[16,64,384]{2,1,0:T(8,128)(2,1)S(1)} %synthesize.1), channel_id=1, replica_groups=mesh['aa'=32,'ba'=16] {'ba'}, dimensions={0} | all-to-all | bytes 1572864 | tf_op jit(solution)/shard_map/all_to_all | solution.py:373
  118.7 0.8 collective-permute-start
  119.4 3.4 %depart_inner.1.inner_ref = bf16[16,64,320]{2,1,0:T(8,128)(2,1)} custom-call(f32[16,3,384]{2,1,0:T(4,128)S(1)} %copy-done.4, bf16[16,64,384]{2,1,0:T(8,128)(2,1)S(1)} %all_to_all.22.grid_ref), custom_call_target="tpu_custom_call" | custom-call | flops 440401920 | bytes 4000000 | tf_op jit(solution)/shard_map/depart_inner/pallas_call | solution.py:304
  122.9 1.0 depart_edges.1
  (26 shorter events, 0.2 us)
Async XLA Ops:
  2.9 7.8 %copy-start.9 = (s32[640]{0:T(1024)S(1)}, s32[640]{0:T(1024)}, u32[]{:S(2)}) copy-start(s32[640]{0:T(1024)} %param.8) | copy-start | bytes 7684
  2.9 8.1 %copy-start.7 = (s32[16,320]{1,0:T(8,128)S(1)}, s32[16,320]{1,0:T(8,128)}, u32[]{:S(2)}) copy-start(s32[16,320]{1,0:T(8,128)} %param.9) | copy-start | bytes 61444
  2.9 8.1 %copy-start.8 = (s32[16,320]{1,0:T(8,128)S(1)}, s32[16,320]{1,0:T(8,128)}, u32[]{:S(2)}) copy-start(s32[16,320]{1,0:T(8,128)} %param.10) | copy-start | bytes 61444
  3.0 35.1 %all-to-all-start = ((bf16[16,71,8,128]{3,2,1,0:T(8,128)(2,1)}), bf16[16,71,8,128]{3,2,1,0:T(8,128)(2,1)S(1)}, u32[]{:S(2)}, u32[]{:S(2)}) async-start(bf16[16,71,8,128]{3,2,1,0:T(8,128)(2,1)} %pack.1), calls=%async_computation | async-start | bytes 4653056 | tf_op jit(solution)/shard_map/all_to_all | solution.py:364
  11.3 0.6 copy-start.3
  12.0 0.7 copy-start.5
  14.1 1.2 copy-start
  38.1 16.2 %copy-start.1 = (bf16[1280,640]{1,0:T(8,128)(2,1)S(1)}, bf16[1280,640]{1,0:T(8,128)(2,1)}, u32[]{:S(2)}) copy-start(bf16[1280,640]{1,0:T(8,128)(2,1)} %copy-done) | copy-start | bytes 4915204
  38.1 61.2 %copy-start.2 = (bf16[2,1280,768]{2,1,0:T(8,128)(2,1)S(1)}, bf16[2,1280,768]{2,1,0:T(8,128)(2,1)}, u32[]{:S(2)}) copy-start(bf16[2,1280,768]{2,1,0:T(8,128)(2,1)} %constant.59.clone.table_ref) | copy-start | bytes 11796484
  99.3 20.1 %copy-start.4 = (f32[16,3,384]{2,1,0:T(4,128)S(1)}, f32[16,3,384]{2,1,0:T(4,128)}, u32[]{:S(2)}) copy-start(f32[16,3,384]{2,1,0:T(4,128)} %copy-done.3) | copy-start | bytes 221188
  101.9 20.9 %copy-start.6 = (bf16[2,384,128]{2,1,0:T(8,128)(2,1)S(1)}, bf16[2,384,128]{2,1,0:T(8,128)(2,1)}, u32[]{:S(2)}) copy-start(bf16[2,384,128]{2,1,0:T(8,128)(2,1)} %copy-done.5) | copy-start | bytes 589828
  118.7 4.2 %collective-permute-start = (bf16[2,64,384]{2,1,0:T(8,128)(2,1)S(1)}, bf16[2,64,384]{2,1,0:T(8,128)(2,1)S(1)}, u32[]{:S(2)}, u32[]{:S(2)}) collective-permute-start(bf16[2,64,384]{2,1,0:T(8,128)(2,1)S(1)} %pad_maximum_fusion), channel_id=1, source_target_pairs={{0,16},{16,32},{32,48},{48,64},{64,80},{80,96},{96,112},{112,128},... | collective-permute-start | bytes 294920 | tf_op jit(solution)/shard_map/ppermute | solution.py:375

commit v8 on v7

--- a/solution.py
+++ b/solution.py
@@ -148,13 +148,18 @@
     return chosen.astype(F32).astype(BF16)
 
 
+def column_kernel(places_ref, out_ref):
+    row = jnp.broadcast_to(places_ref[...].astype(F32), (8, WAVES))
+    out_ref[...] = jnp.broadcast_to(row.T[:, :1], (WAVES, 128)).astype(jnp.int32)
+
+
 def synthesis_kernel(places_ref, coef_ref, table_ref, out_ref, left_ref):
     row, lane = iota((128, 128), 0), iota((128, 128), 1)
     fields = ones_where(lane == (row % FL) // 4 * 8 + row // FL * 4 + row % 4)
-    chosen = ones_where(iota((WAVES, WAVES), 0) == places_ref[...])
+    chosen = ones_where(iota((WAVES, WAVES), 1) == places_ref[:, :1])
     rows = coef_ref[...].reshape(WAVES, 128)
     turned = lax.dot_general(fields, rows, NT, preferred_element_type=F32).astype(BF16)
-    ordered = lax.dot_general(turned, chosen, NT, preferred_element_type=F32)
+    ordered = jnp.dot(turned, chosen, preferred_element_type=F32)
     real, imag = ordered[:FL], ordered[FL:]
     place = iota((1, WAVES), 1)
     wave = jnp.where(place < WAVES // 2, place, WAVES + WAVES // 2 - 1 - place)
@@ -284,6 +289,17 @@
     )(own.reshape(1).astype(jnp.int32))
 
 
+def column_places(places):
+    return pl.pallas_call(
+        column_kernel,
+        out_shape=jax.ShapeDtypeStruct((WAVES, 128), jnp.int32),
+        in_specs=whole(1),
+        out_specs=whole(1)[0],
+        compiler_params=params(8),
+        name="column_places",
+    )(places)
+
+
 def synthesize(places, coefficients):
     return pl.pallas_call(
         synthesis_kernel,
@@ -364,7 +380,7 @@
     rows = lax.all_to_all(pack(legendre, spectral), "ba", 0, 0, tiled=True)
     targets = depart_targets(lat_shift, lon_shift, lax.axis_index("aa") * N_BA)
     pairs, perm, places, targets, bands = lax.optimization_barrier(
-        (pairs, regroup_rows(own), wave_places(slot_pairs), targets, edge_bands(targets))
+        (pairs, regroup_rows(own), column_places(wave_places(slot_pairs)), targets, edge_bands(targets))
     )
     sums = lax.all_to_all(legendre_sums(pairs, rows), "ba", 0, 0, tiled=True)
     by_row = regroup(perm, sums)

time: 124 us -> 124 us (level)
  transfers between devices with their start and end apart: 2 -> 2, of which waited for: 1 -> 1; matrix products, arithmetic and copies ran while one was open for 2% -> 2% of each run, Pallas kernels for 4% -> 5%
where the time goes in v8:
time: 124 us; the launch traced here: 123 us
  blocking collectives  75.8 us (61%)
  waiting for transfers between devices  20.2 us (16%)
  Pallas kernels  13.9 us (11%)
  starting transfers between devices  8.48 us (7%)
  local copies, waits for them, and re-layouts  3.14 us (3%)
  other arithmetic  1.68 us (1%)
    all_to_all x1, blocking collectives, local(): coefficients = lax.all_to_all(by_row, 'aa', 0, 0, tiled=True)  44.3 us
    all_to_all x1, waiting for transfers between devices, local(): rows = lax.all_to_all(pack(legendre, spectral), 'ba', 0, 0, tiled=True)  20.2 us
    all_to_all x1, blocking collectives, local(): grid = lax.all_to_all(blocks, 'ba', 0, 0, tiled=True)  16.7 us
    all_to_all x1, blocking collectives, local(): sums = lax.all_to_all(legendre_sums(pairs, rows), 'ba', 0, 0, tiled=True)  14.8 us
    all_to_all x1, starting transfers between devices, local(): rows = lax.all_to_all(pack(legendre, spectral), 'ba', 0, 0, tiled=True)  7.73 us
    pallas_call x1, Pallas kernels, depart_inner(): pl.pallas_call(inner_kernel, out_shape=jax.ShapeDtypeStruct((N_BA, FL, BL...  3.44 us
    pallas_call x1, Pallas kernels, pack(): pl.pallas_call(pack_kernel, out_shape=jax.ShapeDtypeStruct((N_BA, TILES,...  2.9 us
  transfers between devices with their start and end apart: 2, of which 1 were waited for; matrix products, arithmetic and copies ran while one was open for 2% of the time, Pallas kernels for 5%

profile of v8, /device:TPU:1, one launch (start us, length us, event | category | flops | bytes accessed | tf_op | source)
XLA Modules:
  0.0 123.5 jit_solution(8194297023295707197)
XLA Ops:
  0.0 2.9 %pack.1 = bf16[16,71,8,128]{3,2,1,0:T(8,128)(2,1)} custom-call(bf16[20,32,1281]{2,1,0:T(8,128)(2,1)} %bitcast.7, bf16[20,2,4,1281]{3,2,1,0:T(4,128)(2,1)} %bitcast.8), custom_call_target="tpu_custom_call" | custom-call | tf_op jit(solution)/shard_map/pack/pallas_call | solution.py:243
  2.9 7.7 %all-to-all-start = ((bf16[16,71,8,128]{3,2,1,0:T(8,128)(2,1)}), bf16[16,71,8,128]{3,2,1,0:T(8,128)(2,1)S(1)}, u32[]{:S(2)}, u32[]{:S(2)}) async-start(bf16[16,71,8,128]{3,2,1,0:T(8,128)(2,1)} %pack.1), calls=%async_computation | async-start | bytes 4653056 | tf_op jit(solution)/shard_map/all_to_all | solution.py:380
  10.7 0.1 add.91
  10.8 0.1 broadcast_add_fusion
  10.9 0.1 add.95.places_ref
  11.1 0.1 select_bitcast_fusion.1
  11.2 0.5 column_places.1.places_ref
  11.7 0.1 select_maximum_fusion.target_ref
  11.8 0.3 edge_bands.1
  12.1 1.0 copy-done.3
  13.1 1.5 %regroup_rows.1.perm_ref = bf16[1280,640]{1,0:T(8,128)(2,1)S(1)} custom-call(s32[1]{0:T(128)} %bitcast.own_ref), custom_call_target="tpu_custom_call" | custom-call | tf_op jit(solution)/shard_map/regroup_rows/pallas_call | solution.py:282
  14.6 1.2 copy-done
  15.8 0.7 fusion.4
  16.4 1.4 %pad_add_fusion.pairs_ref = s32[2]{0:T(128)S(1)} fusion(s32[1]{0:T(128)} %get-tuple-element.27, s32[1]{0:T(128)} %get-tuple-element.26), kind=kLoop, calls=%fused_computation.14 | loop fusion | flops 2 | bytes 16 | tf_op jit(solution)/shard_map/stack | solution.py:379
  17.8 20.2 %all-to-all-done.rows_ref = bf16[16,71,8,128]{3,2,1,0:T(8,128)(2,1)S(1)} async-done(((bf16[16,71,8,128]{3,2,1,0:T(8,128)(2,1)}), bf16[16,71,8,128]{3,2,1,0:T(8,128)(2,1)S(1)}, u32[]{:S(2)}, u32[]{:S(2)}) %all-to-all-start) | async-done | bytes 2326560 | tf_op jit(solution)/shard_map/all_to_all | solution.py:380
  38.1 1.3 %legendre_sums.1 = bf16[16,40,256]{2,1,0:T(8,128)(2,1)S(1)} custom-call(s32[2]{0:T(128)S(1)} %pad_add_fusion.pairs_ref, bf16[16,71,8,128]{3,2,1,0:T(8,128)(2,1)S(1)} %all-to-all-done.rows_ref), custom_call_target="tpu_custom_call" | custom-call | tf_op jit(solution)/shard_map/legendre_sums/pallas_call | solution.py:260
  39.4 14.8 %all_to_all.20.sums_ref = bf16[16,40,256]{2,1,0:T(8,128)(2,1)S(1)} all-to-all(bf16[16,40,256]{2,1,0:T(8,128)(2,1)S(1)} %legendre_sums.1), channel_id=1, replica_groups=mesh['aa'=32,'ba'=16] {'ba'}, dimensions={0} | all-to-all | bytes 655360 | tf_op jit(solution)/shard_map/all_to_all | solution.py:385
  54.3 0.7 regroup.1
  55.0 44.3 %all_to_all.21.coef_ref = bf16[32,40,128]{2,1,0:T(8,128)(2,1)S(1)} all-to-all(bf16[32,40,128]{2,1,0:T(8,128)(2,1)S(1)} %regroup.1), channel_id=1, replica_groups=mesh['aa'=32,'ba'=16] {'aa'}, dimensions={0} | all-to-all | bytes 655360 | tf_op jit(solution)/shard_map/all_to_all | solution.py:387
  99.3 2.2 %synthesize.1 = bf16[16,64,384]{2,1,0:T(8,128)(2,1)S(1)} custom-call(s32[1280,128]{1,0:T(8,128)S(1)} %column_places.1.places_ref, bf16[32,40,128]{2,1,0:T(8,128)(2,1)S(1)} %all_to_all.21.coef_ref, bf16[2,1280,768]{2,1,0:T(8,128)(2,1)S(1)} %copy-done.2), custom_call_target="tpu_custom_call" | custom-call | tf_op jit(solution)/shard_map/synthesize/pallas_call | solution.py:304
  101.5 16.7 %all_to_all.22.grid_ref = bf16[16,64,384]{2,1,0:T(8,128)(2,1)S(1)} all-to-all(bf16[16,64,384]{2,1,0:T(8,128)(2,1)S(1)} %synthesize.1), channel_id=1, replica_groups=mesh['aa'=32,'ba'=16] {'ba'}, dimensions={0} | all-to-all | bytes 1572864 | tf_op jit(solution)/shard_map/all_to_all | solution.py:389
  118.3 0.8 collective-permute-start
  119.0 3.4 %depart_inner.1.inner_ref = bf16[16,64,320]{2,1,0:T(8,128)(2,1)} custom-call(f32[16,3,384]{2,1,0:T(4,128)S(1)} %select_maximum_fusion.target_ref, bf16[16,64,384]{2,1,0:T(8,128)(2,1)S(1)} %all_to_all.22.grid_ref), custom_call_target="tpu_custom_call" | custom-call | flops 440401920 | bytes 4000000 | tf_op jit(solution)/shard_map/depart_inner/pallas_call | solution.py:320
  122.5 1.0 depart_edges.1
  (23 shorter events, 0.1 us)
Async XLA Ops:
  2.9 7.8 %copy-start.7 = (s32[640]{0:T(1024)S(1)}, s32[640]{0:T(1024)}, u32[]{:S(2)}) copy-start(s32[640]{0:T(1024)} %param.8) | copy-start | bytes 7684
  2.9 8.1 %copy-start.5 = (s32[16,320]{1,0:T(8,128)S(1)}, s32[16,320]{1,0:T(8,128)}, u32[]{:S(2)}) copy-start(s32[16,320]{1,0:T(8,128)} %param.9) | copy-start | bytes 61444
  2.9 8.1 %copy-start.6 = (s32[16,320]{1,0:T(8,128)S(1)}, s32[16,320]{1,0:T(8,128)}, u32[]{:S(2)}) copy-start(s32[16,320]{1,0:T(8,128)} %param.10) | copy-start | bytes 61444
  2.9 35.1 %all-to-all-start = ((bf16[16,71,8,128]{3,2,1,0:T(8,128)(2,1)}), bf16[16,71,8,128]{3,2,1,0:T(8,128)(2,1)S(1)}, u32[]{:S(2)}, u32[]{:S(2)}) async-start(bf16[16,71,8,128]{3,2,1,0:T(8,128)(2,1)} %pack.1), calls=%async_computation | async-start | bytes 4653056 | tf_op jit(solution)/shard_map/all_to_all | solution.py:380
  12.1 1.0 copy-start.3
  14.6 1.2 copy-start
  38.1 16.2 %copy-start.1 = (bf16[1280,640]{1,0:T(8,128)(2,1)S(1)}, bf16[1280,640]{1,0:T(8,128)(2,1)}, u32[]{:S(2)}) copy-start(bf16[1280,640]{1,0:T(8,128)(2,1)} %copy-done) | copy-start | bytes 4915204
  38.1 61.2 %copy-start.2 = (bf16[2,1280,768]{2,1,0:T(8,128)(2,1)S(1)}, bf16[2,1280,768]{2,1,0:T(8,128)(2,1)}, u32[]{:S(2)}) copy-start(bf16[2,1280,768]{2,1,0:T(8,128)(2,1)} %constant.59.clone.table_ref) | copy-start | bytes 11796484
  101.5 20.9 %copy-start.4 = (bf16[2,1152,256]{2,1,0:T(8,128)(2,1)S(1)}, bf16[2,1152,256]{2,1,0:T(8,128)(2,1)}, u32[]{:S(2)}) copy-start(bf16[2,1152,256]{2,1,0:T(8,128)(2,1)} %copy-done.3) | copy-start | bytes 3538948
  118.3 4.2 %collective-permute-start = (bf16[2,64,384]{2,1,0:T(8,128)(2,1)S(1)}, bf16[2,64,384]{2,1,0:T(8,128)(2,1)S(1)}, u32[]{:S(2)}, u32[]{:S(2)}) collective-permute-start(bf16[2,64,384]{2,1,0:T(8,128)(2,1)S(1)} %pad_maximum_fusion), channel_id=1, source_target_pairs={{0,16},{16,32},{32,48},{48,64},{64,80},{80,96},{96,112},{112,128},... | collective-permute-start | bytes 294920 | tf_op jit(solution)/shard_map/ppermute | solution.py:391

commit v9 on v8

--- a/solution.py
+++ b/solution.py
@@ -163,13 +163,14 @@
     real, imag = ordered[:FL], ordered[FL:]
     place = iota((1, WAVES), 1)
     wave = jnp.where(place < WAVES // 2, place, WAVES + WAVES // 2 - 1 - place)
-    for q in range(4):
-        turn = wave * q % 4
-        alpha = (turn == 0).astype(F32) - (turn == 2).astype(F32)
-        beta = (turn == 1).astype(F32) - (turn == 3).astype(F32)
-        here = pl.ds(q * FL, FL)
-        left_ref[0, here, :] = (real * alpha - imag * beta).astype(BF16)
-        left_ref[1, here, :] = (imag * alpha + real * beta).astype(BF16)
+    alpha = (wave % 4 == 0).astype(F32) - (wave % 4 == 2).astype(F32)
+    beta = (wave % 4 == 1).astype(F32) - (wave % 4 == 3).astype(F32)
+    half = 1.0 - 2.0 * (wave % 2).astype(F32)
+    turns = [(real, imag), (real * alpha - imag * beta, imag * alpha + real * beta)]
+    for q in range(2):
+        for c in range(2):
+            left_ref[c, q * FL : (q + 1) * FL, :] = turns[q][c].astype(BF16)
+            left_ref[c, (q + 2) * FL : (q + 3) * FL, :] = (turns[q][c] * half).astype(BF16)
     even = jnp.dot(left_ref[0], table_ref[0], preferred_element_type=F32)
     odd = jnp.dot(left_ref[1], table_ref[1], preferred_element_type=F32)
     ahead, behind = (even + odd).astype(BF16), (even - odd).astype(BF16)

time: 124 us -> 124 us (level)
  no operation moved by 1% of the time
where the time goes in v9:
time: 124 us; the launch traced here: 123 us
  blocking collectives  75.8 us (61%)
  waiting for transfers between devices  20.2 us (16%)
  Pallas kernels  13.8 us (11%)
  starting transfers between devices  8.48 us (7%)
  local copies, waits for them, and re-layouts  3.14 us (3%)
  other arithmetic  1.68 us (1%)
    all_to_all x1, blocking collectives, local(): coefficients = lax.all_to_all(by_row, 'aa', 0, 0, tiled=True)  44.3 us
    all_to_all x1, waiting for transfers between devices, local(): rows = lax.all_to_all(pack(legendre, spectral), 'ba', 0, 0, tiled=True)  20.2 us
    all_to_all x1, blocking collectives, local(): grid = lax.all_to_all(blocks, 'ba', 0, 0, tiled=True)  16.7 us
    all_to_all x1, blocking collectives, local(): sums = lax.all_to_all(legendre_sums(pairs, rows), 'ba', 0, 0, tiled=True)  14.8 us
    all_to_all x1, starting transfers between devices, local(): rows = lax.all_to_all(pack(legendre, spectral), 'ba', 0, 0, tiled=True)  7.73 us
    pallas_call x1, Pallas kernels, depart_inner(): pl.pallas_call(inner_kernel, out_shape=jax.ShapeDtypeStruct((N_BA, FL, BL...  3.44 us
    pallas_call x1, Pallas kernels, pack(): pl.pallas_call(pack_kernel, out_shape=jax.ShapeDtypeStruct((N_BA, TILES,...  2.9 us
  transfers between devices with their start and end apart: 2, of which 1 were waited for; matrix products, arithmetic and copies ran while one was open for 2% of the time, Pallas kernels for 5%

profile of v9, /device:TPU:1, one launch (start us, length us, event | category | flops | bytes accessed | tf_op | source)
XLA Modules:
  0.0 123.4 jit_solution(11181947649221521841)
XLA Ops:
  0.0 2.9 %pack.1 = bf16[16,71,8,128]{3,2,1,0:T(8,128)(2,1)} custom-call(bf16[20,32,1281]{2,1,0:T(8,128)(2,1)} %bitcast.7, bf16[20,2,4,1281]{3,2,1,0:T(4,128)(2,1)} %bitcast.8), custom_call_target="tpu_custom_call" | custom-call | tf_op jit(solution)/shard_map/pack/pallas_call | solution.py:244
  2.9 7.7 %all-to-all-start = ((bf16[16,71,8,128]{3,2,1,0:T(8,128)(2,1)}), bf16[16,71,8,128]{3,2,1,0:T(8,128)(2,1)S(1)}, u32[]{:S(2)}, u32[]{:S(2)}) async-start(bf16[16,71,8,128]{3,2,1,0:T(8,128)(2,1)} %pack.1), calls=%async_computation | async-start | bytes 4653056 | tf_op jit(solution)/shard_map/all_to_all | solution.py:381
  10.7 0.1 add.91
  10.8 0.1 broadcast_add_fusion
  10.9 0.1 add.95.places_ref
  11.1 0.1 select_bitcast_fusion.1
  11.2 0.5 column_places.1.places_ref
  11.7 0.1 select_maximum_fusion.target_ref
  11.8 0.3 edge_bands.1
  12.1 1.0 copy-done.3
  13.1 1.5 %regroup_rows.1.perm_ref = bf16[1280,640]{1,0:T(8,128)(2,1)S(1)} custom-call(s32[1]{0:T(128)} %bitcast.own_ref), custom_call_target="tpu_custom_call" | custom-call | tf_op jit(solution)/shard_map/regroup_rows/pallas_call | solution.py:283
  14.6 1.2 copy-done
  15.8 0.7 fusion.4
  16.4 1.4 %pad_add_fusion.pairs_ref = s32[2]{0:T(128)S(1)} fusion(s32[1]{0:T(128)} %get-tuple-element.27, s32[1]{0:T(128)} %get-tuple-element.26), kind=kLoop, calls=%fused_computation.14 | loop fusion | flops 2 | bytes 16 | tf_op jit(solution)/shard_map/stack | solution.py:380
  17.8 20.2 %all-to-all-done.rows_ref = bf16[16,71,8,128]{3,2,1,0:T(8,128)(2,1)S(1)} async-done(((bf16[16,71,8,128]{3,2,1,0:T(8,128)(2,1)}), bf16[16,71,8,128]{3,2,1,0:T(8,128)(2,1)S(1)}, u32[]{:S(2)}, u32[]{:S(2)}) %all-to-all-start) | async-done | bytes 2326560 | tf_op jit(solution)/shard_map/all_to_all | solution.py:381
  38.1 1.3 %legendre_sums.1 = bf16[16,40,256]{2,1,0:T(8,128)(2,1)S(1)} custom-call(s32[2]{0:T(128)S(1)} %pad_add_fusion.pairs_ref, bf16[16,71,8,128]{3,2,1,0:T(8,128)(2,1)S(1)} %all-to-all-done.rows_ref), custom_call_target="tpu_custom_call" | custom-call | tf_op jit(solution)/shard_map/legendre_sums/pallas_call | solution.py:261
  39.4 14.8 %all_to_all.20.sums_ref = bf16[16,40,256]{2,1,0:T(8,128)(2,1)S(1)} all-to-all(bf16[16,40,256]{2,1,0:T(8,128)(2,1)S(1)} %legendre_sums.1), channel_id=1, replica_groups=mesh['aa'=32,'ba'=16] {'ba'}, dimensions={0} | all-to-all | bytes 655360 | tf_op jit(solution)/shard_map/all_to_all | solution.py:386
  54.3 0.7 regroup.1
  55.0 44.3 %all_to_all.21.coef_ref = bf16[32,40,128]{2,1,0:T(8,128)(2,1)S(1)} all-to-all(bf16[32,40,128]{2,1,0:T(8,128)(2,1)S(1)} %regroup.1), channel_id=1, replica_groups=mesh['aa'=32,'ba'=16] {'aa'}, dimensions={0} | all-to-all | bytes 655360 | tf_op jit(solution)/shard_map/all_to_all | solution.py:388
  99.3 2.1 %synthesize.1 = bf16[16,64,384]{2,1,0:T(8,128)(2,1)S(1)} custom-call(s32[1280,128]{1,0:T(8,128)S(1)} %column_places.1.places_ref, bf16[32,40,128]{2,1,0:T(8,128)(2,1)S(1)} %all_to_all.21.coef_ref, bf16[2,1280,768]{2,1,0:T(8,128)(2,1)S(1)} %copy-done.2), custom_call_target="tpu_custom_call" | custom-call | tf_op jit(solution)/shard_map/synthesize/pallas_call | solution.py:305
  101.4 16.7 %all_to_all.22.grid_ref = bf16[16,64,384]{2,1,0:T(8,128)(2,1)S(1)} all-to-all(bf16[16,64,384]{2,1,0:T(8,128)(2,1)S(1)} %synthesize.1), channel_id=1, replica_groups=mesh['aa'=32,'ba'=16] {'ba'}, dimensions={0} | all-to-all | bytes 1572864 | tf_op jit(solution)/shard_map/all_to_all | solution.py:390
  118.2 0.8 collective-permute-start
  118.9 3.4 %depart_inner.1.inner_ref = bf16[16,64,320]{2,1,0:T(8,128)(2,1)} custom-call(f32[16,3,384]{2,1,0:T(4,128)S(1)} %select_maximum_fusion.target_ref, bf16[16,64,384]{2,1,0:T(8,128)(2,1)S(1)} %all_to_all.22.grid_ref), custom_call_target="tpu_custom_call" | custom-call | flops 440401920 | bytes 4000000 | tf_op jit(solution)/shard_map/depart_inner/pallas_call | solution.py:321
  122.3 1.0 depart_edges.1
  (23 shorter events, 0.1 us)
Async XLA Ops:
  2.9 7.8 %copy-start.7 = (s32[640]{0:T(1024)S(1)}, s32[640]{0:T(1024)}, u32[]{:S(2)}) copy-start(s32[640]{0:T(1024)} %param.8) | copy-start | bytes 7684
  2.9 8.1 %copy-start.5 = (s32[16,320]{1,0:T(8,128)S(1)}, s32[16,320]{1,0:T(8,128)}, u32[]{:S(2)}) copy-start(s32[16,320]{1,0:T(8,128)} %param.9) | copy-start | bytes 61444
  2.9 8.1 %copy-start.6 = (s32[16,320]{1,0:T(8,128)S(1)}, s32[16,320]{1,0:T(8,128)}, u32[]{:S(2)}) copy-start(s32[16,320]{1,0:T(8,128)} %param.10) | copy-start | bytes 61444
  2.9 35.1 %all-to-all-start = ((bf16[16,71,8,128]{3,2,1,0:T(8,128)(2,1)}), bf16[16,71,8,128]{3,2,1,0:T(8,128)(2,1)S(1)}, u32[]{:S(2)}, u32[]{:S(2)}) async-start(bf16[16,71,8,128]{3,2,1,0:T(8,128)(2,1)} %pack.1), calls=%async_computation | async-start | bytes 4653056 | tf_op jit(solution)/shard_map/all_to_all | solution.py:381
  12.1 1.0 copy-start.3
  14.6 1.2 copy-start
  38.1 16.2 %copy-start.1 = (bf16[1280,640]{1,0:T(8,128)(2,1)S(1)}, bf16[1280,640]{1,0:T(8,128)(2,1)}, u32[]{:S(2)}) copy-start(bf16[1280,640]{1,0:T(8,128)(2,1)} %copy-done) | copy-start | bytes 4915204
  38.1 61.2 %copy-start.2 = (bf16[2,1280,768]{2,1,0:T(8,128)(2,1)S(1)}, bf16[2,1280,768]{2,1,0:T(8,128)(2,1)}, u32[]{:S(2)}) copy-start(bf16[2,1280,768]{2,1,0:T(8,128)(2,1)} %constant.59.clone.table_ref) | copy-start | bytes 11796484
  101.4 20.9 %copy-start.4 = (bf16[2,1152,256]{2,1,0:T(8,128)(2,1)S(1)}, bf16[2,1152,256]{2,1,0:T(8,128)(2,1)}, u32[]{:S(2)}) copy-start(bf16[2,1152,256]{2,1,0:T(8,128)(2,1)} %copy-done.3) | copy-start | bytes 3538948
  118.2 4.2 %collective-permute-start = (bf16[2,64,384]{2,1,0:T(8,128)(2,1)S(1)}, bf16[2,64,384]{2,1,0:T(8,128)(2,1)S(1)}, u32[]{:S(2)}, u32[]{:S(2)}) collective-permute-start(bf16[2,64,384]{2,1,0:T(8,128)(2,1)S(1)} %pad_maximum_fusion), channel_id=1, source_target_pairs={{0,16},{16,32},{32,48},{48,64},{64,80},{80,96},{96,112},{112,128},... | collective-permute-start | bytes 294920 | tf_op jit(solution)/shard_map/ppermute | solution.py:392
